TPU v7x, 32 devices: a whole 2x2x4 slice. The times are simulated.
32 devices in a mesh: ao: 8 (over z, x), ri: 4 (over y, core).
Axes of the slice: x: 2, y: 2, z: 4, core: 2. Of those that a mesh axis runs over, the one named last changes fastest.
Arguments:
- three_center: bfloat16 [64, 3072, 128], P('ri', 'ao'), may hold values from -0.19921875 to 0.19921875
- occ_band: bfloat16 [1024, 640], P('ao'), may hold values from -0.3125 to 0.3125
- virt_band: bfloat16 [1024, 384], P('ao'), may hold values from -0.3125 to 0.3125
- three_mask: int32 [8, 3], P('ao'), may hold values 0 or 1
- occ_mask: int32 [8, 5], P('ao'), may hold values 0 or 1
- virt_mask: int32 [8, 3], P('ao'), may hold values 0 or 1
Outputs:
- chi: float32 [64, 64], P('ri')
All inputs are finite; a program needn't handle non-finite values. No bound on the sum of `three_mask` or of `occ_mask` or of `virt_mask` on one device may be relied on, other than what follows from the above.
Results may differ from a plain program's by a relative error of at most 0.004.
Values may be sent and summed in bfloat16 or wider, within the bound.
No kernel may reach another device: no remote copies, remote signals or barrier semaphores. Data moves between devices by JAX's collectives and lax.ppermute only.
A program may use at most 64 MiB of HBM per device.

v0:
```python
import jax
import jax.numpy as jnp
from jax import lax
from jax.sharding import PartitionSpec as P


def padded(value, sides, width):
    for axis, dim in sides:
        peers, length = (lax.axis_size(axis), value.shape[dim])
        up = [(i, (i + 1) % peers) for i in range(peers)]
        down = [(j, i) for i, j in up]
        last = lax.slice_in_dim(value, length - width, length, axis=dim)
        initial = lax.slice_in_dim(value, 0, width, axis=dim)
        before = lax.ppermute(last, axis, up)
        after = lax.ppermute(initial, axis, down)
        value = jnp.concatenate([before, value, after], axis=dim)
    return value


def from_behind(block, axis, distance):
    devices = range(lax.axis_size(axis))
    route = [((i - distance) % len(devices), i) for i in devices]
    return lax.ppermute(block, axis, route)


def per_device(three_center, occ_band, virt_band, three_mask, occ_mask, virt_mask):
    tile_size = occ_band.shape[0]
    local_rows = three_center.shape[0]
    live_b = (
        three_center.reshape(local_rows, 3, tile_size, tile_size)
        * three_mask[0].astype(three_center.dtype)[None, :, None, None]
    )
    live_b = live_b.reshape(local_rows, 3 * tile_size, tile_size)
    live_occ = occ_band * jnp.repeat(occ_mask[0].astype(occ_band.dtype), tile_size)[None, :]
    live_virt = virt_band * jnp.repeat(virt_mask[0].astype(virt_band.dtype), tile_size)[None, :]
    occ_rows = padded(live_occ, (("ao", 0),), tile_size)
    blank = jnp.zeros((tile_size, tile_size), occ_band.dtype)
    green_block = jnp.concatenate(
        [
            jnp.concatenate([occ_rows[0:tile_size, tile_size:], blank], 1),
            occ_rows[tile_size : 2 * tile_size],
            jnp.concatenate([blank, occ_rows[2 * tile_size :, : 4 * tile_size]], 1),
        ],
        0,
    )
    m_local = jnp.einsum(
        "ml,pmn->pln", green_block, live_b, preferred_element_type=jnp.float32
    ).astype(jnp.bfloat16)
    from_left = from_behind(m_local[:, 2 * tile_size : 5 * tile_size], "ao", 1)
    from_right = from_behind(m_local[:, 0 : 3 * tile_size], "ao", -1)
    needed = jnp.concatenate([from_left, m_local[:, tile_size : 4 * tile_size], from_right], 2)
    product = jnp.einsum(
        "plv,sv->pls", needed, live_virt, preferred_element_type=jnp.float32
    ).astype(jnp.bfloat16)
    product_flat = product.reshape(local_rows, 3 * tile_size * tile_size)
    b_flat = live_b.reshape(local_rows, 3 * tile_size * tile_size)
    product_all, b_all = (
        lax.all_to_all(product_flat, "ri", split_axis=1, concat_axis=0, tiled=True),
        lax.all_to_all(b_flat, "ri", split_axis=1, concat_axis=0, tiled=True),
    )
    partial_chi = lax.dot_general(
        product_all, b_all, (((1,), (1,)), ((), ())), preferred_element_type=jnp.float32
    )
    row_panel = lax.psum_scatter(partial_chi, "ri", scatter_dimension=0, tiled=True)
    summed = lax.psum(row_panel, "ao")
    return -summed


def solution(mesh):
    placed = (
        P("ri", "ao", None),
        P("ao", None),
        P("ao", None),
        P("ao", None),
        P("ao", None),
        P("ao", None),
    )
    return jax.shard_map(
        per_device, mesh=mesh, in_specs=placed, out_specs=P("ri", None), check_vma=False
    )
```

profile of v0, /device:TPU:0, one launch (start us, length us, event | category | flops | bytes accessed | tf_op | source)
XLA Modules:
  0.0 178.4 jit_solution(4304228224178167077)
XLA Ops:
  6.5 0.7 convert_bitcast_fusion.2
  7.2 0.1 broadcast_bitcast_fusion
  7.3 0.9 broadcast_multiply_fusion.1
  8.2 3.0 %collective-permute-start = (bf16[128,640]{1,0:T(8,128)(2,1)S(1)}, bf16[128,640]{1,0:T(8,128)(2,1)}, u32[]{:S(2)}, u32[]{:S(2)}) collective-permute-start(bf16[128,640]{1,0:T(8,128)(2,1)S(1)} %broadcast_multiply_fusion.1), channel_id=1, source_target_pairs={{0,4},{4,8},{8,12},{12,16},{16,20},{20,24},{24,28},{28,0},{1,5},{5... | collective-permute-start | bytes 491528 | tf_op jit(solution)/shard_map/ppermute | solution.py:14
  11.2 3.1 %collective-permute-start.1 = (bf16[128,640]{1,0:T(8,128)(2,1)S(1)}, bf16[128,640]{1,0:T(8,128)(2,1)}, u32[]{:S(2)}, u32[]{:S(2)}) collective-permute-start(bf16[128,640]{1,0:T(8,128)(2,1)S(1)} %broadcast_multiply_fusion.1), channel_id=1, source_target_pairs={{4,0},{8,4},{12,8},{16,12},{20,16},{24,20},{28,24},{0,28},{5,1},{9... | collective-permute-start | bytes 491528 | tf_op jit(solution)/shard_map/ppermute | solution.py:15
  14.3 0.7 convert_bitcast_fusion.3
  15.0 0.1 mul.53
  15.1 0.0 copy-start
  15.1 3.3 %reshape.31 = bf16[16,4,12288]{2,1,0:T(4,128)(2,1)S(1)} reshape(bf16[16,384,128]{2,1,0:T(8,128)(2,1)} %param.6) | data formatting | bytes 3145728 | tf_op jit(solution)/shard_map/reshape | solution.py:30
  18.4 0.1 broadcast_bitcast_fusion.2
  18.5 0.2 collective-permute-done
  18.6 0.9 slice.20
  19.6 0.9 collective-permute-done.1
  20.5 0.9 slice.21
  21.4 0.0 copy-done
  21.4 1.8 %convert_bitcast_fusion = bf16[16,640,128]{1,2,0:T(8,128)(2,1)S(1)} fusion(bf16[16,384,128]{2,1,0:T(8,128)(2,1)S(1)} %copy-done, bf16[384]{0:T(512)(128)(2,1)S(1)} %broadcast_bitcast_fusion.2, bf16[128,512]{1,0:T(8,128)(2,1)S(1)} %slice.21, bf16[128,512]{1,0:T(8,128)(2,1)S(1)} %slice.20, bf16[128,640]{1,0:T(8,128)(2,1)S(1)} %broadcast_multiply_fusion.1), kind=kOutput, calls=%fused_computation.6 | convolution fusion | flops 1011187712 | bytes 4621056 | tf_op jit(solution)/shard_map/ml,pmn->pln/dot_general | solution.py:46
  23.2 2.5 %fusion.32 = (bf16[16,384,128]{1,2,0:T(8,128)(2,1)}, bf16[16,384,128]{1,2,0:T(8,128)(2,1)}, bf16[16,384,128]{1,2,0:T(8,128)(2,1)S(1)}) fusion(bf16[16,640,128]{1,2,0:T(8,128)(2,1)S(1)} %convert_bitcast_fusion), kind=kLoop, calls=%fused_computation.39 | loop fusion | bytes 9437184 | tf_op jit(solution)/shard_map/slice | solution.py:49
  25.7 1.2 collective-permute-start.2
  26.9 3.5 %collective-permute-start.3 = (bf16[16,384,128]{1,2,0:T(8,128)(2,1)}, bf16[16,384,128]{1,2,0:T(8,128)(2,1)}, u32[]{:S(2)}, u32[]{:S(2)}) collective-permute-start(bf16[16,384,128]{1,2,0:T(8,128)(2,1)} %get-tuple-element.6), channel_id=1, source_target_pairs={{4,0},{8,4},{12,8},{16,12},{20,16},{24,20},{28,24},{0,28},{5,1},{9... | collective-permute-start | bytes 4718600 | tf_op jit(solution)/shard_map/ppermute | solution.py:23
  30.4 0.1 broadcast.26
  30.4 0.1 broadcast_multiply_fusion
  30.6 2.0 %copy.19 = bf16[16,4,12288]{2,0,1:T(8,128)(2,1)} copy(bf16[16,4,12288]{2,1,0:T(4,128)(2,1)S(1)} %bitcast.33) | data formatting | bytes 3145728 | tf_op jit(solution)/shard_map/mul | solution.py:30
  32.6 0.0 copy-start.2
  32.6 0.0 copy-start.1
  32.6 3.7 %all-to-all-start.1 = ((bf16[16,4,12288]{2,0,1:T(8,128)(2,1)}), bf16[16,4,12288]{2,0,1:T(8,128)(2,1)S(1)}, u32[]{:S(2)}, u32[]{:S(2)}) async-start(bf16[16,4,12288]{2,0,1:T(8,128)(2,1)} %copy.19), calls=%async_computation.1 | async-start | bytes 3145728 | tf_op jit(solution)/shard_map/all_to_all | solution.py:59
  36.3 0.0 reduce-scatter.2.cloned.1.call-start
  36.4 0.0 copy-done.2
  36.4 0.1 broadcast_bitcast_fusion.1
  36.5 57.2 %collective-permute-done.2 = bf16[16,384,128]{1,2,0:T(8,128)(2,1)} collective-permute-done((bf16[16,384,128]{1,2,0:T(8,128)(2,1)}, bf16[16,384,128]{1,2,0:T(8,128)(2,1)}, u32[]{:S(2)}, u32[]{:S(2)}) %collective-permute-start.2) | collective-permute-done | bytes 1572896 | tf_op jit(solution)/shard_map/ppermute | solution.py:23
  93.7 3.0 %collective-permute-done.3 = bf16[16,384,128]{1,2,0:T(8,128)(2,1)} collective-permute-done((bf16[16,384,128]{1,2,0:T(8,128)(2,1)}, bf16[16,384,128]{1,2,0:T(8,128)(2,1)}, u32[]{:S(2)}, u32[]{:S(2)}) %collective-permute-start.3) | collective-permute-done | bytes 1572896 | tf_op jit(solution)/shard_map/ppermute | solution.py:23
  96.7 0.0 copy-done.1
  96.7 4.5 %fusion.6 = bf16[16,384,128]{2,1,0:T(8,128)(2,1)} fusion(bf16[16,384,128]{1,2,0:T(8,128)(2,1)} %collective-permute-done.3, bf16[16,384,128]{1,2,0:T(8,128)(2,1)S(1)} %get-tuple-element.7, bf16[16,384,128]{1,2,0:T(8,128)(2,1)} %collective-permute-done.2, bf16[128,384]{1,0:T(8,128)(2,1)S(1)} %copy-done.1, bf16[384]{0:T(512)(128)(2,1)S(1)} %broadcast_bitcast_fusion.1), kind=kOutput, calls=%fused_computation.7 | convolution fusion | flops 618971136 | bytes 6390528 | tf_op jit(solution)/shard_map/plv,sv->pls/dot_general | solution.py:52
  101.2 4.0 %all_to_all.26 = bf16[16,4,12288]{2,1,0:T(4,128)(2,1)} reshape(bf16[16,384,128]{2,1,0:T(8,128)(2,1)} %fusion.6) | data formatting | bytes 3145728 | tf_op jit(solution)/shard_map/all_to_all | solution.py:58
  105.2 2.3 %copy.18 = bf16[16,4,12288]{2,0,1:T(8,128)(2,1)S(1)} copy(bf16[16,4,12288]{2,1,0:T(4,128)(2,1)} %all_to_all.26) | data formatting | bytes 3145728 | tf_op jit(solution)/shard_map/all_to_all | solution.py:58
  107.5 0.0 all-to-all-done.1
  107.5 22.7 %all_to_all.35 = bf16[16,4,12288]{2,0,1:T(8,128)(2,1)S(1)} all-to-all(bf16[16,4,12288]{2,0,1:T(8,128)(2,1)S(1)} %copy.18), channel_id=1, replica_groups=mesh['ao'=8,'ri'=4] {'ri'}, dimensions={1} | all-to-all | bytes 3145728 | tf_op jit(solution)/shard_map/all_to_all | solution.py:58
  130.2 1.2 fusion.33
  131.3 0.0 reduce-scatter.2.cloned.1.call-update
  131.4 17.8 %reduce-scatter.2.cloned.1.call-done = f32[16,64]{1,0:T(8,128)} async-done(((f32[64,64]{1,0:T(8,128)}), f32[16,64]{1,0:T(8,128)}) %reduce-scatter.2.cloned.1.call-update) | async-done | bytes 4112 | tf_op jit(solution)/shard_map/reduce_scatter | solution.py:64
  149.2 21.7 %psum.7 = f32[16,64]{1,0:T(8,128)S(1)} all-reduce(f32[16,64]{1,0:T(8,128)} %reduce-scatter.2.cloned.1.call-done), channel_id=1, replica_groups=mesh['ao'=8,'ri'=4] {'ao'}, use_global_device_ids=true, to_apply=%region_1.0 | all-reduce | flops 1024 | bytes 8192 | tf_op jit(solution)/shard_map/psum | solution.py:65
  170.9 0.6 neg.3
  (2 shorter events, 0.0 us)
Async XLA Ops:
  8.2 10.4 %collective-permute-start = (bf16[128,640]{1,0:T(8,128)(2,1)S(1)}, bf16[128,640]{1,0:T(8,128)(2,1)}, u32[]{:S(2)}, u32[]{:S(2)}) collective-permute-start(bf16[128,640]{1,0:T(8,128)(2,1)S(1)} %broadcast_multiply_fusion.1), channel_id=1, source_target_pairs={{0,4},{4,8},{8,12},{12,16},{16,20},{20,24},{24,28},{28,0},{1,5},{5... | collective-permute-start | bytes 491528 | tf_op jit(solution)/shard_map/ppermute | solution.py:14
  11.2 9.3 %collective-permute-start.1 = (bf16[128,640]{1,0:T(8,128)(2,1)S(1)}, bf16[128,640]{1,0:T(8,128)(2,1)}, u32[]{:S(2)}, u32[]{:S(2)}) collective-permute-start(bf16[128,640]{1,0:T(8,128)(2,1)S(1)} %broadcast_multiply_fusion.1), channel_id=1, source_target_pairs={{4,0},{8,4},{12,8},{16,12},{20,16},{24,20},{28,24},{0,28},{5,1},{9... | collective-permute-start | bytes 491528 | tf_op jit(solution)/shard_map/ppermute | solution.py:15
  15.1 6.3 %copy-start = (bf16[16,384,128]{2,1,0:T(8,128)(2,1)S(1)}, bf16[16,384,128]{2,1,0:T(8,128)(2,1)}, u32[]{:S(2)}) copy-start(bf16[16,384,128]{2,1,0:T(8,128)(2,1)} %param.6) | copy-start | bytes 4718596
  25.7 68.0 %collective-permute-start.2 = (bf16[16,384,128]{1,2,0:T(8,128)(2,1)}, bf16[16,384,128]{1,2,0:T(8,128)(2,1)}, u32[]{:S(2)}, u32[]{:S(2)}) collective-permute-start(bf16[16,384,128]{1,2,0:T(8,128)(2,1)} %get-tuple-element.5), channel_id=1, source_target_pairs={{28,0},{0,4},{4,8},{8,12},{12,16},{16,20},{20,24},{24,28},{29,1},{... | collective-permute-start | bytes 4718600 | tf_op jit(solution)/shard_map/ppermute | solution.py:23
  26.9 69.8 %collective-permute-start.3 = (bf16[16,384,128]{1,2,0:T(8,128)(2,1)}, bf16[16,384,128]{1,2,0:T(8,128)(2,1)}, u32[]{:S(2)}, u32[]{:S(2)}) collective-permute-start(bf16[16,384,128]{1,2,0:T(8,128)(2,1)} %get-tuple-element.6), channel_id=1, source_target_pairs={{4,0},{8,4},{12,8},{16,12},{20,16},{24,20},{28,24},{0,28},{5,1},{9... | collective-permute-start | bytes 4718600 | tf_op jit(solution)/shard_map/ppermute | solution.py:23
  32.6 3.8 %copy-start.2 = (s32[1,3]{1,0:T(1,128)S(1)}, s32[1,3]{1,0:T(1,128)}, u32[]{:S(2)}) copy-start(s32[1,3]{1,0:T(1,128)} %param.11) | copy-start | bytes 40
  32.6 64.1 %copy-start.1 = (bf16[128,384]{1,0:T(8,128)(2,1)S(1)}, bf16[128,384]{1,0:T(8,128)(2,1)}, u32[]{:S(2)}) copy-start(bf16[128,384]{1,0:T(8,128)(2,1)} %param.8) | copy-start | bytes 294916
  32.6 74.9 %all-to-all-start.1 = ((bf16[16,4,12288]{2,0,1:T(8,128)(2,1)}), bf16[16,4,12288]{2,0,1:T(8,128)(2,1)S(1)}, u32[]{:S(2)}, u32[]{:S(2)}) async-start(bf16[16,4,12288]{2,0,1:T(8,128)(2,1)} %copy.19), calls=%async_computation.1 | async-start | bytes 3145728 | tf_op jit(solution)/shard_map/all_to_all | solution.py:59
  36.3 112.9 %reduce-scatter.2.cloned.1.call-start = ((), (), s32[]{:S(2)}) async-start(), calls=%async_computation.3 | async-start | bytes 40960 | tf_op jit(solution)/shard_map/reduce_scatter | solution.py:64
Sparse Core Ops, SparseCore 0:
  131.5 17.6 reduce-scatter.1
where the time goes:
time: 179 us; the launch traced here: 178 us
  waiting for transfers between devices  79.2 us (44%)
  blocking collectives  44.4 us (25%)
  local copies, waits for them, and re-layouts  16.3 us (9%)
  starting transfers between devices  14.6 us (8%)
  between operations  13.5 us (8%)
  matrix products  7.44 us (4%)
  other arithmetic  3 us (2%)
    ppermute x2, waiting for transfers between devices, from_behind(): return lax.ppermute(block, axis, route)  60.3 us
    all_to_all x1, blocking collectives, per_device(): lax.all_to_all(product_flat, 'ri', split_axis=1, concat_axis=0, tiled=True)  22.7 us
    psum x1, blocking collectives, per_device(): summed = lax.psum(row_panel, 'ao')  21.7 us
    reduce_scatter x1, waiting for transfers between devices, per_device(): lax.psum_scatter(partial_chi, 'ri', scatter_dimension=0, tiled=True)  17.8 us
    all_to_all x2, local copies, waits for them, and re-layouts, per_device(): lax.all_to_all(product_flat, 'ri', split_axis=1, concat_axis=0, tiled=True)  6.31 us
    ppermute x2, starting transfers between devices, from_behind(): return lax.ppermute(block, axis, route)  4.72 us
    dot_general x1, matrix products, per_device(): jnp.einsum('plv,sv->pls', needed, live_virt, preferred_element_type=jnp.f...  4.49 us
    all_to_all x1, starting transfers between devices, per_device(): lax.all_to_all(b_flat, 'ri', split_axis=1, concat_axis=0, tiled=True)  3.69 us
  transfers between devices with their start and end apart: 6, of which 5 were waited for; matrix products, arithmetic and copies ran while one was open for 8% of the time, Pallas kernels for 0%

commit v1 on v0

v1 whole, which is shorter than its diff:
```python
import functools

import jax
import jax.numpy as jnp
from jax import lax
from jax.experimental import pallas as pl
from jax.experimental.pallas import tpu as pltpu
from jax.sharding import PartitionSpec as P

F32, BF16 = jnp.float32, jnp.bfloat16
VMEM_LIMIT = 56 * 1024 * 1024
PARAMS = pltpu.CompilerParams(vmem_limit_bytes=VMEM_LIMIT)
ANY = pl.BlockSpec(memory_space=pl.ANY)
VMEM = pl.BlockSpec(memory_space=pltpu.VMEM)
SMEM = pl.BlockSpec(memory_space=pltpu.SMEM)
BOTH = ("ao", "ri")
LARGE = pl.CostEstimate(flops=10**11, bytes_accessed=10**9, transcendentals=0)
LITTLE = pl.CostEstimate(flops=1024, bytes_accessed=1024, transcendentals=0)


def call(kernel, name, out_shape, in_specs, out_specs=VMEM, **more):
    return pl.pallas_call(
        kernel,
        name=name,
        out_shape=out_shape,
        in_specs=in_specs,
        out_specs=out_specs,
        compiler_params=PARAMS,
        cost_estimate=LARGE if name in ("halo_panels", "own_m") else LITTLE,
        **more,
    )


def shape(*dims, dtype=BF16):
    return jax.ShapeDtypeStruct(dims, dtype)


def dot_nn(a, b, **more):
    return lax.dot_general(a, b, (((1,), (0,)), ((), ())), preferred_element_type=F32, **more)


def dot_nt(a, b):
    return lax.dot_general(a, b, (((1,), (1,)), ((), ())), preferred_element_type=F32)


def when_core(core, even, odd):
    pl.when(core == 0)(even)
    pl.when(core != 0)(odd)


def pack_kernel(
    core_ref, occ_mask, virt_mask, three_mask, occ_ref, virt_ref, src_ref,
    one_ref, two_ref, near_ref, late_ref, sems,
):
    tile, half = occ_ref.shape[0], near_ref.shape[0]
    moves = [
        pltpu.make_async_copy(src_ref.at[:half], near_ref, sems.at[0]),
        pltpu.make_async_copy(src_ref.at[half:], late_ref, sems.at[1]),
    ]
    for move in moves:
        move.start()

    def occ(k):
        return occ_ref[:, k * tile : (k + 1) * tile] * occ_mask[0, k].astype(BF16)

    def even():
        for k in range(4):
            one_ref[:tile, k * tile : (k + 1) * tile] = occ(k)
        one_ref[:tile, 4 * tile :] = virt_ref[:, :tile] * virt_mask[0, 0].astype(BF16)

    def odd():
        for k in range(3):
            one_ref[:tile, k * tile : (k + 1) * tile] = occ(k + 2)
        one_ref[:tile, 3 * tile :] = jnp.zeros((tile, 2 * tile), BF16)

    when_core(core_ref[0], even, odd)
    one_ref[tile:, :] = jnp.zeros((16, 5 * tile), BF16)
    for k in range(3):
        flag = jnp.full((16, tile), three_mask[0, k].astype(F32), F32)
        one_ref[tile:, k * tile : (k + 1) * tile] = flag.astype(BF16)
    for k in range(2):
        two_ref[:, k * tile : (k + 1) * tile] = occ(k)
    for move in moves:
        move.wait()


def tables_kernel(
    core_ref, occ_mask, virt_mask, three_mask, occ_ref, virt_ref, one_ref, two_ref, far_ref, after_ref,
    own_ref, halo_ref, virt_own_ref, virt_next_ref, lower, upper,
):
    tile = occ_ref.shape[0]

    def even():
        lower[...], upper[...] = far_ref[...], one_ref[...]

    def odd():
        lower[...], upper[...] = one_ref[...], far_ref[...]

    when_core(core_ref[0], even, odd)

    def cols(k):
        return slice(k * tile, (k + 1) * tile)

    def entry(mu, lam):
        if abs(mu - lam) > 2:
            return None
        if mu == -1:
            return lower[:tile, cols(lam + 1)]
        if mu == 0:
            return occ_ref[:, cols(lam + 2)] * occ_mask[0, lam + 2].astype(BF16)
        if mu == 1:
            return upper[:tile, cols(lam + 1)]
        return two_ref[:, cols(lam)]

    blank = jnp.zeros((tile, tile), BF16)
    own = [three_mask[0, k].astype(BF16) for k in range(3)]
    after = [upper[tile : tile + 1, cols(k)] for k in range(3)]
    for lam in range(-1, 2):
        for mu in range(-1, 3):
            block = entry(mu, lam)
            if block is not None:
                block = block.T * own[lam + 1]
            if mu < 2:
                own_ref[cols(lam + 1), cols(mu + 1)] = block * own[mu + 1]
            if mu > -1:
                halo_ref[cols(lam + 1), cols(mu)] = blank if block is None else block * after[mu]
    for mu in range(-1, 2):
        for lam in range(3):
            block = entry(mu, lam)
            value = blank if block is None else block * own[mu + 1] * after[lam]
            halo_ref[cols(mu + 4), cols(lam)] = value
    for k in range(2):
        virt_own_ref[:, cols(k)] = virt_ref[:, cols(k + 1)] * virt_mask[0, k + 1].astype(BF16)
    virt_next_ref[...] = upper[:tile, 4 * tile :]


def relayout_kernel(after_ref, src_ref, out_ref):
    out_ref[...] = jnp.swapaxes(src_ref[...], 0, 1)


def relayout(after, src, steps=3):
    batch, height, width = src.shape
    part = height // steps
    return call(
        relayout_kernel, "relayout", shape(height, batch, width),
        [ANY, pl.BlockSpec((batch, part, width), lambda i: (0, i, 0))],
        pl.BlockSpec((part, batch, width), lambda i: (i, 0, 0)),
        grid=(steps,),
    )(after, src)


def far_kernel(after_ref, near_ref, other_ref, out_ref, held, sems):
    batch, height, width = held.shape[1:]
    moves = [
        pltpu.make_async_copy(ref, held.at[k], sems.at[k])
        for k, ref in enumerate((near_ref, other_ref))
    ]
    for move in moves:
        move.start()
    for move in moves:
        move.wait()
    out_ref[...] = jnp.swapaxes(held[...].reshape(2 * batch, height, width), 0, 1)


def far_rows(after, near, other):
    batch, height, width = near.shape
    return call(
        far_kernel, "far_rows", shape(height, 2 * batch, width), [ANY] * 3,
        scratch_shapes=[
            pltpu.VMEM((2, batch, height, width), BF16),
            pltpu.SemaphoreType.DMA((2,)),
        ],
    )(after, near, other)


def own_m_kernel(green_ref, src_ref, *rest):
    outs, wide = rest[:2], rest[2]
    batch, _, width = src_ref.shape
    height, half = green_ref.shape[0], batch // 2
    for k, out_ref in enumerate(outs):
        for p in range(0, half, 2):
            pair = jnp.concatenate([src_ref[k * half + p], src_ref[k * half + p + 1]], 1)
            both = dot_nn(green_ref[...], pair)
            wide[k, pl.ds(p, height, half), :] = both[:, :width]
            wide[k, pl.ds(p + 1, height, half), :] = both[:, width:]
        out_ref[...] = wide[k].astype(BF16)


def own_m(green, src):
    batch, height, width = src.shape
    rows = width * batch // 2
    return call(
        own_m_kernel, "own_m", [shape(height * batch // 2, width)] * 2,
        [
            pl.BlockSpec((width, height), lambda i: (i, 0)),
            pl.BlockSpec((batch, height, width), lambda i: (0, 0, 0)),
        ],
        [pl.BlockSpec((rows, width), lambda i: (i, 0))] * 2,
        grid=(height // width,),
        scratch_shapes=[pltpu.VMEM((2, rows, width), F32)],
    )(green, src)


def halo_kernel(
    after_ref, halo_ref, m_ref, green_ref, virt_own_ref, virt_next_ref, out_ref,
    held, m_own, wide_m, wide_u, sems,
):
    batch, height, width = held.shape
    halo_move = pltpu.make_async_copy(halo_ref, held, sems.at[0])
    halo_move.start()
    m_move = pltpu.make_async_copy(m_ref, m_own, sems.at[1])
    m_move.start()
    halo_move.wait()
    for p in range(0, batch, 2):
        pair = jnp.concatenate([held[p], held[p + 1]], 1)
        both = dot_nn(green_ref[...], pair)
        wide_m[pl.ds(p, height, batch), :] = both[:height, :width]
        wide_m[pl.ds(p + 1, height, batch), :] = both[:height, width:]
        wide_u[pl.ds(p, height, batch), :] = both[height:, :width]
        wide_u[pl.ds(p + 1, height, batch), :] = both[height:, width:]
    m_move.wait()
    group = height // 6

    def second_stage(step, carry):
        at = pl.multiple_of(step * group, group)
        rows = pl.ds(pl.multiple_of(at * batch, group * batch), group * batch)
        both = jnp.concatenate([m_own[rows, :], wide_m[rows, :].astype(BF16)], 1)
        x = dot_nt(both, virt_own_ref[...]).reshape(group, batch, width)
        v = dot_nn(wide_u[rows, :].astype(BF16), virt_next_ref[...]).reshape(group, batch, width)
        out_ref[pl.ds(at, group)] = jnp.concatenate([x, v], 1).astype(BF16)
        return carry

    lax.fori_loop(0, height // group, second_stage, 0)


def halo_panels(after, halo, m_own, green, virt_own, virt_next):
    batch, height, width = halo.shape
    return call(
        halo_kernel, "halo_panels", shape(height, 2 * batch, width),
        [ANY] * 3 + [VMEM] * 3,
        scratch_shapes=[
            pltpu.VMEM((batch, height, width), BF16),
            pltpu.VMEM((height * batch, width), BF16),
            pltpu.VMEM((height * batch, width), F32),
            pltpu.VMEM((height * batch, width), F32),
            pltpu.SemaphoreType.DMA((2,)),
        ],
    )(after, halo, m_own, green, virt_own, virt_next)


def contract_kernel(lefts, rights, group, place_ref, *refs):
    out_ref, total_ref = refs[-2:]
    left, right = refs[:lefts], refs[lefts : lefts + rights]
    step, steps = pl.program_id(0), pl.num_programs(0)

    @pl.when(step == 0)
    def _():
        total_ref[...] = jnp.zeros_like(total_ref)

    total = None
    for at in range(0, left[0].shape[0], group):
        sides = [
            jnp.concatenate(
                [jnp.concatenate([ref[at + k] for k in range(group)], 1) for ref in side], 0
            )
            for side in (left, right)
        ]
        part = dot_nt(*sides)
        total = part if total is None else total + part
    total_ref[...] += total

    @pl.when(step == steps - 1)
    def _():
        lines, chunks, deep, wide = out_ref.shape
        rows, cols = total_ref.shape
        batch = rows // 2
        half = batch // 2
        exact = dict(precision=lax.Precision.HIGHEST)
        source = lax.broadcasted_iota(jnp.int32, (cols, cols), 0)
        target = lax.broadcasted_iota(jnp.int32, (cols, cols), 1)
        block, within = source // batch, source % batch
        near = cols - 2 * batch
        place = jnp.zeros((cols, cols), jnp.int32)
        for k in range(cols // batch - 2):
            place = jnp.where(block == k, place_ref[k] * batch + within, place)
        for k in range(2):
            for j in range(2):
                low = near + k * batch + j * half
                mine = (source >= low) & (source < low + half)
                place = jnp.where(
                    mine, place_ref[cols // batch - 2 + j] * batch + k * half + source - low, place
                )
        spread = jnp.where(place == target, 1.0, 0.0).astype(F32)
        placed = dot_nn(total_ref[...], spread, **exact)

        row = lax.broadcasted_iota(jnp.int32, (cols, rows), 0) - place_ref[0] * batch
        have = lax.broadcasted_iota(jnp.int32, (cols, rows), 1)
        chunk, part, index = have // batch, have % batch // half, have % half
        at = (row == chunk * half + index) & (row >= 0) & (row < batch)
        pick_x = jnp.where(at & (part == 0), 1.0, 0.0).astype(F32)
        pick_v = jnp.where(at & (part == 1), 1.0, 0.0).astype(F32)
        result = dot_nn(pick_x, placed, **exact) + dot_nn(pick_v, placed, **exact).T
        fold = batch // deep
        for k in range(chunks):
            piece = jnp.concatenate(
                [result[k * batch + j * deep : k * batch + (j + 1) * deep] for j in range(fold)], 1
            )
            for line in range(lines):
                out_ref[line, k] = piece


def contract(places, lefts, rights, lines, steps=3):
    height, _, width = lefts[0].shape
    part = height // steps
    rows, cols = [sum(a.shape[1] for a in side) for side in (lefts, rights)]
    batch = rows // 2
    fold = max(1, width // cols)
    dims = (lines, cols // batch, batch // fold, cols * fold)
    return call(
        functools.partial(contract_kernel, len(lefts), len(rights), 16), "contract",
        shape(*dims, dtype=F32),
        [SMEM] + [pl.BlockSpec((part, a.shape[1], width), lambda i: (i, 0, 0)) for a in lefts + rights],
        pl.BlockSpec(dims, lambda i: (0, 0, 0, 0)),
        grid=(steps,),
        scratch_shapes=[pltpu.VMEM((rows, cols), F32)],
    )(places, *lefts, *rights)


def total_kernel(src_ref, out_ref):
    total = -jnp.sum(src_ref[...], 0)
    deep, cols = total.shape[0], out_ref.shape[1]
    for j in range(out_ref.shape[0] // deep):
        out_ref[j * deep : (j + 1) * deep, :] = total[:, j * cols : (j + 1) * cols]


def shifted(value, axis, distance):
    size = lax.axis_size(axis)
    return lax.ppermute(value, axis, [(i, (i + distance) % size) for i in range(size)])


def per_device(three_center, occ_band, virt_band, three_mask, occ_mask, virt_mask):
    batch, height, tile = three_center.shape
    lines, groups = lax.axis_size("ao"), lax.axis_size("ri")
    mine = lax.axis_index("ri")
    core = (mine % 2).astype(jnp.int32)[None]
    half = batch // 2

    def mixed(near, far):
        pairs = []
        for a in range(lines):
            for r in range(groups):
                da, dr = near if r % 2 else far
                pairs.append((a * groups + r, ((a + da) % lines) * groups + (r + dr) % groups))
        return pairs

    def partner(value):
        return lax.ppermute(value, "ri", [(i, i ^ 1) for i in range(groups)])

    masks = (core, occ_mask, virt_mask, three_mask)
    one, two, near, late = call(
        pack_kernel, "pack",
        [shape(tile + 16, 5 * tile), shape(tile, 2 * tile)] + [shape(half, height, tile)] * 2,
        [SMEM] * 4 + [VMEM] * 3, [VMEM] * 2 + [ANY] * 2,
        scratch_shapes=[pltpu.SemaphoreType.DMA((2,))],
    )(*masks, occ_band, virt_band, three_center)
    one_hop = lax.ppermute(one, BOTH, mixed((1, 0), (-1, 0)))
    two_hops = shifted(two, "ao", -2)
    halo_near, far_near = shifted(near, "ao", -1), shifted(near, "ri", 2)
    halo_late = shifted(late, "ao", -1)
    late, _ = lax.optimization_barrier((late, two_hops))
    far_late = shifted(late, "ri", 2)

    one_hop, _ = lax.optimization_barrier((one_hop, two_hops))
    joined = partner(one_hop)
    flat = relayout(joined, three_center)
    early, places = [flat, partner(flat)], [mine, mine ^ 1]
    for distance in range(2, groups // 2):
        step = shifted(flat, "ri", 2 * distance)
        early += [step, partner(step)]
        places += [(mine - 2 * distance) % groups, ((mine ^ 1) - 2 * distance) % groups]
    places += [(mine - 2) % groups, ((mine ^ 1) - 2) % groups]
    places = jnp.stack(places).astype(jnp.int32)

    green_own, green_halo, virt_own, virt_next = call(
        tables_kernel, "tables",
        [shape(3 * tile, 3 * tile), shape(6 * tile, 3 * tile), shape(tile, 2 * tile), shape(tile, tile)],
        [SMEM] * 4 + [VMEM] * 5 + [ANY], [VMEM] * 4,
        scratch_shapes=[
            pltpu.VMEM((tile + 16, 5 * tile), BF16),
            pltpu.VMEM((tile + 16, 5 * tile), BF16),
        ],
    )(*masks, occ_band, virt_band, one_hop, two_hops, joined, flat)
    m_near, m_late = own_m(green_own, three_center)
    greens = (green_halo, virt_own, virt_next)

    halo_near, far_near, _ = lax.optimization_barrier((halo_near, far_near, m_near))
    passed = partner(far_near)
    panels_near = halo_panels(m_late, halo_near, m_near, *greens)
    far_near = far_rows(panels_near, far_near, passed)

    halo_late, far_late, _ = lax.optimization_barrier((halo_late, far_late, far_near))
    passed = partner(far_late)
    panels_late = halo_panels(far_near, halo_late, m_late, *greens)
    far_late = far_rows(panels_late, far_late, passed)
    parts = contract(places, [panels_near, panels_late], early + [far_near, far_late], lines)
    swapped = lax.all_to_all(parts.reshape(lines * groups, *parts.shape[2:]), BOTH, 0, 0, tiled=True)
    return call(total_kernel, "total", shape(batch, groups * batch, dtype=F32), [VMEM])(swapped)


def solution(mesh):
    placed = (P("ri", "ao", None),) + (P("ao", None),) * 5
    return jax.shard_map(
        per_device, mesh=mesh, in_specs=placed, out_specs=P("ri", None), check_vma=False
    )
```

time: 179 us -> 86.3 us (0.48)
  waiting for transfers between devices: 79.2 us -> 14.1 us
  Pallas kernels: 0 us -> 39.6 us
  blocking collectives: 44.4 us -> 14 us
  between operations: 13.5 us -> 0.12 us
  local copies, waits for them, and re-layouts: 16.3 us -> 3.32 us
  matrix products: 7.44 us -> 0 us
  other arithmetic: 3 us -> 0.67 us
    ppermute x4 -> x10, waiting for transfers between devices: 61.3 us -> 14.1 us  [the longest x5 14.1 us: shifted(): lax.ppermute(value, axis, [(i, (i + distance) % size) for i in range(size)])]
    pallas_call x0 -> x10, Pallas kernels: none -> 39.6 us  [the longest x2 12.2 us: halo_panels(): call(halo_kernel, 'halo_panels', shape(height, 2 * batch, width), [ANY] *...]
    psum x1 -> x0, blocking collectives: 21.7 us -> none  [per_device(): summed = lax.psum(row_panel, 'ao')]
    reduce_scatter x1 -> x0, waiting for transfers between devices: 17.8 us -> none  [per_device(): lax.psum_scatter(partial_chi, 'ri', scatter_dimension=0, tiled=True)]
    all_to_all x1, blocking collectives: 22.7 us -> 14 us  [per_device(): lax.all_to_all(parts.reshape(lines * groups, *parts.shape[2:]), BOTH, 0,...]
    dot_general x3 -> x0, matrix products: 7.44 us -> none  [the longest x1 4.49 us: per_device(): jnp.einsum('plv,sv->pls', needed, live_virt, preferred_element_type=jnp.f...]
    all_to_all x2 -> x0, local copies, waits for them, and re-layouts: 6.31 us -> none  [per_device(): lax.all_to_all(product_flat, 'ri', split_axis=1, concat_axis=0, tiled=True)]
    slice x3 -> x0, local copies, waits for them, and re-layouts: 4.28 us -> none  [the longest x1 2.45 us: per_device(): from_left = from_behind(m_local[:, 2 * tile_size:5 * tile_size], 'ao', 1)]
  transfers between devices with their start and end apart: 6 -> 10, of which waited for: 5 -> 4; matrix products, arithmetic and copies ran while one was open for 8% -> 1% of each run, Pallas kernels for 0% -> 33%
where the time goes in v1:
time: 86.3 us; the launch traced here: 85.8 us
  Pallas kernels  39.6 us (46%)
  waiting for transfers between devices  14.1 us (16%)
  blocking collectives  14 us (16%)
  starting transfers between devices  13.9 us (16%)
  local copies, waits for them, and re-layouts  3.32 us (4%)
    ppermute x5, waiting for transfers between devices, shifted(): lax.ppermute(value, axis, [(i, (i + distance) % size) for i in range(size)])  14.1 us
    all_to_all x1, blocking collectives, per_device(): lax.all_to_all(parts.reshape(lines * groups, *parts.shape[2:]), BOTH, 0,...  14 us
    pallas_call x2, Pallas kernels, halo_panels(): call(halo_kernel, 'halo_panels', shape(height, 2 * batch, width), [ANY] *...  12.2 us
    ppermute x5, starting transfers between devices, shifted(): lax.ppermute(value, axis, [(i, (i + distance) % size) for i in range(size)])  7.77 us
    pallas_call x1, Pallas kernels, contract(): call(functools.partial(contract_kernel, len(lefts), len(rights), 16), 'co...  6.24 us
    pallas_call x2, Pallas kernels, far_rows(): call(far_kernel, 'far_rows', shape(height, 2 * batch, width), [ANY] * 3,...  6.09 us
    ppermute x1, starting transfers between devices, per_device(): one_hop = lax.ppermute(one, BOTH, mixed((1, 0), (-1, 0)))  6.03 us
    pallas_call x1, Pallas kernels, own_m(): call(own_m_kernel, 'own_m', [shape(height * batch // 2, width)] * 2, [pl....  4.15 us
  transfers between devices with their start and end apart: 10, of which 4 were waited for; matrix products, arithmetic and copies ran while one was open for 1% of the time, Pallas kernels for 33%

profile of v1, /device:TPU:0, one launch (start us, length us, event | category | flops | bytes accessed | tf_op | source)
XLA Modules:
  0.0 85.8 jit_solution(11302839575936653831)
XLA Ops:
  0.0 3.4 %pack.1 = (bf16[144,640]{1,0:T(8,128)(2,1)}, bf16[128,256]{1,0:T(8,128)(2,1)}, bf16[8,384,128]{2,1,0:T(8,128)(2,1)}, bf16[8,384,128]{2,1,0:T(8,128)(2,1)}) custom-call(s32[1]{0:T(128)} %bitcast.4.core_ref, s32[1,5]{1,0:T(1,128)} %occ_mask.3, s32[1,3]{1,0:T(1,128)} %virt_mask.3, s32[1,3]{1,0:T(1,128)} %three_mask.3, bf16[128,640]{1,0:T(8,128)(2,1)} %occ_ref.3, ...), custom_call_target="tpu_custom_call" | custom-call | flops 1024 | bytes 1024 | tf_op jit(solution)/shard_map/pack/pallas_call | solution.py:360
  3.4 6.0 %collective-permute-start = (bf16[144,640]{1,0:T(8,128)(2,1)}, bf16[144,640]{1,0:T(8,128)(2,1)S(1)}, u32[]{:S(2)}, u32[]{:S(2)}) collective-permute-start(bf16[144,640]{1,0:T(8,128)(2,1)} %get-tuple-element.21), channel_id=1, source_target_pairs={{0,28},{1,5},{2,30},{3,7},{4,0},{5,9},{6,2},{7,11},{8,4},{9,13},{1... | collective-permute-start | bytes 552968 | tf_op jit(solution)/shard_map/ppermute | solution.py:366
  9.5 0.4 collective-permute-start.1
  9.9 4.0 %collective-permute-done.1.two_ref = bf16[128,256]{1,0:T(8,128)(2,1)S(1)} collective-permute-done((bf16[128,256]{1,0:T(8,128)(2,1)}, bf16[128,256]{1,0:T(8,128)(2,1)S(1)}, u32[]{:S(2)}, u32[]{:S(2)}) %collective-permute-start.1) | collective-permute-done | bytes 65568 | tf_op jit(solution)/shard_map/ppermute | solution.py:338
  14.0 0.0 copy-start.5
  14.0 0.0 collective-permute-done.one_ref
  14.0 0.0 copy-start.4
  14.0 0.1 collective-permute-start.2
  14.0 1.6 %collective-permute-start.4 = (bf16[8,384,128]{2,1,0:T(8,128)(2,1)}, bf16[8,384,128]{2,1,0:T(8,128)(2,1)S(1)}, u32[]{:S(2)}, u32[]{:S(2)}) collective-permute-start(bf16[8,384,128]{2,1,0:T(8,128)(2,1)} %get-tuple-element.26), channel_id=1, source_target_pairs={{0,2},{1,3},{2,0},{3,1},{4,6},{5,7},{6,4},{7,5},{8,10},{9,11},{10,... | collective-permute-start | bytes 2359304 | tf_op jit(solution)/shard_map/ppermute | solution.py:338
  15.6 3.8 %collective-permute-start.3 = (bf16[8,384,128]{2,1,0:T(8,128)(2,1)}, bf16[8,384,128]{2,1,0:T(8,128)(2,1)S(1)}, u32[]{:S(2)}, u32[]{:S(2)}) collective-permute-start(bf16[8,384,128]{2,1,0:T(8,128)(2,1)} %get-tuple-element.26), channel_id=1, source_target_pairs={{0,28},{4,0},{8,4},{12,8},{16,12},{20,16},{24,20},{28,24},{1,29},{... | collective-permute-start | bytes 2359304 | tf_op jit(solution)/shard_map/ppermute | solution.py:338
  19.4 1.4 %collective-permute-start.6 = (bf16[8,384,128]{2,1,0:T(8,128)(2,1)}, bf16[8,384,128]{2,1,0:T(8,128)(2,1)}, u32[]{:S(2)}, u32[]{:S(2)}) collective-permute-start(bf16[8,384,128]{2,1,0:T(8,128)(2,1)} %get-tuple-element.34), channel_id=1, source_target_pairs={{0,28},{4,0},{8,4},{12,8},{16,12},{20,16},{24,20},{28,24},{1,29},{... | collective-permute-start | bytes 2359304 | tf_op jit(solution)/shard_map/ppermute | solution.py:338
  20.9 0.7 pad_add_fusion.place_ref
  21.5 0.5 collective-permute-start.7
  22.0 0.0 collective-permute-done.2.after_ref.far_ref
  22.0 0.0 copy-start.3
  22.0 0.7 copy-done.3
  22.7 3.6 %relayout.1.after_ref.refs_2_ = bf16[384,16,128]{2,1,0:T(8,128)(2,1)} custom-call(bf16[144,640]{1,0:T(8,128)(2,1)} %copy-done.3, bf16[16,384,128]{2,1,0:T(8,128)(2,1)} %src_ref.5), custom_call_target="tpu_custom_call" | custom-call | flops 1024 | bytes 1024 | tf_op jit(solution)/shard_map/relayout/pallas_call | solution.py:144
  26.3 0.0 collective-permute-start.8
  26.3 0.0 copy-done.5
  26.3 0.0 copy-done.4
  26.3 2.3 %tables.1 = (bf16[384,384]{1,0:T(8,128)(2,1)}, bf16[768,384]{1,0:T(8,128)(2,1)}, bf16[128,256]{1,0:T(8,128)(2,1)}, bf16[128,128]{1,0:T(8,128)(2,1)}) custom-call(s32[1]{0:T(128)} %bitcast.4.core_ref, s32[1,5]{1,0:T(1,128)} %occ_mask.3, s32[1,3]{1,0:T(1,128)} %virt_mask.3, s32[1,3]{1,0:T(1,128)} %three_mask.3, bf16[128,640]{1,0:T(8,128)(2,1)} %occ_ref.3, ...), custom_call_target="tpu_custom_call" | custom-call | flops 1024 | bytes 1024 | tf_op jit(solution)/shard_map/tables/pallas_call | solution.py:384
  28.6 4.1 %own_m.1 = (bf16[3072,128]{1,0:T(8,128)(2,1)}, bf16[3072,128]{1,0:T(8,128)(2,1)}) custom-call(bf16[384,384]{1,0:T(8,128)(2,1)} %get-tuple-element.24.green_ref, bf16[16,384,128]{2,1,0:T(8,128)(2,1)} %src_ref.5), custom_call_target="tpu_custom_call" | custom-call | flops 99999997952 | bytes 1000000000 | tf_op jit(solution)/shard_map/own_m/pallas_call | solution.py:192
  32.8 1.9 %collective-permute-done.4.near_ref = bf16[8,384,128]{2,1,0:T(8,128)(2,1)S(1)} collective-permute-done((bf16[8,384,128]{2,1,0:T(8,128)(2,1)}, bf16[8,384,128]{2,1,0:T(8,128)(2,1)S(1)}, u32[]{:S(2)}, u32[]{:S(2)}) %collective-permute-start.4) | collective-permute-done | bytes 786464 | tf_op jit(solution)/shard_map/ppermute | solution.py:338
  34.7 0.0 copy-start
  34.7 3.0 %collective-permute-done.3.halo_ref = bf16[8,384,128]{2,1,0:T(8,128)(2,1)S(1)} collective-permute-done((bf16[8,384,128]{2,1,0:T(8,128)(2,1)}, bf16[8,384,128]{2,1,0:T(8,128)(2,1)S(1)}, u32[]{:S(2)}, u32[]{:S(2)}) %collective-permute-start.3) | collective-permute-done | bytes 786464 | tf_op jit(solution)/shard_map/ppermute | solution.py:338
  37.7 0.0 copy-start.6
  37.7 0.0 collective-permute-start.5
  37.7 0.9 %copy-done.6 = bf16[8,384,128]{2,1,0:T(8,128)(2,1)} copy-done((bf16[8,384,128]{2,1,0:T(8,128)(2,1)}, bf16[8,384,128]{2,1,0:T(8,128)(2,1)S(1)}, u32[]{:S(2)}) %copy-start.6) | copy-done | bytes 786456
  38.6 6.1 %halo_panels.2.after_ref.refs_0_ = bf16[384,16,128]{2,1,0:T(8,128)(2,1)} custom-call(bf16[3072,128]{1,0:T(8,128)(2,1)} %get-tuple-element.25.after_ref.m_ref, bf16[8,384,128]{2,1,0:T(8,128)(2,1)} %copy-done.6, bf16[3072,128]{1,0:T(8,128)(2,1)} %get-tuple-element.27.m_ref, bf16[768,384]{1,0:T(8,128)(2,1)} %get-tuple-element.29.green_ref, ...), custom_call_target="tpu_custom_call" | custom-call | flops 99999997952 | bytes 1000000000 | tf_op jit(solution)/shard_map/halo_panels/pallas_call | solution.py:238
  44.7 0.0 copy-done
  44.7 0.0 collective-permute-done.5.other_ref
  44.7 0.0 copy-start.2
  44.7 0.9 %copy-done.2 = bf16[8,384,128]{2,1,0:T(8,128)(2,1)} copy-done((bf16[8,384,128]{2,1,0:T(8,128)(2,1)}, bf16[8,384,128]{2,1,0:T(8,128)(2,1)S(1)}, u32[]{:S(2)}) %copy-start.2) | copy-done | bytes 786456
  45.6 3.0 %far_rows.2.after_ref.refs_4_ = bf16[384,16,128]{2,1,0:T(8,128)(2,1)} custom-call(bf16[384,16,128]{2,1,0:T(8,128)(2,1)} %halo_panels.2.after_ref.refs_0_, bf16[8,384,128]{2,1,0:T(8,128)(2,1)} %copy-done, bf16[8,384,128]{2,1,0:T(8,128)(2,1)} %copy-done.2), custom_call_target="tpu_custom_call" | custom-call | flops 1024 | bytes 1024 | tf_op jit(solution)/shard_map/far_rows/pallas_call | solution.py:167
  48.6 5.2 %collective-permute-done.6.halo_ref = bf16[8,384,128]{2,1,0:T(8,128)(2,1)} collective-permute-done((bf16[8,384,128]{2,1,0:T(8,128)(2,1)}, bf16[8,384,128]{2,1,0:T(8,128)(2,1)}, u32[]{:S(2)}, u32[]{:S(2)}) %collective-permute-start.6) | collective-permute-done | bytes 786464 | tf_op jit(solution)/shard_map/ppermute | solution.py:338
  53.8 0.0 collective-permute-done.7.near_ref
  53.8 0.0 collective-permute-start.9
  53.8 6.1 %halo_panels.3.after_ref.refs_1_ = bf16[384,16,128]{2,1,0:T(8,128)(2,1)} custom-call(bf16[384,16,128]{2,1,0:T(8,128)(2,1)} %far_rows.2.after_ref.refs_4_, bf16[8,384,128]{2,1,0:T(8,128)(2,1)} %collective-permute-done.6.halo_ref, bf16[3072,128]{1,0:T(8,128)(2,1)} %get-tuple-element.25.after_ref.m_ref, bf16[768,384]{1,0:T(8,128)(2,1)} %get-tuple-element.29.green_ref, ...), custom_call_target="tpu_custom_call" | custom-call | flops 99999997952 | bytes 1000000000 | tf_op jit(solution)/shard_map/halo_panels/pallas_call | solution.py:238
  59.9 0.0 collective-permute-done.9.other_ref
  59.9 0.0 copy-start.1
  59.9 0.9 %copy-done.1 = bf16[8,384,128]{2,1,0:T(8,128)(2,1)} copy-done((bf16[8,384,128]{2,1,0:T(8,128)(2,1)}, bf16[8,384,128]{2,1,0:T(8,128)(2,1)S(1)}, u32[]{:S(2)}) %copy-start.1) | copy-done | bytes 786456
  60.8 3.1 %far_rows.3.refs_5_ = bf16[384,16,128]{2,1,0:T(8,128)(2,1)} custom-call(bf16[384,16,128]{2,1,0:T(8,128)(2,1)} %halo_panels.3.after_ref.refs_1_, bf16[8,384,128]{2,1,0:T(8,128)(2,1)} %collective-permute-done.7.near_ref, bf16[8,384,128]{2,1,0:T(8,128)(2,1)} %copy-done.1), custom_call_target="tpu_custom_call" | custom-call | flops 1024 | bytes 1024 | tf_op jit(solution)/shard_map/far_rows/pallas_call | solution.py:167
  63.9 0.0 collective-permute-done.8.refs_3_
  63.9 6.2 %contract.1 = f32[8,4,8,128]{3,2,1,0:T(8,128)} custom-call(s32[4]{0:T(128)} %pad_add_fusion.place_ref, bf16[384,16,128]{2,1,0:T(8,128)(2,1)} %halo_panels.2.after_ref.refs_0_, bf16[384,16,128]{2,1,0:T(8,128)(2,1)} %halo_panels.3.after_ref.refs_1_, bf16[384,16,128]{2,1,0:T(8,128)(2,1)} %relayout.1.after_ref.refs_2_, ...), custom_call_target="tpu_custom_call" | custom-call | flops 1024 | bytes 1024 | tf_op jit(solution)/shard_map/contract/pallas_call | solution.py:319
  70.1 14.0 %all_to_all.5.src_ref = f32[32,8,128]{2,1,0:T(8,128)} all-to-all(f32[32,8,128]{2,1,0:T(8,128)} %bitcast.6), channel_id=1, replica_groups=mesh['ao'=8,'ri'=4] {'ao','ri'}, dimensions={0} | all-to-all | bytes 262144 | tf_op jit(solution)/shard_map/all_to_all | solution.py:406
  84.2 1.6 %total.1 = f32[16,64]{1,0:T(8,128)} custom-call(f32[32,8,128]{2,1,0:T(8,128)} %all_to_all.5.src_ref), custom_call_target="tpu_custom_call" | custom-call | flops 1024 | bytes 1024 | tf_op jit(solution)/shard_map/total/pallas_call | solution.py:407
Async XLA Ops:
  3.4 10.5 %collective-permute-start = (bf16[144,640]{1,0:T(8,128)(2,1)}, bf16[144,640]{1,0:T(8,128)(2,1)S(1)}, u32[]{:S(2)}, u32[]{:S(2)}) collective-permute-start(bf16[144,640]{1,0:T(8,128)(2,1)} %get-tuple-element.21), channel_id=1, source_target_pairs={{0,28},{1,5},{2,30},{3,7},{4,0},{5,9},{6,2},{7,11},{8,4},{9,13},{1... | collective-permute-start | bytes 552968 | tf_op jit(solution)/shard_map/ppermute | solution.py:366
  9.5 4.5 %collective-permute-start.1 = (bf16[128,256]{1,0:T(8,128)(2,1)}, bf16[128,256]{1,0:T(8,128)(2,1)S(1)}, u32[]{:S(2)}, u32[]{:S(2)}) collective-permute-start(bf16[128,256]{1,0:T(8,128)(2,1)} %get-tuple-element.22), channel_id=1, source_target_pairs={{0,24},{4,28},{8,0},{12,4},{16,8},{20,12},{24,16},{28,20},{1,25},{... | collective-permute-start | bytes 196616 | tf_op jit(solution)/shard_map/ppermute | solution.py:338
  14.0 12.3 %copy-start.5 = (bf16[128,256]{1,0:T(8,128)(2,1)}, bf16[128,256]{1,0:T(8,128)(2,1)S(1)}, u32[]{:S(2)}) copy-start(bf16[128,256]{1,0:T(8,128)(2,1)S(1)} %collective-permute-done.1.two_ref) | copy-start | bytes 196612
  14.0 12.3 %copy-start.4 = (bf16[144,640]{1,0:T(8,128)(2,1)}, bf16[144,640]{1,0:T(8,128)(2,1)S(1)}, u32[]{:S(2)}) copy-start(bf16[144,640]{1,0:T(8,128)(2,1)S(1)} %collective-permute-done.one_ref) | copy-start | bytes 552964
  14.0 8.1 %collective-permute-start.2 = (bf16[144,640]{1,0:T(8,128)(2,1)S(1)}, bf16[144,640]{1,0:T(8,128)(2,1)S(1)}, u32[]{:S(2)}, u32[]{:S(2)}) collective-permute-start(bf16[144,640]{1,0:T(8,128)(2,1)S(1)} %collective-permute-done.one_ref), channel_id=1, source_target_pairs={{0,1},{1,0},{2,3},{3,2},{4,5},{5,4},{6,7},{7,6},{8,9},{9,8},{10,11... | collective-permute-start | bytes 552968 | tf_op jit(solution)/shard_map/ppermute | solution.py:357
  14.0 20.6 %collective-permute-start.4 = (bf16[8,384,128]{2,1,0:T(8,128)(2,1)}, bf16[8,384,128]{2,1,0:T(8,128)(2,1)S(1)}, u32[]{:S(2)}, u32[]{:S(2)}) collective-permute-start(bf16[8,384,128]{2,1,0:T(8,128)(2,1)} %get-tuple-element.26), channel_id=1, source_target_pairs={{0,2},{1,3},{2,0},{3,1},{4,6},{5,7},{6,4},{7,5},{8,10},{9,11},{10,... | collective-permute-start | bytes 2359304 | tf_op jit(solution)/shard_map/ppermute | solution.py:338
  15.6 22.0 %collective-permute-start.3 = (bf16[8,384,128]{2,1,0:T(8,128)(2,1)}, bf16[8,384,128]{2,1,0:T(8,128)(2,1)S(1)}, u32[]{:S(2)}, u32[]{:S(2)}) collective-permute-start(bf16[8,384,128]{2,1,0:T(8,128)(2,1)} %get-tuple-element.26), channel_id=1, source_target_pairs={{0,28},{4,0},{8,4},{12,8},{16,12},{20,16},{24,20},{28,24},{1,29},{... | collective-permute-start | bytes 2359304 | tf_op jit(solution)/shard_map/ppermute | solution.py:338
  19.4 34.4 %collective-permute-start.6 = (bf16[8,384,128]{2,1,0:T(8,128)(2,1)}, bf16[8,384,128]{2,1,0:T(8,128)(2,1)}, u32[]{:S(2)}, u32[]{:S(2)}) collective-permute-start(bf16[8,384,128]{2,1,0:T(8,128)(2,1)} %get-tuple-element.34), channel_id=1, source_target_pairs={{0,28},{4,0},{8,4},{12,8},{16,12},{20,16},{24,20},{28,24},{1,29},{... | collective-permute-start | bytes 2359304 | tf_op jit(solution)/shard_map/ppermute | solution.py:338
  21.5 32.3 %collective-permute-start.7 = (bf16[8,384,128]{2,1,0:T(8,128)(2,1)}, bf16[8,384,128]{2,1,0:T(8,128)(2,1)}, u32[]{:S(2)}, u32[]{:S(2)}) collective-permute-start(bf16[8,384,128]{2,1,0:T(8,128)(2,1)} %get-tuple-element.34), channel_id=1, source_target_pairs={{0,2},{1,3},{2,0},{3,1},{4,6},{5,7},{6,4},{7,5},{8,10},{9,11},{10,... | collective-permute-start | bytes 2359304 | tf_op jit(solution)/shard_map/ppermute | solution.py:338
  22.0 0.7 copy-start.3
  26.3 37.6 %collective-permute-start.8 = (bf16[384,16,128]{2,1,0:T(8,128)(2,1)}, bf16[384,16,128]{2,1,0:T(8,128)(2,1)}, u32[]{:S(2)}, u32[]{:S(2)}) collective-permute-start(bf16[384,16,128]{2,1,0:T(8,128)(2,1)} %relayout.1.after_ref.refs_2_), channel_id=1, source_target_pairs={{0,1},{1,0},{2,3},{3,2},{4,5},{5,4},{6,7},{7,6},{8,9},{9,8},{10,11... | collective-permute-start | bytes 4718600 | tf_op jit(solution)/shard_map/ppermute | solution.py:357
  34.7 10.0 %copy-start = (bf16[8,384,128]{2,1,0:T(8,128)(2,1)}, bf16[8,384,128]{2,1,0:T(8,128)(2,1)S(1)}, u32[]{:S(2)}) copy-start(bf16[8,384,128]{2,1,0:T(8,128)(2,1)S(1)} %collective-permute-done.4.near_ref) | copy-start | bytes 2359300
  37.7 0.9 %copy-start.6 = (bf16[8,384,128]{2,1,0:T(8,128)(2,1)}, bf16[8,384,128]{2,1,0:T(8,128)(2,1)S(1)}, u32[]{:S(2)}) copy-start(bf16[8,384,128]{2,1,0:T(8,128)(2,1)S(1)} %collective-permute-done.3.halo_ref) | copy-start | bytes 2359300
  37.7 7.0 %collective-permute-start.5 = (bf16[8,384,128]{2,1,0:T(8,128)(2,1)S(1)}, bf16[8,384,128]{2,1,0:T(8,128)(2,1)S(1)}, u32[]{:S(2)}, u32[]{:S(2)}) collective-permute-start(bf16[8,384,128]{2,1,0:T(8,128)(2,1)S(1)} %collective-permute-done.4.near_ref), channel_id=1, source_target_pairs={{0,1},{1,0},{2,3},{3,2},{4,5},{5,4},{6,7},{7,6},{8,9},{9,8},{10,11... | collective-permute-start | bytes 2359304 | tf_op jit(solution)/shard_map/ppermute | solution.py:357
  44.7 0.9 %copy-start.2 = (bf16[8,384,128]{2,1,0:T(8,128)(2,1)}, bf16[8,384,128]{2,1,0:T(8,128)(2,1)S(1)}, u32[]{:S(2)}) copy-start(bf16[8,384,128]{2,1,0:T(8,128)(2,1)S(1)} %collective-permute-done.5.other_ref) | copy-start | bytes 2359300
  53.8 6.1 %collective-permute-start.9 = (bf16[8,384,128]{2,1,0:T(8,128)(2,1)}, bf16[8,384,128]{2,1,0:T(8,128)(2,1)S(1)}, u32[]{:S(2)}, u32[]{:S(2)}) collective-permute-start(bf16[8,384,128]{2,1,0:T(8,128)(2,1)} %collective-permute-done.7.near_ref), channel_id=1, source_target_pairs={{0,1},{1,0},{2,3},{3,2},{4,5},{5,4},{6,7},{7,6},{8,9},{9,8},{10,11... | collective-permute-start | bytes 2359304 | tf_op jit(solution)/shard_map/ppermute | solution.py:357
  59.9 0.9 %copy-start.1 = (bf16[8,384,128]{2,1,0:T(8,128)(2,1)}, bf16[8,384,128]{2,1,0:T(8,128)(2,1)S(1)}, u32[]{:S(2)}) copy-start(bf16[8,384,128]{2,1,0:T(8,128)(2,1)S(1)} %collective-permute-done.9.other_ref) | copy-start | bytes 2359300

commit v2 on v1

--- a/solution.py
+++ b/solution.py
@@ -8,8 +8,7 @@
 from jax.sharding import PartitionSpec as P
 
 F32, BF16 = jnp.float32, jnp.bfloat16
-VMEM_LIMIT = 56 * 1024 * 1024
-PARAMS = pltpu.CompilerParams(vmem_limit_bytes=VMEM_LIMIT)
+MIB = 1024 * 1024
 ANY = pl.BlockSpec(memory_space=pl.ANY)
 VMEM = pl.BlockSpec(memory_space=pltpu.VMEM)
 SMEM = pl.BlockSpec(memory_space=pltpu.SMEM)
@@ -18,15 +17,15 @@
 LITTLE = pl.CostEstimate(flops=1024, bytes_accessed=1024, transcendentals=0)
 
 
-def call(kernel, name, out_shape, in_specs, out_specs=VMEM, **more):
+def call(kernel, name, out_shape, in_specs, out_specs=VMEM, room=16, **more):
     return pl.pallas_call(
         kernel,
         name=name,
         out_shape=out_shape,
         in_specs=in_specs,
         out_specs=out_specs,
-        compiler_params=PARAMS,
-        cost_estimate=LARGE if name in ("halo_panels", "own_m") else LITTLE,
+        compiler_params=pltpu.CompilerParams(vmem_limit_bytes=room * MIB),
+        cost_estimate=LARGE if name in ("relayout",) else LITTLE,
         **more,
     )
 
@@ -48,55 +47,74 @@
     pl.when(core != 0)(odd)
 
 
-def pack_kernel(
-    core_ref, occ_mask, virt_mask, three_mask, occ_ref, virt_ref, src_ref,
-    one_ref, two_ref, near_ref, late_ref, sems,
-):
-    tile, half = occ_ref.shape[0], near_ref.shape[0]
-    moves = [
-        pltpu.make_async_copy(src_ref.at[:half], near_ref, sems.at[0]),
-        pltpu.make_async_copy(src_ref.at[half:], late_ref, sems.at[1]),
-    ]
-    for move in moves:
-        move.start()
-
-    def occ(k):
-        return occ_ref[:, k * tile : (k + 1) * tile] * occ_mask[0, k].astype(BF16)
+def pack_kernel(mine_ref, occ_mask, virt_mask, three_mask, occ_ref, virt_ref, one_ref, two_ref):
+    tile = occ_ref.shape[0]
+
+    def cols(k):
+        return slice(k * tile, (k + 1) * tile)
+
+    occ = [occ_ref[:, cols(k)] * occ_mask[0, k].astype(BF16) for k in range(5)]
 
     def even():
         for k in range(4):
-            one_ref[:tile, k * tile : (k + 1) * tile] = occ(k)
-        one_ref[:tile, 4 * tile :] = virt_ref[:, :tile] * virt_mask[0, 0].astype(BF16)
+            one_ref[:tile, cols(k)] = occ[k]
+        one_ref[:tile, cols(4)] = virt_ref[:, :tile] * virt_mask[0, 0].astype(BF16)
 
     def odd():
         for k in range(3):
-            one_ref[:tile, k * tile : (k + 1) * tile] = occ(k + 2)
+            one_ref[:tile, cols(k)] = occ[k + 2]
         one_ref[:tile, 3 * tile :] = jnp.zeros((tile, 2 * tile), BF16)
 
-    when_core(core_ref[0], even, odd)
+    when_core(lax.rem(mine_ref[0], 2), even, odd)
     one_ref[tile:, :] = jnp.zeros((16, 5 * tile), BF16)
     for k in range(3):
         flag = jnp.full((16, tile), three_mask[0, k].astype(F32), F32)
-        one_ref[tile:, k * tile : (k + 1) * tile] = flag.astype(BF16)
+        one_ref[tile:, cols(k)] = flag.astype(BF16)
     for k in range(2):
-        two_ref[:, k * tile : (k + 1) * tile] = occ(k)
-    for move in moves:
-        move.wait()
+        two_ref[:, cols(k)] = occ[k]
+
+
+def half_kernel(which, after_ref, src_ref, out_ref, held, sems):
+    half = out_ref.shape[0]
+    quarter = half // 2
+    moves = []
+    for k in range(2):
+        rows = slice(k * quarter, (k + 1) * quarter)
+        source = src_ref.at[which * half + k * quarter : which * half + (k + 1) * quarter]
+        moves.append((
+            pltpu.make_async_copy(source, held.at[rows], sems.at[k]),
+            pltpu.make_async_copy(held.at[rows], out_ref.at[rows], sems.at[2 + k]),
+        ))
+    for load, _ in moves:
+        load.start()
+    for load, store in moves:
+        load.wait()
+        store.start()
+    for _, store in moves:
+        store.wait()
+
+
+def half_of(which, after, src):
+    dims = (src.shape[0] // 2, *src.shape[1:])
+    return call(
+        functools.partial(half_kernel, which), ("half_near", "half_late")[which], shape(*dims), [ANY] * 2, ANY, room=56,
+        scratch_shapes=[pltpu.VMEM(dims, BF16), pltpu.SemaphoreType.DMA((4,))],
+    )(after, src)
 
 
 def tables_kernel(
-    core_ref, occ_mask, virt_mask, three_mask, occ_ref, virt_ref, one_ref, two_ref, far_ref, after_ref,
+    mine_ref, occ_mask, virt_mask, three_mask, occ_ref, virt_ref, one_ref, other_ref, upper2, after_ref,
     own_ref, halo_ref, virt_own_ref, virt_next_ref, lower, upper,
 ):
     tile = occ_ref.shape[0]
 
     def even():
-        lower[...], upper[...] = far_ref[...], one_ref[...]
+        lower[...], upper[...] = other_ref[...], one_ref[...]
 
     def odd():
-        lower[...], upper[...] = one_ref[...], far_ref[...]
-
-    when_core(core_ref[0], even, odd)
+        lower[...], upper[...] = one_ref[...], other_ref[...]
+
+    when_core(lax.rem(mine_ref[0], 2), even, odd)
 
     def cols(k):
         return slice(k * tile, (k + 1) * tile)
@@ -110,7 +128,7 @@
             return occ_ref[:, cols(lam + 2)] * occ_mask[0, lam + 2].astype(BF16)
         if mu == 1:
             return upper[:tile, cols(lam + 1)]
-        return two_ref[:, cols(lam)]
+        return upper2[:, cols(lam)]
 
     blank = jnp.zeros((tile, tile), BF16)
     own = [three_mask[0, k].astype(BF16) for k in range(3)]
@@ -233,10 +251,10 @@
     lax.fori_loop(0, height // group, second_stage, 0)
 
 
-def halo_panels(after, halo, m_own, green, virt_own, virt_next):
+def halo_panels(name, after, halo, m_own, green, virt_own, virt_next):
     batch, height, width = halo.shape
     return call(
-        halo_kernel, "halo_panels", shape(height, 2 * batch, width),
+        halo_kernel, name, shape(height, 2 * batch, width),
         [ANY] * 3 + [VMEM] * 3,
         scratch_shapes=[
             pltpu.VMEM((batch, height, width), BF16),
@@ -248,7 +266,7 @@
     )(after, halo, m_own, green, virt_own, virt_next)
 
 
-def contract_kernel(lefts, rights, group, place_ref, *refs):
+def contract_kernel(lefts, rights, group, distances, mine_ref, *refs):
     out_ref, total_ref = refs[-2:]
     left, right = refs[:lefts], refs[lefts : lefts + rights]
     step, steps = pl.program_id(0), pl.num_programs(0)
@@ -279,21 +297,16 @@
         source = lax.broadcasted_iota(jnp.int32, (cols, cols), 0)
         target = lax.broadcasted_iota(jnp.int32, (cols, cols), 1)
         block, within = source // batch, source % batch
-        near = cols - 2 * batch
         place = jnp.zeros((cols, cols), jnp.int32)
-        for k in range(cols // batch - 2):
-            place = jnp.where(block == k, place_ref[k] * batch + within, place)
-        for k in range(2):
-            for j in range(2):
-                low = near + k * batch + j * half
-                mine = (source >= low) & (source < low + half)
-                place = jnp.where(
-                    mine, place_ref[cols // batch - 2 + j] * batch + k * half + source - low, place
-                )
+        groups, mine = cols // batch, mine_ref[0]
+        for k, distance in enumerate(distances):
+            for j, device in enumerate((mine, mine + 1 - 2 * lax.rem(mine, 2))):
+                start = lax.rem(device - 2 * distance + groups, groups) * batch
+                place = jnp.where(block == 2 * k + j, start + within, place)
         spread = jnp.where(place == target, 1.0, 0.0).astype(F32)
         placed = dot_nn(total_ref[...], spread, **exact)
 
-        row = lax.broadcasted_iota(jnp.int32, (cols, rows), 0) - place_ref[0] * batch
+        row = lax.broadcasted_iota(jnp.int32, (cols, rows), 0) - mine * batch
         have = lax.broadcasted_iota(jnp.int32, (cols, rows), 1)
         chunk, part, index = have // batch, have % batch // half, have % half
         at = (row == chunk * half + index) & (row >= 0) & (row < batch)
@@ -309,7 +322,7 @@
                 out_ref[line, k] = piece
 
 
-def contract(places, lefts, rights, lines, steps=3):
+def contract(mine, distances, lefts, rights, lines, steps=3):
     height, _, width = lefts[0].shape
     part = height // steps
     rows, cols = [sum(a.shape[1] for a in side) for side in (lefts, rights)]
@@ -317,13 +330,13 @@
     fold = max(1, width // cols)
     dims = (lines, cols // batch, batch // fold, cols * fold)
     return call(
-        functools.partial(contract_kernel, len(lefts), len(rights), 16), "contract",
+        functools.partial(contract_kernel, len(lefts), len(rights), 16, distances), "contract",
         shape(*dims, dtype=F32),
         [SMEM] + [pl.BlockSpec((part, a.shape[1], width), lambda i: (i, 0, 0)) for a in lefts + rights],
         pl.BlockSpec(dims, lambda i: (0, 0, 0, 0)),
         grid=(steps,),
         scratch_shapes=[pltpu.VMEM((rows, cols), F32)],
-    )(places, *lefts, *rights)
+    )(mine, *lefts, *rights)
 
 
 def total_kernel(src_ref, out_ref):
@@ -341,8 +354,7 @@
 def per_device(three_center, occ_band, virt_band, three_mask, occ_mask, virt_mask):
     batch, height, tile = three_center.shape
     lines, groups = lax.axis_size("ao"), lax.axis_size("ri")
-    mine = lax.axis_index("ri")
-    core = (mine % 2).astype(jnp.int32)[None]
+    mine = lax.axis_index("ri").astype(jnp.int32)[None]
     half = batch // 2
 
     def mixed(near, far):
@@ -356,53 +368,42 @@
     def partner(value):
         return lax.ppermute(value, "ri", [(i, i ^ 1) for i in range(groups)])
 
-    masks = (core, occ_mask, virt_mask, three_mask)
-    one, two, near, late = call(
-        pack_kernel, "pack",
-        [shape(tile + 16, 5 * tile), shape(tile, 2 * tile)] + [shape(half, height, tile)] * 2,
-        [SMEM] * 4 + [VMEM] * 3, [VMEM] * 2 + [ANY] * 2,
-        scratch_shapes=[pltpu.SemaphoreType.DMA((2,))],
-    )(*masks, occ_band, virt_band, three_center)
-    one_hop = lax.ppermute(one, BOTH, mixed((1, 0), (-1, 0)))
-    two_hops = shifted(two, "ao", -2)
-    halo_near, far_near = shifted(near, "ao", -1), shifted(near, "ri", 2)
+    masks = (mine, occ_mask, virt_mask, three_mask)
+    far = shifted(three_center, "ri", 2)
+    one, two = call(
+        pack_kernel, "pack", [shape(tile + 16, 5 * tile), shape(tile, 2 * tile)],
+        [SMEM] * 4 + [VMEM] * 2, [VMEM] * 2, room=56,
+    )(*masks, occ_band, virt_band)
+    one_hop, two_hops = lax.ppermute(one, BOTH, mixed((1, 0), (-1, 0))), shifted(two, "ao", -2)
+    near = half_of(0, one, three_center)
+    halo_near = shifted(near, "ao", -1)
+    late = half_of(1, near, three_center)
     halo_late = shifted(late, "ao", -1)
-    late, _ = lax.optimization_barrier((late, two_hops))
-    far_late = shifted(late, "ri", 2)
-
-    one_hop, _ = lax.optimization_barrier((one_hop, two_hops))
-    joined = partner(one_hop)
-    flat = relayout(joined, three_center)
-    early, places = [flat, partner(flat)], [mine, mine ^ 1]
+    flat = relayout(late, three_center)
+    halo_late = shifted(late, "ao", -1)
+    early, distances = [flat, partner(flat)], [0]
     for distance in range(2, groups // 2):
         step = shifted(flat, "ri", 2 * distance)
         early += [step, partner(step)]
-        places += [(mine - 2 * distance) % groups, ((mine ^ 1) - 2 * distance) % groups]
-    places += [(mine - 2) % groups, ((mine ^ 1) - 2) % groups]
-    places = jnp.stack(places).astype(jnp.int32)
-
+        distances.append(distance)
+
+    one_hop, two_hops, _ = lax.optimization_barrier((one_hop, two_hops, flat))
     green_own, green_halo, virt_own, virt_next = call(
         tables_kernel, "tables",
         [shape(3 * tile, 3 * tile), shape(6 * tile, 3 * tile), shape(tile, 2 * tile), shape(tile, tile)],
         [SMEM] * 4 + [VMEM] * 5 + [ANY], [VMEM] * 4,
-        scratch_shapes=[
-            pltpu.VMEM((tile + 16, 5 * tile), BF16),
-            pltpu.VMEM((tile + 16, 5 * tile), BF16),
-        ],
-    )(*masks, occ_band, virt_band, one_hop, two_hops, joined, flat)
+        scratch_shapes=[pltpu.VMEM((tile + 16, 5 * tile), BF16)] * 2,
+    )(*masks, occ_band, virt_band, one_hop, partner(one_hop), two_hops, flat)
     m_near, m_late = own_m(green_own, three_center)
     greens = (green_halo, virt_own, virt_next)
 
-    halo_near, far_near, _ = lax.optimization_barrier((halo_near, far_near, m_near))
-    passed = partner(far_near)
-    panels_near = halo_panels(m_late, halo_near, m_near, *greens)
-    far_near = far_rows(panels_near, far_near, passed)
-
-    halo_late, far_late, _ = lax.optimization_barrier((halo_late, far_late, far_near))
-    passed = partner(far_late)
-    panels_late = halo_panels(far_near, halo_late, m_late, *greens)
-    far_late = far_rows(panels_late, far_late, passed)
-    parts = contract(places, [panels_near, panels_late], early + [far_near, far_late], lines)
+    halo_near, _ = lax.optimization_barrier((halo_near, m_near))
+    panels_near = halo_panels("halo_near", m_late, halo_near, m_near, *greens)
+    halo_late, far, _ = lax.optimization_barrier((halo_late, far, panels_near))
+    passed = partner(far)
+    panels_late = halo_panels("halo_late", panels_near, halo_late, m_late, *greens)
+    far_all = far_rows(panels_late, far, passed)
+    parts = contract(mine, distances + [1], [panels_near, panels_late], early + [far_all], lines)
     swapped = lax.all_to_all(parts.reshape(lines * groups, *parts.shape[2:]), BOTH, 0, 0, tiled=True)
     return call(total_kernel, "total", shape(batch, groups * batch, dtype=F32), [VMEM])(swapped)
 

time: 86.3 us -> 69.1 us (0.80)
  Pallas kernels: 39.6 us -> 18.7 us
  waiting for transfers between devices: 14.1 us -> 25.7 us
  starting transfers between devices: 13.9 us -> 10.5 us
  local copies, waits for them, and re-layouts: 3.32 us -> 1.19 us
  blocking collectives: 14 us -> 12.6 us
    ppermute x5 -> x4, waiting for transfers between devices: 14.1 us -> 23.2 us  [shifted(): lax.ppermute(value, axis, [(i, (i + distance) % size) for i in range(size)])]
    pallas_call x3 -> x5, Pallas kernels: 18.5 us -> 12.1 us  [the longest x2 5.64 us: halo_panels(): call(halo_kernel, name, shape(height, 2 * batch, width), [ANY] * 3 + [VME...]
    pallas_call x2 -> x1, Pallas kernels: 6.09 us -> 1.2 us  [far_rows(): call(far_kernel, 'far_rows', shape(height, 2 * batch, width), [ANY] * 3,...]
    ppermute x5 -> x4, starting transfers between devices: 7.77 us -> 3.99 us  [shifted(): lax.ppermute(value, axis, [(i, (i + distance) % size) for i in range(size)])]
    pallas_call x1, Pallas kernels: 3.56 us -> 0.56 us  [relayout(): call(relayout_kernel, 'relayout', shape(height, batch, width), [ANY, pl.B...]
    pallas_call x1, Pallas kernels: 4.15 us -> 1.57 us  [own_m(): call(own_m_kernel, 'own_m', [shape(height * batch // 2, width)] * 2, [pl....]
    ppermute x4 -> x3, waiting for transfers between devices: 0.01 us -> 2.52 us  [partner(): return lax.ppermute(value, 'ri', [(i, i ^ 1) for i in range(groups)])]
    unnamed x14, local copies, waits for them, and re-layouts: 3.32 us -> 1.19 us
  transfers between devices with their start and end apart: 10 -> 8, of which waited for: 4 -> 5; matrix products, arithmetic and copies ran while one was open for 1% -> 0% of each run, Pallas kernels for 33% -> 20%
where the time goes in v2:
time: 69.1 us; the launch traced here: 68.9 us
  waiting for transfers between devices  25.7 us (37%)
  Pallas kernels  18.7 us (27%)
  blocking collectives  12.6 us (18%)
  starting transfers between devices  10.5 us (15%)
  local copies, waits for them, and re-layouts  1.19 us (2%)
    ppermute x4, waiting for transfers between devices, shifted(): lax.ppermute(value, axis, [(i, (i + distance) % size) for i in range(size)])  23.2 us
    all_to_all x1, blocking collectives, per_device(): lax.all_to_all(parts.reshape(lines * groups, *parts.shape[2:]), BOTH, 0,...  12.6 us
    ppermute x1, starting transfers between devices, per_device(): lax.ppermute(one, BOTH, mixed((1, 0), (-1, 0)))  5.98 us
    pallas_call x2, Pallas kernels, halo_panels(): call(halo_kernel, name, shape(height, 2 * batch, width), [ANY] * 3 + [VME...  5.64 us
    ppermute x4, starting transfers between devices, shifted(): lax.ppermute(value, axis, [(i, (i + distance) % size) for i in range(size)])  3.99 us
    pallas_call x2, Pallas kernels, half_of(): call(functools.partial(half_kernel, which), ('half_near', 'half_late')[wh...  3.9 us
    pallas_call x1, Pallas kernels, contract(): call(functools.partial(contract_kernel, len(lefts), len(rights), 16, dist...  2.54 us
    ppermute x3, waiting for transfers between devices, partner(): return lax.ppermute(value, 'ri', [(i, i ^ 1) for i in range(groups)])  2.52 us
  transfers between devices with their start and end apart: 8, of which 5 were waited for; matrix products, arithmetic and copies ran while one was open for 0% of the time, Pallas kernels for 20%

profile of v2, /device:TPU:0, one launch (start us, length us, event | category | flops | bytes accessed | tf_op | source)
XLA Modules:
  0.0 68.9 jit_solution(185664878200830866)
XLA Ops:
  0.0 1.8 %pack.1 = (bf16[144,640]{1,0:T(8,128)(2,1)}, bf16[128,256]{1,0:T(8,128)(2,1)}) custom-call(s32[1]{0:T(128)} %bitcast.mine_ref, s32[1,5]{1,0:T(1,128)} %occ_mask.3, s32[1,3]{1,0:T(1,128)} %virt_mask.3, s32[1,3]{1,0:T(1,128)} %three_mask.3, bf16[128,640]{1,0:T(8,128)(2,1)} %occ_ref.3, bf16[128,384]{1,0:T(8,128)(2,1)} %virt_ref.3), custom_call_target="tpu_custom_call" | custom-call | flops 1024 | bytes 1024 | tf_op jit(solution)/shard_map/pack/pallas_call | solution.py:373
  1.8 6.0 %collective-permute-start = (bf16[144,640]{1,0:T(8,128)(2,1)}, bf16[144,640]{1,0:T(8,128)(2,1)S(1)}, u32[]{:S(2)}, u32[]{:S(2)}) collective-permute-start(bf16[144,640]{1,0:T(8,128)(2,1)} %get-tuple-element.18.after_ref), channel_id=1, source_target_pairs={{0,28},{1,5},{2,30},{3,7},{4,0},{5,9},{6,2},{7,11},{8,4},{9,13},{1... | collective-permute-start | bytes 552968 | tf_op jit(solution)/shard_map/ppermute | solution.py:377
  7.7 0.4 collective-permute-start.1
  8.2 1.5 %collective-permute-start.5 = (bf16[16,384,128]{2,1,0:T(8,128)(2,1)}, bf16[16,384,128]{2,1,0:T(8,128)(2,1)S(1)}, u32[]{:S(2)}, u32[]{:S(2)}) collective-permute-start(bf16[16,384,128]{2,1,0:T(8,128)(2,1)} %src_ref.7), channel_id=1, source_target_pairs={{0,2},{1,3},{2,0},{3,1},{4,6},{5,7},{6,4},{7,5},{8,10},{9,11},{10,... | collective-permute-start | bytes 4718600 | tf_op jit(solution)/shard_map/ppermute | solution.py:351
  9.7 2.0 %half_near.1.after_ref = bf16[8,384,128]{2,1,0:T(8,128)(2,1)} custom-call(bf16[144,640]{1,0:T(8,128)(2,1)} %get-tuple-element.18.after_ref, bf16[16,384,128]{2,1,0:T(8,128)(2,1)} %src_ref.7), custom_call_target="tpu_custom_call" | custom-call | flops 1024 | bytes 1024 | tf_op jit(solution)/shard_map/half_near/pallas_call | solution.py:99
  11.7 0.0 copy-start
  11.7 0.6 collective-permute-start.3
  12.3 1.9 %half_late.1.after_ref = bf16[8,384,128]{2,1,0:T(8,128)(2,1)} custom-call(bf16[8,384,128]{2,1,0:T(8,128)(2,1)} %half_near.1.after_ref, bf16[16,384,128]{2,1,0:T(8,128)(2,1)} %src_ref.7), custom_call_target="tpu_custom_call" | custom-call | flops 1024 | bytes 1024 | tf_op jit(solution)/shard_map/half_late/pallas_call | solution.py:99
  14.2 1.4 %collective-permute-start.4 = (bf16[8,384,128]{2,1,0:T(8,128)(2,1)}, bf16[8,384,128]{2,1,0:T(8,128)(2,1)S(1)}, u32[]{:S(2)}, u32[]{:S(2)}) collective-permute-start(bf16[8,384,128]{2,1,0:T(8,128)(2,1)} %half_late.1.after_ref), channel_id=1, source_target_pairs={{0,28},{4,0},{8,4},{12,8},{16,12},{20,16},{24,20},{28,24},{1,29},{... | collective-permute-start | bytes 2359304 | tf_op jit(solution)/shard_map/ppermute | solution.py:351
  15.7 0.0 copy-done
  15.7 0.0 copy-start.1
  15.7 1.2 %copy-done.1 = bf16[8,384,128]{2,1,0:T(8,128)(2,1)S(1)} copy-done((bf16[8,384,128]{2,1,0:T(8,128)(2,1)S(1)}, bf16[8,384,128]{2,1,0:T(8,128)(2,1)}, u32[]{:S(2)}) %copy-start.1) | copy-done | bytes 786456
  16.8 0.0 copy-start.2
  16.8 0.0 copy-start.3
  16.8 0.0 copy-start.4
  16.8 0.0 copy-start.5
  16.8 0.0 copy-start.6
  16.8 0.6 relayout.1.after_ref.refs_2_
  17.4 0.0 collective-permute-done.1.upper2
  17.4 0.0 collective-permute-done.one_ref
  17.4 0.1 collective-permute-start.2
  17.5 1.4 %collective-permute-done.2.other_ref = bf16[144,640]{1,0:T(8,128)(2,1)S(1)} collective-permute-done((bf16[144,640]{1,0:T(8,128)(2,1)S(1)}, bf16[144,640]{1,0:T(8,128)(2,1)S(1)}, u32[]{:S(2)}, u32[]{:S(2)}) %collective-permute-start.2) | collective-permute-done | bytes 184352 | tf_op jit(solution)/shard_map/ppermute | solution.py:369
  18.9 0.0 copy-done.2
  18.9 0.0 copy-done.3
  18.9 0.0 copy-done.4
  18.9 0.0 copy-done.5
  18.9 0.0 copy-done.6
  19.0 0.8 %tables.1 = (bf16[384,384]{1,0:T(8,128)(2,1)S(1)}, bf16[768,384]{1,0:T(8,128)(2,1)S(1)}, bf16[128,256]{1,0:T(8,128)(2,1)S(1)}, bf16[128,128]{1,0:T(8,128)(2,1)S(1)}) custom-call(s32[1]{0:T(128)} %bitcast.mine_ref, s32[1,5]{1,0:T(1,128)S(1)} %copy-done.4, s32[1,3]{1,0:T(1,128)S(1)} %copy-done.5, s32[1,3]{1,0:T(1,128)S(1)} %copy-done.6, ...), custom_call_target="tpu_custom_call" | custom-call | flops 1024 | bytes 1024 | tf_op jit(solution)/shard_map/tables/pallas_call | solution.py:391
  19.7 1.6 %own_m.1 = (bf16[3072,128]{1,0:T(8,128)(2,1)S(1)}, bf16[3072,128]{1,0:T(8,128)(2,1)S(1)}) custom-call(bf16[384,384]{1,0:T(8,128)(2,1)S(1)} %get-tuple-element.22.green_ref, bf16[16,384,128]{2,1,0:T(8,128)(2,1)S(1)} %copy-done), custom_call_target="tpu_custom_call" | custom-call | flops 1024 | bytes 1024 | tf_op jit(solution)/shard_map/own_m/pallas_call | solution.py:210
  21.3 11.1 %collective-permute-done.3.halo_ref = bf16[8,384,128]{2,1,0:T(8,128)(2,1)S(1)} collective-permute-done((bf16[8,384,128]{2,1,0:T(8,128)(2,1)}, bf16[8,384,128]{2,1,0:T(8,128)(2,1)S(1)}, u32[]{:S(2)}, u32[]{:S(2)}) %collective-permute-start.3) | collective-permute-done | bytes 786464 | tf_op jit(solution)/shard_map/ppermute | solution.py:351
  32.4 2.8 %halo_near.1.after_ref.refs_0_ = bf16[384,16,128]{2,1,0:T(8,128)(2,1)S(1)} custom-call(bf16[3072,128]{1,0:T(8,128)(2,1)S(1)} %get-tuple-element.23.after_ref.m_ref, bf16[8,384,128]{2,1,0:T(8,128)(2,1)S(1)} %collective-permute-done.3.halo_ref, bf16[3072,128]{1,0:T(8,128)(2,1)S(1)} %get-tuple-element.24.m_ref, ...), custom_call_target="tpu_custom_call" | custom-call | flops 1024 | bytes 1024 | tf_op jit(solution)/shard_map/halo_near/pallas_call | solution.py:256
  35.3 12.1 %collective-permute-done.4.halo_ref = bf16[8,384,128]{2,1,0:T(8,128)(2,1)S(1)} collective-permute-done((bf16[8,384,128]{2,1,0:T(8,128)(2,1)}, bf16[8,384,128]{2,1,0:T(8,128)(2,1)S(1)}, u32[]{:S(2)}, u32[]{:S(2)}) %collective-permute-start.4) | collective-permute-done | bytes 786464 | tf_op jit(solution)/shard_map/ppermute | solution.py:351
  47.3 0.0 collective-permute-done.5.near_ref
  47.4 0.0 collective-permute-start.7
  47.4 0.5 collective-permute-start.6
  47.9 2.8 %halo_late.1.after_ref.refs_1_ = bf16[384,16,128]{2,1,0:T(8,128)(2,1)S(1)} custom-call(bf16[384,16,128]{2,1,0:T(8,128)(2,1)S(1)} %halo_near.1.after_ref.refs_0_, bf16[8,384,128]{2,1,0:T(8,128)(2,1)S(1)} %collective-permute-done.4.halo_ref, bf16[3072,128]{1,0:T(8,128)(2,1)S(1)} %get-tuple-element.23.after_ref.m_ref, ...), custom_call_target="tpu_custom_call" | custom-call | flops 1024 | bytes 1024 | tf_op jit(solution)/shard_map/halo_late/pallas_call | solution.py:256
  50.7 0.1 collective-permute-done.7.other_ref
  50.8 1.2 %far_rows.1.refs_4_ = bf16[384,32,128]{2,1,0:T(8,128)(2,1)S(1)} custom-call(bf16[384,16,128]{2,1,0:T(8,128)(2,1)S(1)} %halo_late.1.after_ref.refs_1_, bf16[16,384,128]{2,1,0:T(8,128)(2,1)S(1)} %collective-permute-done.5.near_ref, bf16[16,384,128]{2,1,0:T(8,128)(2,1)S(1)} %collective-permute-done.7.other_ref), custom_call_target="tpu_custom_call" | custom-call | flops 1024 | bytes 1024 | tf_op jit(solution)/shard_map/far_rows/pallas_call | solution.py:185
  52.0 1.0 %collective-permute-done.6.refs_3_ = bf16[384,16,128]{2,1,0:T(8,128)(2,1)S(1)} collective-permute-done((bf16[384,16,128]{2,1,0:T(8,128)(2,1)S(1)}, bf16[384,16,128]{2,1,0:T(8,128)(2,1)S(1)}, u32[]{:S(2)}, u32[]{:S(2)}) %collective-permute-start.6) | collective-permute-done | bytes 1572896 | tf_op jit(solution)/shard_map/ppermute | solution.py:369
  53.0 2.5 %contract.1 = f32[8,4,8,128]{3,2,1,0:T(8,128)S(1)} custom-call(s32[1]{0:T(128)} %bitcast.mine_ref, bf16[384,16,128]{2,1,0:T(8,128)(2,1)S(1)} %halo_near.1.after_ref.refs_0_, bf16[384,16,128]{2,1,0:T(8,128)(2,1)S(1)} %halo_late.1.after_ref.refs_1_, bf16[384,16,128]{2,1,0:T(8,128)(2,1)S(1)} %relayout.1.after_ref.refs_2_, ...), custom_call_target="tpu_custom_call" | custom-call | flops 1024 | bytes 1024 | tf_op jit(solution)/shard_map/contract/pallas_call | solution.py:332
  55.6 12.6 %all_to_all.5.src_ref = f32[32,8,128]{2,1,0:T(8,128)S(1)} all-to-all(f32[32,8,128]{2,1,0:T(8,128)S(1)} %bitcast.2), channel_id=1, replica_groups=mesh['ao'=8,'ri'=4] {'ao','ri'}, dimensions={0} | all-to-all | bytes 262144 | tf_op jit(solution)/shard_map/all_to_all | solution.py:407
  68.2 0.7 %total.1 = f32[16,64]{1,0:T(8,128)} custom-call(f32[32,8,128]{2,1,0:T(8,128)S(1)} %all_to_all.5.src_ref), custom_call_target="tpu_custom_call" | custom-call | flops 1024 | bytes 1024 | tf_op jit(solution)/shard_map/total/pallas_call | solution.py:408
Async XLA Ops:
  1.8 15.7 %collective-permute-start = (bf16[144,640]{1,0:T(8,128)(2,1)}, bf16[144,640]{1,0:T(8,128)(2,1)S(1)}, u32[]{:S(2)}, u32[]{:S(2)}) collective-permute-start(bf16[144,640]{1,0:T(8,128)(2,1)} %get-tuple-element.18.after_ref), channel_id=1, source_target_pairs={{0,28},{1,5},{2,30},{3,7},{4,0},{5,9},{6,2},{7,11},{8,4},{9,13},{1... | collective-permute-start | bytes 552968 | tf_op jit(solution)/shard_map/ppermute | solution.py:377
  7.7 9.7 %collective-permute-start.1 = (bf16[128,256]{1,0:T(8,128)(2,1)}, bf16[128,256]{1,0:T(8,128)(2,1)S(1)}, u32[]{:S(2)}, u32[]{:S(2)}) collective-permute-start(bf16[128,256]{1,0:T(8,128)(2,1)} %get-tuple-element.19), channel_id=1, source_target_pairs={{0,24},{4,28},{8,0},{12,4},{16,8},{20,12},{24,16},{28,20},{1,25},{... | collective-permute-start | bytes 196616 | tf_op jit(solution)/shard_map/ppermute | solution.py:351
  8.2 39.2 %collective-permute-start.5 = (bf16[16,384,128]{2,1,0:T(8,128)(2,1)}, bf16[16,384,128]{2,1,0:T(8,128)(2,1)S(1)}, u32[]{:S(2)}, u32[]{:S(2)}) collective-permute-start(bf16[16,384,128]{2,1,0:T(8,128)(2,1)} %src_ref.7), channel_id=1, source_target_pairs={{0,2},{1,3},{2,0},{3,1},{4,6},{5,7},{6,4},{7,5},{8,10},{9,11},{10,... | collective-permute-start | bytes 4718600 | tf_op jit(solution)/shard_map/ppermute | solution.py:351
  11.7 4.0 %copy-start = (bf16[16,384,128]{2,1,0:T(8,128)(2,1)S(1)}, bf16[16,384,128]{2,1,0:T(8,128)(2,1)}, u32[]{:S(2)}) copy-start(bf16[16,384,128]{2,1,0:T(8,128)(2,1)} %src_ref.7) | copy-start | bytes 4718596
  11.7 20.7 %collective-permute-start.3 = (bf16[8,384,128]{2,1,0:T(8,128)(2,1)}, bf16[8,384,128]{2,1,0:T(8,128)(2,1)S(1)}, u32[]{:S(2)}, u32[]{:S(2)}) collective-permute-start(bf16[8,384,128]{2,1,0:T(8,128)(2,1)} %half_near.1.after_ref), channel_id=1, source_target_pairs={{0,28},{4,0},{8,4},{12,8},{16,12},{20,16},{24,20},{28,24},{1,29},{... | collective-permute-start | bytes 2359304 | tf_op jit(solution)/shard_map/ppermute | solution.py:351
  14.2 33.1 %collective-permute-start.4 = (bf16[8,384,128]{2,1,0:T(8,128)(2,1)}, bf16[8,384,128]{2,1,0:T(8,128)(2,1)S(1)}, u32[]{:S(2)}, u32[]{:S(2)}) collective-permute-start(bf16[8,384,128]{2,1,0:T(8,128)(2,1)} %half_late.1.after_ref), channel_id=1, source_target_pairs={{0,28},{4,0},{8,4},{12,8},{16,12},{20,16},{24,20},{28,24},{1,29},{... | collective-permute-start | bytes 2359304 | tf_op jit(solution)/shard_map/ppermute | solution.py:351
  15.7 1.2 %copy-start.1 = (bf16[8,384,128]{2,1,0:T(8,128)(2,1)S(1)}, bf16[8,384,128]{2,1,0:T(8,128)(2,1)}, u32[]{:S(2)}) copy-start(bf16[8,384,128]{2,1,0:T(8,128)(2,1)} %half_late.1.after_ref) | copy-start | bytes 2359300
  16.8 2.1 %copy-start.2 = (bf16[128,640]{1,0:T(8,128)(2,1)S(1)}, bf16[128,640]{1,0:T(8,128)(2,1)}, u32[]{:S(2)}) copy-start(bf16[128,640]{1,0:T(8,128)(2,1)} %occ_ref.3) | copy-start | bytes 491524
  16.8 2.1 %copy-start.3 = (bf16[128,384]{1,0:T(8,128)(2,1)S(1)}, bf16[128,384]{1,0:T(8,128)(2,1)}, u32[]{:S(2)}) copy-start(bf16[128,384]{1,0:T(8,128)(2,1)} %virt_ref.3) | copy-start | bytes 294916
  16.8 2.1 %copy-start.4 = (s32[1,5]{1,0:T(1,128)S(1)}, s32[1,5]{1,0:T(1,128)}, u32[]{:S(2)}) copy-start(s32[1,5]{1,0:T(1,128)} %occ_mask.3) | copy-start | bytes 64
  16.8 2.1 %copy-start.5 = (s32[1,3]{1,0:T(1,128)S(1)}, s32[1,3]{1,0:T(1,128)}, u32[]{:S(2)}) copy-start(s32[1,3]{1,0:T(1,128)} %virt_mask.3) | copy-start | bytes 40
  16.8 2.1 %copy-start.6 = (s32[1,3]{1,0:T(1,128)S(1)}, s32[1,3]{1,0:T(1,128)}, u32[]{:S(2)}) copy-start(s32[1,3]{1,0:T(1,128)} %three_mask.3) | copy-start | bytes 40
  17.4 1.5 %collective-permute-start.2 = (bf16[144,640]{1,0:T(8,128)(2,1)S(1)}, bf16[144,640]{1,0:T(8,128)(2,1)S(1)}, u32[]{:S(2)}, u32[]{:S(2)}) collective-permute-start(bf16[144,640]{1,0:T(8,128)(2,1)S(1)} %collective-permute-done.one_ref), channel_id=1, source_target_pairs={{0,1},{1,0},{2,3},{3,2},{4,5},{5,4},{6,7},{7,6},{8,9},{9,8},{10,11... | collective-permute-start | bytes 552968 | tf_op jit(solution)/shard_map/ppermute | solution.py:369
  47.4 3.4 %collective-permute-start.7 = (bf16[16,384,128]{2,1,0:T(8,128)(2,1)S(1)}, bf16[16,384,128]{2,1,0:T(8,128)(2,1)S(1)}, u32[]{:S(2)}, u32[]{:S(2)}) collective-permute-start(bf16[16,384,128]{2,1,0:T(8,128)(2,1)S(1)} %collective-permute-done.5.near_ref), channel_id=1, source_target_pairs={{0,1},{1,0},{2,3},{3,2},{4,5},{5,4},{6,7},{7,6},{8,9},{9,8},{10,11... | collective-permute-start | bytes 4718600 | tf_op jit(solution)/shard_map/ppermute | solution.py:369
  47.4 5.7 %collective-permute-start.6 = (bf16[384,16,128]{2,1,0:T(8,128)(2,1)S(1)}, bf16[384,16,128]{2,1,0:T(8,128)(2,1)S(1)}, u32[]{:S(2)}, u32[]{:S(2)}) collective-permute-start(bf16[384,16,128]{2,1,0:T(8,128)(2,1)S(1)} %relayout.1.after_ref.refs_2_), channel_id=1, source_target_pairs={{0,1},{1,0},{2,3},{3,2},{4,5},{5,4},{6,7},{7,6},{8,9},{9,8},{10,11... | collective-permute-start | bytes 4718600 | tf_op jit(solution)/shard_map/ppermute | solution.py:369

commit v3 on v2

--- a/solution.py
+++ b/solution.py
@@ -25,7 +25,7 @@
         in_specs=in_specs,
         out_specs=out_specs,
         compiler_params=pltpu.CompilerParams(vmem_limit_bytes=room * MIB),
-        cost_estimate=LARGE if name in ("relayout",) else LITTLE,
+        cost_estimate=LARGE if name in ("halo_near", "half_late") else LITTLE,
         **more,
     )
 
@@ -239,16 +239,12 @@
     m_move.wait()
     group = height // 6
 
-    def second_stage(step, carry):
-        at = pl.multiple_of(step * group, group)
-        rows = pl.ds(pl.multiple_of(at * batch, group * batch), group * batch)
+    for at in range(0, height, group):
+        rows = pl.ds(at * batch, group * batch)
         both = jnp.concatenate([m_own[rows, :], wide_m[rows, :].astype(BF16)], 1)
         x = dot_nt(both, virt_own_ref[...]).reshape(group, batch, width)
         v = dot_nn(wide_u[rows, :].astype(BF16), virt_next_ref[...]).reshape(group, batch, width)
-        out_ref[pl.ds(at, group)] = jnp.concatenate([x, v], 1).astype(BF16)
-        return carry
-
-    lax.fori_loop(0, height // group, second_stage, 0)
+        out_ref[at : at + group] = jnp.concatenate([x, v], 1).astype(BF16)
 
 
 def halo_panels(name, after, halo, m_own, green, virt_own, virt_next):
@@ -380,13 +376,6 @@
     late = half_of(1, near, three_center)
     halo_late = shifted(late, "ao", -1)
     flat = relayout(late, three_center)
-    halo_late = shifted(late, "ao", -1)
-    early, distances = [flat, partner(flat)], [0]
-    for distance in range(2, groups // 2):
-        step = shifted(flat, "ri", 2 * distance)
-        early += [step, partner(step)]
-        distances.append(distance)
-
     one_hop, two_hops, _ = lax.optimization_barrier((one_hop, two_hops, flat))
     green_own, green_halo, virt_own, virt_next = call(
         tables_kernel, "tables",
@@ -395,14 +384,21 @@
         scratch_shapes=[pltpu.VMEM((tile + 16, 5 * tile), BF16)] * 2,
     )(*masks, occ_band, virt_band, one_hop, partner(one_hop), two_hops, flat)
     m_near, m_late = own_m(green_own, three_center)
+    early, distances = [flat, partner(lax.optimization_barrier((flat, m_near))[0])], [0]
+    for distance in range(2, groups // 2):
+        step = shifted(flat, "ri", 2 * distance)
+        early += [step, partner(step)]
+        distances.append(distance)
+
     greens = (green_halo, virt_own, virt_next)
 
     halo_near, _ = lax.optimization_barrier((halo_near, m_near))
     panels_near = halo_panels("halo_near", m_late, halo_near, m_near, *greens)
-    halo_late, far, _ = lax.optimization_barrier((halo_late, far, panels_near))
+    far, _ = lax.optimization_barrier((far, m_near))
     passed = partner(far)
-    panels_late = halo_panels("halo_late", panels_near, halo_late, m_late, *greens)
-    far_all = far_rows(panels_late, far, passed)
+    far_all = far_rows(panels_near, far, passed)
+    halo_late, _ = lax.optimization_barrier((halo_late, far_all))
+    panels_late = halo_panels("halo_late", early[1], halo_late, m_late, *greens)
     parts = contract(mine, distances + [1], [panels_near, panels_late], early + [far_all], lines)
     swapped = lax.all_to_all(parts.reshape(lines * groups, *parts.shape[2:]), BOTH, 0, 0, tiled=True)
     return call(total_kernel, "total", shape(batch, groups * batch, dtype=F32), [VMEM])(swapped)

time: 69.1 us -> 65.4 us (0.946)
  Pallas kernels: 18.7 us -> 17.1 us
  blocking collectives: 12.6 us -> 11.2 us
  local copies, waits for them, and re-layouts: 1.19 us -> 0.04 us
  waiting for transfers between devices: 25.7 us -> 26.4 us
    ppermute x4, waiting for transfers between devices: 23.2 us -> 25.1 us  [shifted(): lax.ppermute(value, axis, [(i, (i + distance) % size) for i in range(size)])]
    pallas_call x2, Pallas kernels: 5.64 us -> 4.03 us  [halo_panels(): call(halo_kernel, name, shape(height, 2 * batch, width), [ANY] * 3 + [VME...]
    all_to_all x1, blocking collectives: 12.6 us -> 11.2 us  [per_device(): lax.all_to_all(parts.reshape(lines * groups, *parts.shape[2:]), BOTH, 0,...]
    unnamed x14 -> x12, local copies, waits for them, and re-layouts: 1.19 us -> 0.04 us
    ppermute x3, waiting for transfers between devices: 2.52 us -> 1.39 us  [partner(): return lax.ppermute(value, 'ri', [(i, i ^ 1) for i in range(groups)])]
  transfers between devices with their start and end apart: 8 -> 8, of which waited for: 5 -> 3; matrix products, arithmetic and copies ran while one was open for 0% -> 0% of each run, Pallas kernels for 20% -> 15%
where the time goes in v3:
time: 65.4 us; the launch traced here: 65.2 us
  waiting for transfers between devices  26.4 us (40%)
  Pallas kernels  17.1 us (26%)
  blocking collectives  11.2 us (17%)
  starting transfers between devices  10.3 us (16%)
    ppermute x4, waiting for transfers between devices, shifted(): lax.ppermute(value, axis, [(i, (i + distance) % size) for i in range(size)])  25.1 us
    all_to_all x1, blocking collectives, per_device(): lax.all_to_all(parts.reshape(lines * groups, *parts.shape[2:]), BOTH, 0,...  11.2 us
    ppermute x1, starting transfers between devices, per_device(): lax.ppermute(one, BOTH, mixed((1, 0), (-1, 0)))  5.98 us
    pallas_call x2, Pallas kernels, halo_panels(): call(halo_kernel, name, shape(height, 2 * batch, width), [ANY] * 3 + [VME...  4.03 us
    ppermute x4, starting transfers between devices, shifted(): lax.ppermute(value, axis, [(i, (i + distance) % size) for i in range(size)])  3.99 us
    pallas_call x2, Pallas kernels, half_of(): call(functools.partial(half_kernel, which), ('half_near', 'half_late')[wh...  3.91 us
    pallas_call x1, Pallas kernels, contract(): call(functools.partial(contract_kernel, len(lefts), len(rights), 16, dist...  2.56 us
    pallas_call x1, Pallas kernels, per_device(): call(pack_kernel, 'pack', [shape(tile + 16, 5 * tile), shape(tile, 2 * ti...  1.75 us
  transfers between devices with their start and end apart: 8, of which 3 were waited for; matrix products, arithmetic and copies ran while one was open for 0% of the time, Pallas kernels for 15%

profile of v3, /device:TPU:0, one launch (start us, length us, event | category | flops | bytes accessed | tf_op | source)
XLA Modules:
  0.0 65.2 jit_solution(10777870181224041127)
XLA Ops:
  0.0 1.7 %pack.1 = (bf16[144,640]{1,0:T(8,128)(2,1)}, bf16[128,256]{1,0:T(8,128)(2,1)}) custom-call(s32[1]{0:T(128)} %bitcast.mine_ref, s32[1,5]{1,0:T(1,128)} %occ_mask.3, s32[1,3]{1,0:T(1,128)} %virt_mask.3, s32[1,3]{1,0:T(1,128)} %three_mask.3, bf16[128,640]{1,0:T(8,128)(2,1)} %occ_ref.3, bf16[128,384]{1,0:T(8,128)(2,1)} %virt_ref.3), custom_call_target="tpu_custom_call" | custom-call | flops 1024 | bytes 1024 | tf_op jit(solution)/shard_map/pack/pallas_call | solution.py:369
  1.7 6.0 %collective-permute-start = (bf16[144,640]{1,0:T(8,128)(2,1)}, bf16[144,640]{1,0:T(8,128)(2,1)S(1)}, u32[]{:S(2)}, u32[]{:S(2)}) collective-permute-start(bf16[144,640]{1,0:T(8,128)(2,1)} %get-tuple-element.19.after_ref), channel_id=1, source_target_pairs={{0,28},{1,5},{2,30},{3,7},{4,0},{5,9},{6,2},{7,11},{8,4},{9,13},{1... | collective-permute-start | bytes 552968 | tf_op jit(solution)/shard_map/ppermute | solution.py:373
  7.7 0.4 collective-permute-start.1
  8.2 1.5 %collective-permute-start.6 = (bf16[16,384,128]{2,1,0:T(8,128)(2,1)}, bf16[16,384,128]{2,1,0:T(8,128)(2,1)S(1)}, u32[]{:S(2)}, u32[]{:S(2)}) collective-permute-start(bf16[16,384,128]{2,1,0:T(8,128)(2,1)} %src_ref.7), channel_id=1, source_target_pairs={{0,2},{1,3},{2,0},{3,1},{4,6},{5,7},{6,4},{7,5},{8,10},{9,11},{10,... | collective-permute-start | bytes 4718600 | tf_op jit(solution)/shard_map/ppermute | solution.py:347
  9.7 2.0 %half_near.1.after_ref = bf16[8,384,128]{2,1,0:T(8,128)(2,1)} custom-call(bf16[144,640]{1,0:T(8,128)(2,1)} %get-tuple-element.19.after_ref, bf16[16,384,128]{2,1,0:T(8,128)(2,1)} %src_ref.7), custom_call_target="tpu_custom_call" | custom-call | flops 1024 | bytes 1024 | tf_op jit(solution)/shard_map/half_near/pallas_call | solution.py:99
  11.7 0.0 copy-start
  11.7 0.6 collective-permute-start.3
  12.3 1.9 %half_late.1.after_ref = bf16[8,384,128]{2,1,0:T(8,128)(2,1)} custom-call(bf16[8,384,128]{2,1,0:T(8,128)(2,1)} %half_near.1.after_ref, bf16[16,384,128]{2,1,0:T(8,128)(2,1)} %src_ref.7), custom_call_target="tpu_custom_call" | custom-call | flops 99999997952 | bytes 1000000000 | tf_op jit(solution)/shard_map/half_late/pallas_call | solution.py:99
  14.2 0.0 copy-done
  14.2 0.0 copy-start.1
  14.2 0.0 copy-start.2
  14.3 0.0 copy-start.3
  14.3 0.0 copy-start.4
  14.3 0.0 copy-start.5
  14.3 0.6 relayout.1.after_ref.refs_2_
  14.9 0.0 collective-permute-done.1.upper2
  14.9 0.0 collective-permute-done.one_ref
  14.9 0.1 collective-permute-start.2
  15.0 1.4 %collective-permute-start.5 = (bf16[8,384,128]{2,1,0:T(8,128)(2,1)}, bf16[8,384,128]{2,1,0:T(8,128)(2,1)S(1)}, u32[]{:S(2)}, u32[]{:S(2)}) collective-permute-start(bf16[8,384,128]{2,1,0:T(8,128)(2,1)} %half_late.1.after_ref), channel_id=1, source_target_pairs={{0,28},{4,0},{8,4},{12,8},{16,12},{20,16},{24,20},{28,24},{1,29},{... | collective-permute-start | bytes 2359304 | tf_op jit(solution)/shard_map/ppermute | solution.py:347
  16.4 0.0 collective-permute-done.2.other_ref
  16.4 0.0 copy-done.1
  16.4 0.0 copy-done.2
  16.4 0.0 copy-done.3
  16.4 0.0 copy-done.4
  16.4 0.0 copy-done.5
  16.4 0.8 %tables.1 = (bf16[384,384]{1,0:T(8,128)(2,1)S(1)}, bf16[768,384]{1,0:T(8,128)(2,1)S(1)}, bf16[128,256]{1,0:T(8,128)(2,1)S(1)}, bf16[128,128]{1,0:T(8,128)(2,1)S(1)}) custom-call(s32[1]{0:T(128)} %bitcast.mine_ref, s32[1,5]{1,0:T(1,128)S(1)} %copy-done.3, s32[1,3]{1,0:T(1,128)S(1)} %copy-done.4, s32[1,3]{1,0:T(1,128)S(1)} %copy-done.5, ...), custom_call_target="tpu_custom_call" | custom-call | flops 1024 | bytes 1024 | tf_op jit(solution)/shard_map/tables/pallas_call | solution.py:380
  17.2 1.6 %own_m.1 = (bf16[3072,128]{1,0:T(8,128)(2,1)S(1)}, bf16[3072,128]{1,0:T(8,128)(2,1)S(1)}) custom-call(bf16[384,384]{1,0:T(8,128)(2,1)S(1)} %get-tuple-element.23.green_ref, bf16[16,384,128]{2,1,0:T(8,128)(2,1)S(1)} %copy-done), custom_call_target="tpu_custom_call" | custom-call | flops 1024 | bytes 1024 | tf_op jit(solution)/shard_map/own_m/pallas_call | solution.py:210
  18.8 0.2 collective-permute-start.4
  19.0 13.4 %collective-permute-done.3.halo_ref = bf16[8,384,128]{2,1,0:T(8,128)(2,1)S(1)} collective-permute-done((bf16[8,384,128]{2,1,0:T(8,128)(2,1)}, bf16[8,384,128]{2,1,0:T(8,128)(2,1)S(1)}, u32[]{:S(2)}, u32[]{:S(2)}) %collective-permute-start.3) | collective-permute-done | bytes 786464 | tf_op jit(solution)/shard_map/ppermute | solution.py:347
  32.4 11.6 %collective-permute-done.6.near_ref = bf16[16,384,128]{2,1,0:T(8,128)(2,1)S(1)} collective-permute-done((bf16[16,384,128]{2,1,0:T(8,128)(2,1)}, bf16[16,384,128]{2,1,0:T(8,128)(2,1)S(1)}, u32[]{:S(2)}, u32[]{:S(2)}) %collective-permute-start.6) | collective-permute-done | bytes 1572896 | tf_op jit(solution)/shard_map/ppermute | solution.py:347
  44.1 0.0 collective-permute-start.7
  44.1 2.0 %halo_near.1.after_ref.refs_0_ = bf16[384,16,128]{2,1,0:T(8,128)(2,1)S(1)} custom-call(bf16[3072,128]{1,0:T(8,128)(2,1)S(1)} %get-tuple-element.24.after_ref.m_ref, bf16[8,384,128]{2,1,0:T(8,128)(2,1)S(1)} %collective-permute-done.3.halo_ref, bf16[3072,128]{1,0:T(8,128)(2,1)S(1)} %get-tuple-element.25.m_ref, ...), custom_call_target="tpu_custom_call" | custom-call | flops 99999997952 | bytes 1000000000 | tf_op jit(solution)/shard_map/halo_near/pallas_call | solution.py:252
  46.1 1.4 %collective-permute-done.7.other_ref = bf16[16,384,128]{2,1,0:T(8,128)(2,1)S(1)} collective-permute-done((bf16[16,384,128]{2,1,0:T(8,128)(2,1)S(1)}, bf16[16,384,128]{2,1,0:T(8,128)(2,1)S(1)}, u32[]{:S(2)}, u32[]{:S(2)}) %collective-permute-start.7) | collective-permute-done | bytes 1572896 | tf_op jit(solution)/shard_map/ppermute | solution.py:365
  47.5 1.2 %far_rows.1.refs_4_ = bf16[384,32,128]{2,1,0:T(8,128)(2,1)S(1)} custom-call(bf16[384,16,128]{2,1,0:T(8,128)(2,1)S(1)} %halo_near.1.after_ref.refs_0_, bf16[16,384,128]{2,1,0:T(8,128)(2,1)S(1)} %collective-permute-done.6.near_ref, bf16[16,384,128]{2,1,0:T(8,128)(2,1)S(1)} %collective-permute-done.7.other_ref), custom_call_target="tpu_custom_call" | custom-call | flops 1024 | bytes 1024 | tf_op jit(solution)/shard_map/far_rows/pallas_call | solution.py:185
  48.7 0.0 collective-permute-done.5.halo_ref
  48.7 0.0 collective-permute-done.4.after_ref.refs_3_
  48.7 2.0 %halo_late.1.refs_1_ = bf16[384,16,128]{2,1,0:T(8,128)(2,1)S(1)} custom-call(bf16[384,16,128]{2,1,0:T(8,128)(2,1)S(1)} %collective-permute-done.4.after_ref.refs_3_, bf16[8,384,128]{2,1,0:T(8,128)(2,1)S(1)} %collective-permute-done.5.halo_ref, bf16[3072,128]{1,0:T(8,128)(2,1)S(1)} %get-tuple-element.24.after_ref.m_ref, ...), custom_call_target="tpu_custom_call" | custom-call | flops 1024 | bytes 1024 | tf_op jit(solution)/shard_map/halo_late/pallas_call | solution.py:252
  50.7 2.6 %contract.1 = f32[8,4,8,128]{3,2,1,0:T(8,128)S(1)} custom-call(s32[1]{0:T(128)} %bitcast.mine_ref, bf16[384,16,128]{2,1,0:T(8,128)(2,1)S(1)} %halo_near.1.after_ref.refs_0_, bf16[384,16,128]{2,1,0:T(8,128)(2,1)S(1)} %halo_late.1.refs_1_, bf16[384,16,128]{2,1,0:T(8,128)(2,1)S(1)} %relayout.1.after_ref.refs_2_, ...), custom_call_target="tpu_custom_call" | custom-call | flops 1024 | bytes 1024 | tf_op jit(solution)/shard_map/contract/pallas_call | solution.py:328
  53.3 11.2 %all_to_all.5.src_ref = f32[32,8,128]{2,1,0:T(8,128)S(1)} all-to-all(f32[32,8,128]{2,1,0:T(8,128)S(1)} %bitcast.2), channel_id=1, replica_groups=mesh['ao'=8,'ri'=4] {'ao','ri'}, dimensions={0} | all-to-all | bytes 262144 | tf_op jit(solution)/shard_map/all_to_all | solution.py:403
  64.5 0.7 %total.1 = f32[16,64]{1,0:T(8,128)} custom-call(f32[32,8,128]{2,1,0:T(8,128)S(1)} %all_to_all.5.src_ref), custom_call_target="tpu_custom_call" | custom-call | flops 1024 | bytes 1024 | tf_op jit(solution)/shard_map/total/pallas_call | solution.py:404
Async XLA Ops:
  1.7 13.1 %collective-permute-start = (bf16[144,640]{1,0:T(8,128)(2,1)}, bf16[144,640]{1,0:T(8,128)(2,1)S(1)}, u32[]{:S(2)}, u32[]{:S(2)}) collective-permute-start(bf16[144,640]{1,0:T(8,128)(2,1)} %get-tuple-element.19.after_ref), channel_id=1, source_target_pairs={{0,28},{1,5},{2,30},{3,7},{4,0},{5,9},{6,2},{7,11},{8,4},{9,13},{1... | collective-permute-start | bytes 552968 | tf_op jit(solution)/shard_map/ppermute | solution.py:373
  7.7 7.1 %collective-permute-start.1 = (bf16[128,256]{1,0:T(8,128)(2,1)}, bf16[128,256]{1,0:T(8,128)(2,1)S(1)}, u32[]{:S(2)}, u32[]{:S(2)}) collective-permute-start(bf16[128,256]{1,0:T(8,128)(2,1)} %get-tuple-element.20), channel_id=1, source_target_pairs={{0,24},{4,28},{8,0},{12,4},{16,8},{20,12},{24,16},{28,20},{1,25},{... | collective-permute-start | bytes 196616 | tf_op jit(solution)/shard_map/ppermute | solution.py:347
  8.2 35.9 %collective-permute-start.6 = (bf16[16,384,128]{2,1,0:T(8,128)(2,1)}, bf16[16,384,128]{2,1,0:T(8,128)(2,1)S(1)}, u32[]{:S(2)}, u32[]{:S(2)}) collective-permute-start(bf16[16,384,128]{2,1,0:T(8,128)(2,1)} %src_ref.7), channel_id=1, source_target_pairs={{0,2},{1,3},{2,0},{3,1},{4,6},{5,7},{6,4},{7,5},{8,10},{9,11},{10,... | collective-permute-start | bytes 4718600 | tf_op jit(solution)/shard_map/ppermute | solution.py:347
  11.7 2.6 %copy-start = (bf16[16,384,128]{2,1,0:T(8,128)(2,1)S(1)}, bf16[16,384,128]{2,1,0:T(8,128)(2,1)}, u32[]{:S(2)}) copy-start(bf16[16,384,128]{2,1,0:T(8,128)(2,1)} %src_ref.7) | copy-start | bytes 4718596
  11.7 20.7 %collective-permute-start.3 = (bf16[8,384,128]{2,1,0:T(8,128)(2,1)}, bf16[8,384,128]{2,1,0:T(8,128)(2,1)S(1)}, u32[]{:S(2)}, u32[]{:S(2)}) collective-permute-start(bf16[8,384,128]{2,1,0:T(8,128)(2,1)} %half_near.1.after_ref), channel_id=1, source_target_pairs={{0,28},{4,0},{8,4},{12,8},{16,12},{20,16},{24,20},{28,24},{1,29},{... | collective-permute-start | bytes 2359304 | tf_op jit(solution)/shard_map/ppermute | solution.py:347
  14.2 2.2 %copy-start.1 = (bf16[128,640]{1,0:T(8,128)(2,1)S(1)}, bf16[128,640]{1,0:T(8,128)(2,1)}, u32[]{:S(2)}) copy-start(bf16[128,640]{1,0:T(8,128)(2,1)} %occ_ref.3) | copy-start | bytes 491524
  14.2 2.2 %copy-start.2 = (bf16[128,384]{1,0:T(8,128)(2,1)S(1)}, bf16[128,384]{1,0:T(8,128)(2,1)}, u32[]{:S(2)}) copy-start(bf16[128,384]{1,0:T(8,128)(2,1)} %virt_ref.3) | copy-start | bytes 294916
  14.3 2.2 %copy-start.3 = (s32[1,5]{1,0:T(1,128)S(1)}, s32[1,5]{1,0:T(1,128)}, u32[]{:S(2)}) copy-start(s32[1,5]{1,0:T(1,128)} %occ_mask.3) | copy-start | bytes 64
  14.3 2.1 %copy-start.4 = (s32[1,3]{1,0:T(1,128)S(1)}, s32[1,3]{1,0:T(1,128)}, u32[]{:S(2)}) copy-start(s32[1,3]{1,0:T(1,128)} %virt_mask.3) | copy-start | bytes 40
  14.3 2.1 %copy-start.5 = (s32[1,3]{1,0:T(1,128)S(1)}, s32[1,3]{1,0:T(1,128)}, u32[]{:S(2)}) copy-start(s32[1,3]{1,0:T(1,128)} %three_mask.3) | copy-start | bytes 40
  14.9 1.5 %collective-permute-start.2 = (bf16[144,640]{1,0:T(8,128)(2,1)S(1)}, bf16[144,640]{1,0:T(8,128)(2,1)S(1)}, u32[]{:S(2)}, u32[]{:S(2)}) collective-permute-start(bf16[144,640]{1,0:T(8,128)(2,1)S(1)} %collective-permute-done.one_ref), channel_id=1, source_target_pairs={{0,1},{1,0},{2,3},{3,2},{4,5},{5,4},{6,7},{7,6},{8,9},{9,8},{10,11... | collective-permute-start | bytes 552968 | tf_op jit(solution)/shard_map/ppermute | solution.py:365
  15.0 33.7 %collective-permute-start.5 = (bf16[8,384,128]{2,1,0:T(8,128)(2,1)}, bf16[8,384,128]{2,1,0:T(8,128)(2,1)S(1)}, u32[]{:S(2)}, u32[]{:S(2)}) collective-permute-start(bf16[8,384,128]{2,1,0:T(8,128)(2,1)} %half_late.1.after_ref), channel_id=1, source_target_pairs={{0,28},{4,0},{8,4},{12,8},{16,12},{20,16},{24,20},{28,24},{1,29},{... | collective-permute-start | bytes 2359304 | tf_op jit(solution)/shard_map/ppermute | solution.py:347
  18.8 29.9 %collective-permute-start.4 = (bf16[384,16,128]{2,1,0:T(8,128)(2,1)S(1)}, bf16[384,16,128]{2,1,0:T(8,128)(2,1)S(1)}, u32[]{:S(2)}, u32[]{:S(2)}) collective-permute-start(bf16[384,16,128]{2,1,0:T(8,128)(2,1)S(1)} %relayout.1.after_ref.refs_2_), channel_id=1, source_target_pairs={{0,1},{1,0},{2,3},{3,2},{4,5},{5,4},{6,7},{7,6},{8,9},{9,8},{10,11... | collective-permute-start | bytes 4718600 | tf_op jit(solution)/shard_map/ppermute | solution.py:365
  44.1 3.4 %collective-permute-start.7 = (bf16[16,384,128]{2,1,0:T(8,128)(2,1)S(1)}, bf16[16,384,128]{2,1,0:T(8,128)(2,1)S(1)}, u32[]{:S(2)}, u32[]{:S(2)}) collective-permute-start(bf16[16,384,128]{2,1,0:T(8,128)(2,1)S(1)} %collective-permute-done.6.near_ref), channel_id=1, source_target_pairs={{0,1},{1,0},{2,3},{3,2},{4,5},{5,4},{6,7},{7,6},{8,9},{9,8},{10,11... | collective-permute-start | bytes 4718600 | tf_op jit(solution)/shard_map/ppermute | solution.py:365

commit v4 on v3

--- a/solution.py
+++ b/solution.py
@@ -220,15 +220,9 @@
 
 
 def halo_kernel(
-    after_ref, halo_ref, m_ref, green_ref, virt_own_ref, virt_next_ref, out_ref,
-    held, m_own, wide_m, wide_u, sems,
+    after_ref, held, m_own, green_ref, virt_own_ref, virt_next_ref, out_ref, wide_m, wide_u
 ):
     batch, height, width = held.shape
-    halo_move = pltpu.make_async_copy(halo_ref, held, sems.at[0])
-    halo_move.start()
-    m_move = pltpu.make_async_copy(m_ref, m_own, sems.at[1])
-    m_move.start()
-    halo_move.wait()
     for p in range(0, batch, 2):
         pair = jnp.concatenate([held[p], held[p + 1]], 1)
         both = dot_nn(green_ref[...], pair)
@@ -236,7 +230,6 @@
         wide_m[pl.ds(p + 1, height, batch), :] = both[:height, width:]
         wide_u[pl.ds(p, height, batch), :] = both[height:, :width]
         wide_u[pl.ds(p + 1, height, batch), :] = both[height:, width:]
-    m_move.wait()
     group = height // 6
 
     for at in range(0, height, group):
@@ -251,13 +244,10 @@
     batch, height, width = halo.shape
     return call(
         halo_kernel, name, shape(height, 2 * batch, width),
-        [ANY] * 3 + [VMEM] * 3,
+        [ANY] + [VMEM] * 5,
         scratch_shapes=[
-            pltpu.VMEM((batch, height, width), BF16),
-            pltpu.VMEM((height * batch, width), BF16),
             pltpu.VMEM((height * batch, width), F32),
             pltpu.VMEM((height * batch, width), F32),
-            pltpu.SemaphoreType.DMA((2,)),
         ],
     )(after, halo, m_own, green, virt_own, virt_next)
 
@@ -265,12 +255,6 @@
 def contract_kernel(lefts, rights, group, distances, mine_ref, *refs):
     out_ref, total_ref = refs[-2:]
     left, right = refs[:lefts], refs[lefts : lefts + rights]
-    step, steps = pl.program_id(0), pl.num_programs(0)
-
-    @pl.when(step == 0)
-    def _():
-        total_ref[...] = jnp.zeros_like(total_ref)
-
     total = None
     for at in range(0, left[0].shape[0], group):
         sides = [
@@ -281,56 +265,51 @@
         ]
         part = dot_nt(*sides)
         total = part if total is None else total + part
-    total_ref[...] += total
-
-    @pl.when(step == steps - 1)
-    def _():
-        lines, chunks, deep, wide = out_ref.shape
-        rows, cols = total_ref.shape
-        batch = rows // 2
-        half = batch // 2
-        exact = dict(precision=lax.Precision.HIGHEST)
-        source = lax.broadcasted_iota(jnp.int32, (cols, cols), 0)
-        target = lax.broadcasted_iota(jnp.int32, (cols, cols), 1)
-        block, within = source // batch, source % batch
-        place = jnp.zeros((cols, cols), jnp.int32)
-        groups, mine = cols // batch, mine_ref[0]
-        for k, distance in enumerate(distances):
-            for j, device in enumerate((mine, mine + 1 - 2 * lax.rem(mine, 2))):
-                start = lax.rem(device - 2 * distance + groups, groups) * batch
-                place = jnp.where(block == 2 * k + j, start + within, place)
-        spread = jnp.where(place == target, 1.0, 0.0).astype(F32)
-        placed = dot_nn(total_ref[...], spread, **exact)
-
-        row = lax.broadcasted_iota(jnp.int32, (cols, rows), 0) - mine * batch
-        have = lax.broadcasted_iota(jnp.int32, (cols, rows), 1)
-        chunk, part, index = have // batch, have % batch // half, have % half
-        at = (row == chunk * half + index) & (row >= 0) & (row < batch)
-        pick_x = jnp.where(at & (part == 0), 1.0, 0.0).astype(F32)
-        pick_v = jnp.where(at & (part == 1), 1.0, 0.0).astype(F32)
-        result = dot_nn(pick_x, placed, **exact) + dot_nn(pick_v, placed, **exact).T
-        fold = batch // deep
-        for k in range(chunks):
-            piece = jnp.concatenate(
-                [result[k * batch + j * deep : k * batch + (j + 1) * deep] for j in range(fold)], 1
-            )
-            for line in range(lines):
-                out_ref[line, k] = piece
-
-
-def contract(mine, distances, lefts, rights, lines, steps=3):
+    total_ref[...] = total
+
+    lines, chunks, deep, wide = out_ref.shape
+    rows, cols = total_ref.shape
+    batch = rows // 2
+    half = batch // 2
+    exact = dict(precision=lax.Precision.HIGHEST)
+    source = lax.broadcasted_iota(jnp.int32, (cols, cols), 0)
+    target = lax.broadcasted_iota(jnp.int32, (cols, cols), 1)
+    block, within = source // batch, source % batch
+    place = jnp.zeros((cols, cols), jnp.int32)
+    groups, mine = cols // batch, mine_ref[0]
+    for k, distance in enumerate(distances):
+        for j, device in enumerate((mine, mine + 1 - 2 * lax.rem(mine, 2))):
+            start = lax.rem(device - 2 * distance + groups, groups) * batch
+            place = jnp.where(block == 2 * k + j, start + within, place)
+    spread = jnp.where(place == target, 1.0, 0.0).astype(F32)
+    placed = dot_nn(total_ref[...], spread, **exact)
+
+    row = lax.broadcasted_iota(jnp.int32, (cols, rows), 0) - mine * batch
+    have = lax.broadcasted_iota(jnp.int32, (cols, rows), 1)
+    chunk, part, index = have // batch, have % batch // half, have % half
+    at = (row == chunk * half + index) & (row >= 0) & (row < batch)
+    pick_x = jnp.where(at & (part == 0), 1.0, 0.0).astype(F32)
+    pick_v = jnp.where(at & (part == 1), 1.0, 0.0).astype(F32)
+    result = dot_nn(pick_x, placed, **exact) + dot_nn(pick_v, placed, **exact).T
+    fold = batch // deep
+    for k in range(chunks):
+        piece = jnp.concatenate(
+            [result[k * batch + j * deep : k * batch + (j + 1) * deep] for j in range(fold)], 1
+        )
+        for line in range(lines):
+            out_ref[line, k] = piece
+
+
+def contract(mine, distances, lefts, rights, lines):
     height, _, width = lefts[0].shape
-    part = height // steps
     rows, cols = [sum(a.shape[1] for a in side) for side in (lefts, rights)]
     batch = rows // 2
     fold = max(1, width // cols)
     dims = (lines, cols // batch, batch // fold, cols * fold)
+    room = 12 + (rows + cols) * height * width * 2 // MIB
     return call(
         functools.partial(contract_kernel, len(lefts), len(rights), 16, distances), "contract",
-        shape(*dims, dtype=F32),
-        [SMEM] + [pl.BlockSpec((part, a.shape[1], width), lambda i: (i, 0, 0)) for a in lefts + rights],
-        pl.BlockSpec(dims, lambda i: (0, 0, 0, 0)),
-        grid=(steps,),
+        shape(*dims, dtype=F32), [SMEM] + [VMEM] * (len(lefts) + len(rights)), room=room,
         scratch_shapes=[pltpu.VMEM((rows, cols), F32)],
     )(mine, *lefts, *rights)
 
@@ -371,7 +350,7 @@
         [SMEM] * 4 + [VMEM] * 2, [VMEM] * 2, room=56,
     )(*masks, occ_band, virt_band)
     one_hop, two_hops = lax.ppermute(one, BOTH, mixed((1, 0), (-1, 0))), shifted(two, "ao", -2)
-    near = half_of(0, one, three_center)
+    near = lax.optimization_barrier((three_center, one))[0][:half]
     halo_near = shifted(near, "ao", -1)
     late = half_of(1, near, three_center)
     halo_late = shifted(late, "ao", -1)

time: 65.4 us -> 64.9 us (level)
  Pallas kernels: 17.1 us -> 14.2 us
  local copies, waits for them, and re-layouts: 0.04 us -> 1.56 us
    pallas_call x2 -> x1, Pallas kernels: 3.91 us -> 1.93 us  [half_of(): call(functools.partial(half_kernel, which), ('half_near', 'half_late')[wh...]
    slice x0 -> x1, local copies, waits for them, and re-layouts: none -> 1.22 us  [per_device(): near = lax.optimization_barrier((three_center, one))[0][:half]]
  transfers between devices with their start and end apart: 8 -> 8, of which waited for: 3 -> 3; matrix products, arithmetic and copies ran while one was open for 0% -> 2% of each run, Pallas kernels for 15% -> 12%
where the time goes in v4:
time: 64.9 us; the launch traced here: 64.7 us
  waiting for transfers between devices  26.9 us (41%)
  Pallas kernels  14.2 us (22%)
  blocking collectives  11.2 us (17%)
  starting transfers between devices  10.6 us (16%)
  local copies, waits for them, and re-layouts  1.56 us (2%)
    ppermute x4, waiting for transfers between devices, shifted(): lax.ppermute(value, axis, [(i, (i + distance) % size) for i in range(size)])  25.3 us
    all_to_all x1, blocking collectives, per_device(): lax.all_to_all(parts.reshape(lines * groups, *parts.shape[2:]), BOTH, 0,...  11.2 us
    ppermute x1, starting transfers between devices, per_device(): lax.ppermute(one, BOTH, mixed((1, 0), (-1, 0)))  5.98 us
    ppermute x4, starting transfers between devices, shifted(): lax.ppermute(value, axis, [(i, (i + distance) % size) for i in range(size)])  4.22 us
    pallas_call x2, Pallas kernels, halo_panels(): call(halo_kernel, name, shape(height, 2 * batch, width), [ANY] + [VMEM] *...  3.52 us
    pallas_call x1, Pallas kernels, contract(): call(functools.partial(contract_kernel, len(lefts), len(rights), 16, dist...  2.29 us
    pallas_call x1, Pallas kernels, half_of(): call(functools.partial(half_kernel, which), ('half_near', 'half_late')[wh...  1.93 us
    pallas_call x1, Pallas kernels, per_device(): call(pack_kernel, 'pack', [shape(tile + 16, 5 * tile), shape(tile, 2 * ti...  1.76 us
  transfers between devices with their start and end apart: 8, of which 3 were waited for; matrix products, arithmetic and copies ran while one was open for 2% of the time, Pallas kernels for 12%

profile of v4, /device:TPU:0, one launch (start us, length us, event | category | flops | bytes accessed | tf_op | source)
XLA Modules:
  0.0 64.7 jit_solution(11203108038353701641)
XLA Ops:
  0.0 1.8 %pack.1 = (bf16[144,640]{1,0:T(8,128)(2,1)}, bf16[128,256]{1,0:T(8,128)(2,1)}) custom-call(s32[1]{0:T(128)} %bitcast.mine_ref, s32[1,5]{1,0:T(1,128)} %occ_mask.3, s32[1,3]{1,0:T(1,128)} %virt_mask.3, s32[1,3]{1,0:T(1,128)} %three_mask.3, bf16[128,640]{1,0:T(8,128)(2,1)} %occ_ref.3, bf16[128,384]{1,0:T(8,128)(2,1)} %virt_ref.3), custom_call_target="tpu_custom_call" | custom-call | flops 1024 | bytes 1024 | tf_op jit(solution)/shard_map/pack/pallas_call | solution.py:348
  1.8 6.0 %collective-permute-start = (bf16[144,640]{1,0:T(8,128)(2,1)}, bf16[144,640]{1,0:T(8,128)(2,1)S(1)}, u32[]{:S(2)}, u32[]{:S(2)}) collective-permute-start(bf16[144,640]{1,0:T(8,128)(2,1)} %get-tuple-element.20), channel_id=1, source_target_pairs={{0,28},{1,5},{2,30},{3,7},{4,0},{5,9},{6,2},{7,11},{8,4},{9,13},{1... | collective-permute-start | bytes 552968 | tf_op jit(solution)/shard_map/ppermute | solution.py:352
  7.7 0.4 collective-permute-start.1
  8.2 1.5 %collective-permute-start.6 = (bf16[16,384,128]{2,1,0:T(8,128)(2,1)}, bf16[16,384,128]{2,1,0:T(8,128)(2,1)S(1)}, u32[]{:S(2)}, u32[]{:S(2)}) collective-permute-start(bf16[16,384,128]{2,1,0:T(8,128)(2,1)} %src_ref.5), channel_id=1, source_target_pairs={{0,2},{1,3},{2,0},{3,1},{4,6},{5,7},{6,4},{7,5},{8,10},{9,11},{10,... | collective-permute-start | bytes 4718600 | tf_op jit(solution)/shard_map/ppermute | solution.py:326
  9.7 1.2 %slice.3.after_ref = bf16[8,384,128]{2,1,0:T(8,128)(2,1)S(1)} slice(bf16[16,384,128]{2,1,0:T(8,128)(2,1)} %src_ref.5), slice={[0:8], [0:384], [0:128]} | slice | bytes 1572864 | tf_op jit(solution)/shard_map/slice | solution.py:353
  10.9 0.0 copy-start.6
  10.9 0.0 copy-start
  11.0 0.6 collective-permute-start.3
  11.5 0.3 copy-done.6
  11.8 1.9 %half_late.1.after_ref = bf16[8,384,128]{2,1,0:T(8,128)(2,1)} custom-call(bf16[8,384,128]{2,1,0:T(8,128)(2,1)} %copy-done.6, bf16[16,384,128]{2,1,0:T(8,128)(2,1)} %src_ref.5), custom_call_target="tpu_custom_call" | custom-call | flops 99999997952 | bytes 1000000000 | tf_op jit(solution)/shard_map/half_late/pallas_call | solution.py:99
  13.8 0.0 copy-done
  13.8 0.0 copy-start.1
  13.8 0.0 copy-start.2
  13.8 0.0 copy-start.3
  13.8 0.0 copy-start.4
  13.8 0.0 copy-start.5
  13.9 0.6 relayout.1.after_ref.refs_2_
  14.4 0.0 collective-permute-done.1.upper2
  14.4 0.0 collective-permute-done.one_ref
  14.4 0.1 collective-permute-start.2
  14.5 1.7 %collective-permute-start.5 = (bf16[8,384,128]{2,1,0:T(8,128)(2,1)}, bf16[8,384,128]{2,1,0:T(8,128)(2,1)S(1)}, u32[]{:S(2)}, u32[]{:S(2)}) collective-permute-start(bf16[8,384,128]{2,1,0:T(8,128)(2,1)} %half_late.1.after_ref), channel_id=1, source_target_pairs={{0,28},{4,0},{8,4},{12,8},{16,12},{20,16},{24,20},{28,24},{1,29},{... | collective-permute-start | bytes 2359304 | tf_op jit(solution)/shard_map/ppermute | solution.py:326
  16.2 0.0 collective-permute-done.2.other_ref
  16.2 0.0 copy-done.1
  16.2 0.0 copy-done.2
  16.2 0.0 copy-done.3
  16.2 0.0 copy-done.4
  16.2 0.0 copy-done.5
  16.2 0.8 %tables.1 = (bf16[384,384]{1,0:T(8,128)(2,1)S(1)}, bf16[768,384]{1,0:T(8,128)(2,1)S(1)}, bf16[128,256]{1,0:T(8,128)(2,1)S(1)}, bf16[128,128]{1,0:T(8,128)(2,1)S(1)}) custom-call(s32[1]{0:T(128)} %bitcast.mine_ref, s32[1,5]{1,0:T(1,128)S(1)} %copy-done.3, s32[1,3]{1,0:T(1,128)S(1)} %copy-done.4, s32[1,3]{1,0:T(1,128)S(1)} %copy-done.5, ...), custom_call_target="tpu_custom_call" | custom-call | flops 1024 | bytes 1024 | tf_op jit(solution)/shard_map/tables/pallas_call | solution.py:359
  17.0 1.5 %own_m.1 = (bf16[3072,128]{1,0:T(8,128)(2,1)S(1)}, bf16[3072,128]{1,0:T(8,128)(2,1)S(1)}) custom-call(bf16[384,384]{1,0:T(8,128)(2,1)S(1)} %get-tuple-element.25.green_ref, bf16[16,384,128]{2,1,0:T(8,128)(2,1)S(1)} %copy-done), custom_call_target="tpu_custom_call" | custom-call | flops 1024 | bytes 1024 | tf_op jit(solution)/shard_map/own_m/pallas_call | solution.py:210
  18.5 0.3 collective-permute-start.4
  18.8 12.7 %collective-permute-done.3.held = bf16[8,384,128]{2,1,0:T(8,128)(2,1)S(1)} collective-permute-done((bf16[8,384,128]{2,1,0:T(8,128)(2,1)S(1)}, bf16[8,384,128]{2,1,0:T(8,128)(2,1)S(1)}, u32[]{:S(2)}, u32[]{:S(2)}) %collective-permute-start.3) | collective-permute-done | bytes 786464 | tf_op jit(solution)/shard_map/ppermute | solution.py:326
  31.5 12.6 %collective-permute-done.6.near_ref = bf16[16,384,128]{2,1,0:T(8,128)(2,1)S(1)} collective-permute-done((bf16[16,384,128]{2,1,0:T(8,128)(2,1)}, bf16[16,384,128]{2,1,0:T(8,128)(2,1)S(1)}, u32[]{:S(2)}, u32[]{:S(2)}) %collective-permute-start.6) | collective-permute-done | bytes 1572896 | tf_op jit(solution)/shard_map/ppermute | solution.py:326
  44.1 0.0 collective-permute-start.7
  44.1 1.8 %halo_near.1.after_ref.refs_0_ = bf16[384,16,128]{2,1,0:T(8,128)(2,1)S(1)} custom-call(bf16[3072,128]{1,0:T(8,128)(2,1)S(1)} %get-tuple-element.26.after_ref.m_own, bf16[8,384,128]{2,1,0:T(8,128)(2,1)S(1)} %collective-permute-done.3.held, bf16[3072,128]{1,0:T(8,128)(2,1)S(1)} %get-tuple-element.27.m_own, bf16[768,384]{1,0:T(8,128)(2,1)S(1)} %get-tuple-element.29.green_ref, ...), custom_call_target="tpu_custom_call" | custom-call | flops 99999997952 | bytes 1000000000 | tf_op jit(solution)/shard_map/halo_near/pallas_call | solution.py:245
  45.8 1.6 %collective-permute-done.7.other_ref = bf16[16,384,128]{2,1,0:T(8,128)(2,1)S(1)} collective-permute-done((bf16[16,384,128]{2,1,0:T(8,128)(2,1)S(1)}, bf16[16,384,128]{2,1,0:T(8,128)(2,1)S(1)}, u32[]{:S(2)}, u32[]{:S(2)}) %collective-permute-start.7) | collective-permute-done | bytes 1572896 | tf_op jit(solution)/shard_map/ppermute | solution.py:344
  47.5 1.2 %far_rows.1.refs_4_ = bf16[384,32,128]{2,1,0:T(8,128)(2,1)S(1)} custom-call(bf16[384,16,128]{2,1,0:T(8,128)(2,1)S(1)} %halo_near.1.after_ref.refs_0_, bf16[16,384,128]{2,1,0:T(8,128)(2,1)S(1)} %collective-permute-done.6.near_ref, bf16[16,384,128]{2,1,0:T(8,128)(2,1)S(1)} %collective-permute-done.7.other_ref), custom_call_target="tpu_custom_call" | custom-call | flops 1024 | bytes 1024 | tf_op jit(solution)/shard_map/far_rows/pallas_call | solution.py:185
  48.7 0.0 collective-permute-done.5.held
  48.7 0.0 collective-permute-done.4.after_ref.refs_3_
  48.7 1.8 %halo_late.1.refs_1_ = bf16[384,16,128]{2,1,0:T(8,128)(2,1)S(1)} custom-call(bf16[384,16,128]{2,1,0:T(8,128)(2,1)S(1)} %collective-permute-done.4.after_ref.refs_3_, bf16[8,384,128]{2,1,0:T(8,128)(2,1)S(1)} %collective-permute-done.5.held, bf16[3072,128]{1,0:T(8,128)(2,1)S(1)} %get-tuple-element.26.after_ref.m_own, ...), custom_call_target="tpu_custom_call" | custom-call | flops 1024 | bytes 1024 | tf_op jit(solution)/shard_map/halo_late/pallas_call | solution.py:245
  50.5 2.3 %contract.1 = f32[8,4,8,128]{3,2,1,0:T(8,128)S(1)} custom-call(s32[1]{0:T(128)} %bitcast.mine_ref, bf16[384,16,128]{2,1,0:T(8,128)(2,1)S(1)} %halo_near.1.after_ref.refs_0_, bf16[384,16,128]{2,1,0:T(8,128)(2,1)S(1)} %halo_late.1.refs_1_, bf16[384,16,128]{2,1,0:T(8,128)(2,1)S(1)} %relayout.1.after_ref.refs_2_, ...), custom_call_target="tpu_custom_call" | custom-call | flops 1024 | bytes 1024 | tf_op jit(solution)/shard_map/contract/pallas_call | solution.py:310
  52.8 11.2 %all_to_all.5.src_ref = f32[32,8,128]{2,1,0:T(8,128)S(1)} all-to-all(f32[32,8,128]{2,1,0:T(8,128)S(1)} %bitcast.2), channel_id=1, replica_groups=mesh['ao'=8,'ri'=4] {'ao','ri'}, dimensions={0} | all-to-all | bytes 262144 | tf_op jit(solution)/shard_map/all_to_all | solution.py:382
  64.0 0.7 %total.1 = f32[16,64]{1,0:T(8,128)} custom-call(f32[32,8,128]{2,1,0:T(8,128)S(1)} %all_to_all.5.src_ref), custom_call_target="tpu_custom_call" | custom-call | flops 1024 | bytes 1024 | tf_op jit(solution)/shard_map/total/pallas_call | solution.py:383
Async XLA Ops:
  1.8 12.7 %collective-permute-start = (bf16[144,640]{1,0:T(8,128)(2,1)}, bf16[144,640]{1,0:T(8,128)(2,1)S(1)}, u32[]{:S(2)}, u32[]{:S(2)}) collective-permute-start(bf16[144,640]{1,0:T(8,128)(2,1)} %get-tuple-element.20), channel_id=1, source_target_pairs={{0,28},{1,5},{2,30},{3,7},{4,0},{5,9},{6,2},{7,11},{8,4},{9,13},{1... | collective-permute-start | bytes 552968 | tf_op jit(solution)/shard_map/ppermute | solution.py:352
  7.7 6.7 %collective-permute-start.1 = (bf16[128,256]{1,0:T(8,128)(2,1)}, bf16[128,256]{1,0:T(8,128)(2,1)S(1)}, u32[]{:S(2)}, u32[]{:S(2)}) collective-permute-start(bf16[128,256]{1,0:T(8,128)(2,1)} %get-tuple-element.21), channel_id=1, source_target_pairs={{0,24},{4,28},{8,0},{12,4},{16,8},{20,12},{24,16},{28,20},{1,25},{... | collective-permute-start | bytes 196616 | tf_op jit(solution)/shard_map/ppermute | solution.py:326
  8.2 35.9 %collective-permute-start.6 = (bf16[16,384,128]{2,1,0:T(8,128)(2,1)}, bf16[16,384,128]{2,1,0:T(8,128)(2,1)S(1)}, u32[]{:S(2)}, u32[]{:S(2)}) collective-permute-start(bf16[16,384,128]{2,1,0:T(8,128)(2,1)} %src_ref.5), channel_id=1, source_target_pairs={{0,2},{1,3},{2,0},{3,1},{4,6},{5,7},{6,4},{7,5},{8,10},{9,11},{10,... | collective-permute-start | bytes 4718600 | tf_op jit(solution)/shard_map/ppermute | solution.py:326
  10.9 0.9 %copy-start.6 = (bf16[8,384,128]{2,1,0:T(8,128)(2,1)}, bf16[8,384,128]{2,1,0:T(8,128)(2,1)S(1)}, u32[]{:S(2)}) copy-start(bf16[8,384,128]{2,1,0:T(8,128)(2,1)S(1)} %slice.3.after_ref) | copy-start | bytes 2359300
  10.9 2.8 %copy-start = (bf16[16,384,128]{2,1,0:T(8,128)(2,1)S(1)}, bf16[16,384,128]{2,1,0:T(8,128)(2,1)}, u32[]{:S(2)}) copy-start(bf16[16,384,128]{2,1,0:T(8,128)(2,1)} %src_ref.5) | copy-start | bytes 4718596
  11.0 20.5 %collective-permute-start.3 = (bf16[8,384,128]{2,1,0:T(8,128)(2,1)S(1)}, bf16[8,384,128]{2,1,0:T(8,128)(2,1)S(1)}, u32[]{:S(2)}, u32[]{:S(2)}) collective-permute-start(bf16[8,384,128]{2,1,0:T(8,128)(2,1)S(1)} %slice.3.after_ref), channel_id=1, source_target_pairs={{0,28},{4,0},{8,4},{12,8},{16,12},{20,16},{24,20},{28,24},{1,29},{... | collective-permute-start | bytes 2359304 | tf_op jit(solution)/shard_map/ppermute | solution.py:326
  13.8 2.4 %copy-start.1 = (bf16[128,640]{1,0:T(8,128)(2,1)S(1)}, bf16[128,640]{1,0:T(8,128)(2,1)}, u32[]{:S(2)}) copy-start(bf16[128,640]{1,0:T(8,128)(2,1)} %occ_ref.3) | copy-start | bytes 491524
  13.8 2.4 %copy-start.2 = (bf16[128,384]{1,0:T(8,128)(2,1)S(1)}, bf16[128,384]{1,0:T(8,128)(2,1)}, u32[]{:S(2)}) copy-start(bf16[128,384]{1,0:T(8,128)(2,1)} %virt_ref.3) | copy-start | bytes 294916
  13.8 2.4 %copy-start.3 = (s32[1,5]{1,0:T(1,128)S(1)}, s32[1,5]{1,0:T(1,128)}, u32[]{:S(2)}) copy-start(s32[1,5]{1,0:T(1,128)} %occ_mask.3) | copy-start | bytes 64
  13.8 2.4 %copy-start.4 = (s32[1,3]{1,0:T(1,128)S(1)}, s32[1,3]{1,0:T(1,128)}, u32[]{:S(2)}) copy-start(s32[1,3]{1,0:T(1,128)} %virt_mask.3) | copy-start | bytes 40
  13.8 2.4 %copy-start.5 = (s32[1,3]{1,0:T(1,128)S(1)}, s32[1,3]{1,0:T(1,128)}, u32[]{:S(2)}) copy-start(s32[1,3]{1,0:T(1,128)} %three_mask.3) | copy-start | bytes 40
  14.4 1.7 %collective-permute-start.2 = (bf16[144,640]{1,0:T(8,128)(2,1)S(1)}, bf16[144,640]{1,0:T(8,128)(2,1)S(1)}, u32[]{:S(2)}, u32[]{:S(2)}) collective-permute-start(bf16[144,640]{1,0:T(8,128)(2,1)S(1)} %collective-permute-done.one_ref), channel_id=1, source_target_pairs={{0,1},{1,0},{2,3},{3,2},{4,5},{5,4},{6,7},{7,6},{8,9},{9,8},{10,11... | collective-permute-start | bytes 552968 | tf_op jit(solution)/shard_map/ppermute | solution.py:344
  14.5 34.2 %collective-permute-start.5 = (bf16[8,384,128]{2,1,0:T(8,128)(2,1)}, bf16[8,384,128]{2,1,0:T(8,128)(2,1)S(1)}, u32[]{:S(2)}, u32[]{:S(2)}) collective-permute-start(bf16[8,384,128]{2,1,0:T(8,128)(2,1)} %half_late.1.after_ref), channel_id=1, source_target_pairs={{0,28},{4,0},{8,4},{12,8},{16,12},{20,16},{24,20},{28,24},{1,29},{... | collective-permute-start | bytes 2359304 | tf_op jit(solution)/shard_map/ppermute | solution.py:326
  18.5 30.2 %collective-permute-start.4 = (bf16[384,16,128]{2,1,0:T(8,128)(2,1)S(1)}, bf16[384,16,128]{2,1,0:T(8,128)(2,1)S(1)}, u32[]{:S(2)}, u32[]{:S(2)}) collective-permute-start(bf16[384,16,128]{2,1,0:T(8,128)(2,1)S(1)} %relayout.1.after_ref.refs_2_), channel_id=1, source_target_pairs={{0,1},{1,0},{2,3},{3,2},{4,5},{5,4},{6,7},{7,6},{8,9},{9,8},{10,11... | collective-permute-start | bytes 4718600 | tf_op jit(solution)/shard_map/ppermute | solution.py:344
  44.1 3.4 %collective-permute-start.7 = (bf16[16,384,128]{2,1,0:T(8,128)(2,1)S(1)}, bf16[16,384,128]{2,1,0:T(8,128)(2,1)S(1)}, u32[]{:S(2)}, u32[]{:S(2)}) collective-permute-start(bf16[16,384,128]{2,1,0:T(8,128)(2,1)S(1)} %collective-permute-done.6.near_ref), channel_id=1, source_target_pairs={{0,1},{1,0},{2,3},{3,2},{4,5},{5,4},{6,7},{7,6},{8,9},{9,8},{10,11... | collective-permute-start | bytes 4718600 | tf_op jit(solution)/shard_map/ppermute | solution.py:344

commit v5 on v4

--- a/solution.py
+++ b/solution.py
@@ -13,7 +13,7 @@
 VMEM = pl.BlockSpec(memory_space=pltpu.VMEM)
 SMEM = pl.BlockSpec(memory_space=pltpu.SMEM)
 BOTH = ("ao", "ri")
-LARGE = pl.CostEstimate(flops=10**11, bytes_accessed=10**9, transcendentals=0)
+LENGTHS = {"halo_near": 10**11, "relayout": 10**10, "pack": 10**11}
 LITTLE = pl.CostEstimate(flops=1024, bytes_accessed=1024, transcendentals=0)
 
 
@@ -25,7 +25,7 @@
         in_specs=in_specs,
         out_specs=out_specs,
         compiler_params=pltpu.CompilerParams(vmem_limit_bytes=room * MIB),
-        cost_estimate=LARGE if name in ("halo_near", "half_late") else LITTLE,
+        cost_estimate=pl.CostEstimate(flops=LENGTHS.get(name, 1024), bytes_accessed=1024, transcendentals=0),
         **more,
     )
 
@@ -47,7 +47,7 @@
     pl.when(core != 0)(odd)
 
 
-def pack_kernel(mine_ref, occ_mask, virt_mask, three_mask, occ_ref, virt_ref, one_ref, two_ref):
+def pack_kernel(mine_ref, occ_mask, virt_mask, occ_ref, virt_ref, one_ref, two_ref):
     tile = occ_ref.shape[0]
 
     def cols(k):
@@ -57,49 +57,17 @@
 
     def even():
         for k in range(4):
-            one_ref[:tile, cols(k)] = occ[k]
-        one_ref[:tile, cols(4)] = virt_ref[:, :tile] * virt_mask[0, 0].astype(BF16)
+            one_ref[:, cols(k)] = occ[k]
+        one_ref[:, cols(4)] = virt_ref[:, :tile] * virt_mask[0, 0].astype(BF16)
 
     def odd():
         for k in range(3):
-            one_ref[:tile, cols(k)] = occ[k + 2]
-        one_ref[:tile, 3 * tile :] = jnp.zeros((tile, 2 * tile), BF16)
+            one_ref[:, cols(k)] = occ[k + 2]
+        one_ref[:, 3 * tile :] = jnp.zeros((tile, 2 * tile), BF16)
 
     when_core(lax.rem(mine_ref[0], 2), even, odd)
-    one_ref[tile:, :] = jnp.zeros((16, 5 * tile), BF16)
-    for k in range(3):
-        flag = jnp.full((16, tile), three_mask[0, k].astype(F32), F32)
-        one_ref[tile:, cols(k)] = flag.astype(BF16)
     for k in range(2):
         two_ref[:, cols(k)] = occ[k]
-
-
-def half_kernel(which, after_ref, src_ref, out_ref, held, sems):
-    half = out_ref.shape[0]
-    quarter = half // 2
-    moves = []
-    for k in range(2):
-        rows = slice(k * quarter, (k + 1) * quarter)
-        source = src_ref.at[which * half + k * quarter : which * half + (k + 1) * quarter]
-        moves.append((
-            pltpu.make_async_copy(source, held.at[rows], sems.at[k]),
-            pltpu.make_async_copy(held.at[rows], out_ref.at[rows], sems.at[2 + k]),
-        ))
-    for load, _ in moves:
-        load.start()
-    for load, store in moves:
-        load.wait()
-        store.start()
-    for _, store in moves:
-        store.wait()
-
-
-def half_of(which, after, src):
-    dims = (src.shape[0] // 2, *src.shape[1:])
-    return call(
-        functools.partial(half_kernel, which), ("half_near", "half_late")[which], shape(*dims), [ANY] * 2, ANY, room=56,
-        scratch_shapes=[pltpu.VMEM(dims, BF16), pltpu.SemaphoreType.DMA((4,))],
-    )(after, src)
 
 
 def tables_kernel(
@@ -132,7 +100,6 @@
 
     blank = jnp.zeros((tile, tile), BF16)
     own = [three_mask[0, k].astype(BF16) for k in range(3)]
-    after = [upper[tile : tile + 1, cols(k)] for k in range(3)]
     for lam in range(-1, 2):
         for mu in range(-1, 3):
             block = entry(mu, lam)
@@ -141,11 +108,11 @@
             if mu < 2:
                 own_ref[cols(lam + 1), cols(mu + 1)] = block * own[mu + 1]
             if mu > -1:
-                halo_ref[cols(lam + 1), cols(mu)] = blank if block is None else block * after[mu]
+                halo_ref[cols(lam + 1), cols(mu)] = blank if block is None else block
     for mu in range(-1, 2):
         for lam in range(3):
             block = entry(mu, lam)
-            value = blank if block is None else block * own[mu + 1] * after[lam]
+            value = blank if block is None else block * own[mu + 1]
             halo_ref[cols(mu + 4), cols(lam)] = value
     for k in range(2):
         virt_own_ref[:, cols(k)] = virt_ref[:, cols(k + 1)] * virt_mask[0, k + 1].astype(BF16)
@@ -346,21 +313,22 @@
     masks = (mine, occ_mask, virt_mask, three_mask)
     far = shifted(three_center, "ri", 2)
     one, two = call(
-        pack_kernel, "pack", [shape(tile + 16, 5 * tile), shape(tile, 2 * tile)],
-        [SMEM] * 4 + [VMEM] * 2, [VMEM] * 2, room=56,
-    )(*masks, occ_band, virt_band)
+        pack_kernel, "pack", [shape(tile, 5 * tile), shape(tile, 2 * tile)],
+        [SMEM] * 3 + [VMEM] * 2, [VMEM] * 2, room=56,
+    )(*masks[:3], occ_band, virt_band)
     one_hop, two_hops = lax.ppermute(one, BOTH, mixed((1, 0), (-1, 0))), shifted(two, "ao", -2)
-    near = lax.optimization_barrier((three_center, one))[0][:half]
+    flags = jnp.repeat(three_mask[0].astype(BF16), tile)[None, :, None]
+    near = lax.optimization_barrier((three_center, one))[0][:half] * flags
     halo_near = shifted(near, "ao", -1)
-    late = half_of(1, near, three_center)
+    late = lax.optimization_barrier((three_center, near))[0][half:] * flags
     halo_late = shifted(late, "ao", -1)
     flat = relayout(late, three_center)
-    one_hop, two_hops, _ = lax.optimization_barrier((one_hop, two_hops, flat))
+    one_hop, _ = lax.optimization_barrier((one_hop, flat))
     green_own, green_halo, virt_own, virt_next = call(
         tables_kernel, "tables",
         [shape(3 * tile, 3 * tile), shape(6 * tile, 3 * tile), shape(tile, 2 * tile), shape(tile, tile)],
         [SMEM] * 4 + [VMEM] * 5 + [ANY], [VMEM] * 4,
-        scratch_shapes=[pltpu.VMEM((tile + 16, 5 * tile), BF16)] * 2,
+        scratch_shapes=[pltpu.VMEM((tile, 5 * tile), BF16)] * 2,
     )(*masks, occ_band, virt_band, one_hop, partner(one_hop), two_hops, flat)
     m_near, m_late = own_m(green_own, three_center)
     early, distances = [flat, partner(lax.optimization_barrier((flat, m_near))[0])], [0]

time: 64.9 us -> 64.7 us (level)
  starting transfers between devices: 10.6 us -> 13.3 us
  blocking collectives: 11.2 us -> 13.8 us
  waiting for transfers between devices: 26.9 us -> 24.5 us
  Pallas kernels: 14.2 us -> 12.4 us
  local copies, waits for them, and re-layouts: 1.56 us -> 0.11 us
    ppermute x4, waiting for transfers between devices: 25.3 us -> 21.3 us  [shifted(): lax.ppermute(value, axis, [(i, (i + distance) % size) for i in range(size)])]
    ppermute x4, starting transfers between devices: 4.22 us -> 7.24 us  [shifted(): lax.ppermute(value, axis, [(i, (i + distance) % size) for i in range(size)])]
    all_to_all x1, blocking collectives: 11.2 us -> 13.8 us  [per_device(): lax.all_to_all(parts.reshape(lines * groups, *parts.shape[2:]), BOTH, 0,...]
    pallas_call x2 -> x1, Pallas kernels: 3.68 us -> 1.85 us  [per_device(): call(pack_kernel, 'pack', [shape(tile, 5 * tile), shape(tile, 2 * tile)],...]
    ppermute x1, waiting for transfers between devices: 0.01 us -> 1.56 us  [per_device(): lax.ppermute(one, BOTH, mixed((1, 0), (-1, 0)))]
    slice x1 -> x0, local copies, waits for them, and re-layouts: 1.22 us -> none  [per_device(): near = lax.optimization_barrier((three_center, one))[0][:half]]
  transfers between devices with their start and end apart: 8 -> 8, of which waited for: 3 -> 5; matrix products, arithmetic and copies ran while one was open for 2% -> 1% of each run, Pallas kernels for 12% -> 9%
where the time goes in v5:
time: 64.7 us; the launch traced here: 64.5 us
  waiting for transfers between devices  24.5 us (38%)
  blocking collectives  13.8 us (21%)
  starting transfers between devices  13.3 us (21%)
  Pallas kernels  12.4 us (19%)
    ppermute x4, waiting for transfers between devices, shifted(): lax.ppermute(value, axis, [(i, (i + distance) % size) for i in range(size)])  21.3 us
    all_to_all x1, blocking collectives, per_device(): lax.all_to_all(parts.reshape(lines * groups, *parts.shape[2:]), BOTH, 0,...  13.8 us
    ppermute x4, starting transfers between devices, shifted(): lax.ppermute(value, axis, [(i, (i + distance) % size) for i in range(size)])  7.24 us
    ppermute x1, starting transfers between devices, per_device(): lax.ppermute(one, BOTH, mixed((1, 0), (-1, 0)))  5.98 us
    pallas_call x2, Pallas kernels, halo_panels(): call(halo_kernel, name, shape(height, 2 * batch, width), [ANY] + [VMEM] *...  3.54 us
    pallas_call x1, Pallas kernels, contract(): call(functools.partial(contract_kernel, len(lefts), len(rights), 16, dist...  2.28 us
    pallas_call x1, Pallas kernels, per_device(): call(pack_kernel, 'pack', [shape(tile, 5 * tile), shape(tile, 2 * tile)],...  1.85 us
    ppermute x3, waiting for transfers between devices, partner(): return lax.ppermute(value, 'ri', [(i, i ^ 1) for i in range(groups)])  1.64 us
  transfers between devices with their start and end apart: 8, of which 5 were waited for; matrix products, arithmetic and copies ran while one was open for 1% of the time, Pallas kernels for 9%

profile of v5, /device:TPU:0, one launch (start us, length us, event | category | flops | bytes accessed | tf_op | source)
XLA Modules:
  0.0 64.5 jit_solution(2443823303356046153)
XLA Ops:
  0.0 0.0 copy-start
  0.0 0.0 copy-start.5
  0.0 1.8 %pack.1 = (bf16[128,640]{1,0:T(8,128)(2,1)}, bf16[128,256]{1,0:T(8,128)(2,1)}) custom-call(s32[1]{0:T(128)} %bitcast.mine_ref, s32[1,5]{1,0:T(1,128)} %occ_mask.3, s32[1,3]{1,0:T(1,128)} %virt_mask.3, bf16[128,640]{1,0:T(8,128)(2,1)} %occ_ref.3, bf16[128,384]{1,0:T(8,128)(2,1)} %virt_ref.3), custom_call_target="tpu_custom_call" | custom-call | flops 99999997952 | bytes 1024 | tf_op jit(solution)/shard_map/pack/pallas_call | solution.py:315
  1.9 6.0 %collective-permute-start = (bf16[128,640]{1,0:T(8,128)(2,1)}, bf16[128,640]{1,0:T(8,128)(2,1)S(1)}, u32[]{:S(2)}, u32[]{:S(2)}) collective-permute-start(bf16[128,640]{1,0:T(8,128)(2,1)} %get-tuple-element.20), channel_id=1, source_target_pairs={{0,28},{1,5},{2,30},{3,7},{4,0},{5,9},{6,2},{7,11},{8,4},{9,13},{1... | collective-permute-start | bytes 491528 | tf_op jit(solution)/shard_map/ppermute | solution.py:319
  7.8 0.0 copy-done
  7.8 1.5 %collective-permute-start.6 = (bf16[16,384,128]{2,1,0:T(8,128)(2,1)S(1)}, bf16[16,384,128]{2,1,0:T(8,128)(2,1)S(1)}, u32[]{:S(2)}, u32[]{:S(2)}) collective-permute-start(bf16[16,384,128]{2,1,0:T(8,128)(2,1)S(1)} %copy-done), channel_id=1, source_target_pairs={{0,2},{1,3},{2,0},{3,1},{4,6},{5,7},{6,4},{7,5},{8,10},{9,11},{10,... | collective-permute-start | bytes 4718600 | tf_op jit(solution)/shard_map/ppermute | solution.py:293
  9.4 0.0 copy-done.5
  9.4 0.1 broadcast_bitcast_fusion
  9.4 0.1 slice_multiply_fusion.1
  9.6 0.6 collective-permute-start.3
  10.2 0.1 slice_multiply_fusion.after_ref
  10.3 0.0 copy-start.6
  10.3 0.0 copy-start.1
  10.3 0.0 copy-start.2
  10.3 0.0 copy-start.3
  10.4 0.0 copy-start.4
  10.4 0.6 relayout.1.after_ref.refs_2_
  10.9 1.6 %collective-permute-done.one_ref = bf16[128,640]{1,0:T(8,128)(2,1)S(1)} collective-permute-done((bf16[128,640]{1,0:T(8,128)(2,1)}, bf16[128,640]{1,0:T(8,128)(2,1)S(1)}, u32[]{:S(2)}, u32[]{:S(2)}) %collective-permute-start) | collective-permute-done | bytes 163872 | tf_op jit(solution)/shard_map/ppermute | solution.py:319
  12.5 0.0 collective-permute-start.1
  12.5 0.0 copy-done.6
  12.5 3.1 %collective-permute-start.2 = (bf16[128,256]{1,0:T(8,128)(2,1)S(1)}, bf16[128,256]{1,0:T(8,128)(2,1)S(1)}, u32[]{:S(2)}, u32[]{:S(2)}) collective-permute-start(bf16[128,256]{1,0:T(8,128)(2,1)S(1)} %copy-done.6), channel_id=1, source_target_pairs={{0,24},{4,28},{8,0},{12,4},{16,8},{20,12},{24,16},{28,20},{1,25},{... | collective-permute-start | bytes 196616 | tf_op jit(solution)/shard_map/ppermute | solution.py:293
  15.6 2.0 %collective-permute-start.5 = (bf16[8,384,128]{2,1,0:T(8,128)(2,1)S(1)}, bf16[8,384,128]{2,1,0:T(8,128)(2,1)S(1)}, u32[]{:S(2)}, u32[]{:S(2)}) collective-permute-start(bf16[8,384,128]{2,1,0:T(8,128)(2,1)S(1)} %slice_multiply_fusion.after_ref), channel_id=1, source_target_pairs={{0,28},{4,0},{8,4},{12,8},{16,12},{20,16},{24,20},{28,24},{1,29},{... | collective-permute-start | bytes 2359304 | tf_op jit(solution)/shard_map/ppermute | solution.py:293
  17.6 13.0 %collective-permute-done.2.upper2 = bf16[128,256]{1,0:T(8,128)(2,1)S(1)} collective-permute-done((bf16[128,256]{1,0:T(8,128)(2,1)S(1)}, bf16[128,256]{1,0:T(8,128)(2,1)S(1)}, u32[]{:S(2)}, u32[]{:S(2)}) %collective-permute-start.2) | collective-permute-done | bytes 65568 | tf_op jit(solution)/shard_map/ppermute | solution.py:293
  30.7 0.0 collective-permute-done.1.other_ref
  30.7 0.0 copy-done.1
  30.7 0.0 copy-done.2
  30.7 0.0 copy-done.3
  30.7 0.0 copy-done.4
  30.7 0.8 %tables.1 = (bf16[384,384]{1,0:T(8,128)(2,1)S(1)}, bf16[768,384]{1,0:T(8,128)(2,1)S(1)}, bf16[128,256]{1,0:T(8,128)(2,1)S(1)}, bf16[128,128]{1,0:T(8,128)(2,1)S(1)}) custom-call(s32[1]{0:T(128)} %bitcast.mine_ref, s32[1,5]{1,0:T(1,128)S(1)} %copy-done.3, s32[1,3]{1,0:T(1,128)S(1)} %copy-done.4, s32[1,3]{1,0:T(1,128)S(1)} %copy-done.5, ...), custom_call_target="tpu_custom_call" | custom-call | flops 1024 | bytes 1024 | tf_op jit(solution)/shard_map/tables/pallas_call | solution.py:327
  31.5 1.5 %own_m.1 = (bf16[3072,128]{1,0:T(8,128)(2,1)S(1)}, bf16[3072,128]{1,0:T(8,128)(2,1)S(1)}) custom-call(bf16[384,384]{1,0:T(8,128)(2,1)S(1)} %get-tuple-element.25.green_ref, bf16[16,384,128]{2,1,0:T(8,128)(2,1)S(1)} %copy-done), custom_call_target="tpu_custom_call" | custom-call | flops 1024 | bytes 1024 | tf_op jit(solution)/shard_map/own_m/pallas_call | solution.py:177
  33.0 0.1 collective-permute-start.4
  33.1 0.0 collective-permute-done.3.held
  33.1 7.6 %collective-permute-done.6.near_ref = bf16[16,384,128]{2,1,0:T(8,128)(2,1)S(1)} collective-permute-done((bf16[16,384,128]{2,1,0:T(8,128)(2,1)S(1)}, bf16[16,384,128]{2,1,0:T(8,128)(2,1)S(1)}, u32[]{:S(2)}, u32[]{:S(2)}) %collective-permute-start.6) | collective-permute-done | bytes 1572896 | tf_op jit(solution)/shard_map/ppermute | solution.py:293
  40.6 0.0 collective-permute-start.7
  40.6 1.8 %halo_near.1.after_ref.refs_0_ = bf16[384,16,128]{2,1,0:T(8,128)(2,1)S(1)} custom-call(bf16[3072,128]{1,0:T(8,128)(2,1)S(1)} %get-tuple-element.26.after_ref.m_own, bf16[8,384,128]{2,1,0:T(8,128)(2,1)S(1)} %collective-permute-done.3.held, bf16[3072,128]{1,0:T(8,128)(2,1)S(1)} %get-tuple-element.27.m_own, bf16[768,384]{1,0:T(8,128)(2,1)S(1)} %get-tuple-element.29.green_ref, ...), custom_call_target="tpu_custom_call" | custom-call | flops 99999997952 | bytes 1024 | tf_op jit(solution)/shard_map/halo_near/pallas_call | solution.py:212
  42.4 1.6 %collective-permute-done.7.other_ref = bf16[16,384,128]{2,1,0:T(8,128)(2,1)S(1)} collective-permute-done((bf16[16,384,128]{2,1,0:T(8,128)(2,1)S(1)}, bf16[16,384,128]{2,1,0:T(8,128)(2,1)S(1)}, u32[]{:S(2)}, u32[]{:S(2)}) %collective-permute-start.7) | collective-permute-done | bytes 1572896 | tf_op jit(solution)/shard_map/ppermute | solution.py:311
  44.1 1.2 %far_rows.1.refs_4_ = bf16[384,32,128]{2,1,0:T(8,128)(2,1)S(1)} custom-call(bf16[384,16,128]{2,1,0:T(8,128)(2,1)S(1)} %halo_near.1.after_ref.refs_0_, bf16[16,384,128]{2,1,0:T(8,128)(2,1)S(1)} %collective-permute-done.6.near_ref, bf16[16,384,128]{2,1,0:T(8,128)(2,1)S(1)} %collective-permute-done.7.other_ref), custom_call_target="tpu_custom_call" | custom-call | flops 1024 | bytes 1024 | tf_op jit(solution)/shard_map/far_rows/pallas_call | solution.py:152
  45.3 0.7 %collective-permute-done.5.held = bf16[8,384,128]{2,1,0:T(8,128)(2,1)S(1)} collective-permute-done((bf16[8,384,128]{2,1,0:T(8,128)(2,1)S(1)}, bf16[8,384,128]{2,1,0:T(8,128)(2,1)S(1)}, u32[]{:S(2)}, u32[]{:S(2)}) %collective-permute-start.5) | collective-permute-done | bytes 786464 | tf_op jit(solution)/shard_map/ppermute | solution.py:293
  46.0 0.0 collective-permute-done.4.after_ref.refs_3_
  46.0 1.8 %halo_late.1.refs_1_ = bf16[384,16,128]{2,1,0:T(8,128)(2,1)S(1)} custom-call(bf16[384,16,128]{2,1,0:T(8,128)(2,1)S(1)} %collective-permute-done.4.after_ref.refs_3_, bf16[8,384,128]{2,1,0:T(8,128)(2,1)S(1)} %collective-permute-done.5.held, bf16[3072,128]{1,0:T(8,128)(2,1)S(1)} %get-tuple-element.26.after_ref.m_own, ...), custom_call_target="tpu_custom_call" | custom-call | flops 1024 | bytes 1024 | tf_op jit(solution)/shard_map/halo_late/pallas_call | solution.py:212
  47.8 2.3 %contract.1 = f32[8,4,8,128]{3,2,1,0:T(8,128)S(1)} custom-call(s32[1]{0:T(128)} %bitcast.mine_ref, bf16[384,16,128]{2,1,0:T(8,128)(2,1)S(1)} %halo_near.1.after_ref.refs_0_, bf16[384,16,128]{2,1,0:T(8,128)(2,1)S(1)} %halo_late.1.refs_1_, bf16[384,16,128]{2,1,0:T(8,128)(2,1)S(1)} %relayout.1.after_ref.refs_2_, ...), custom_call_target="tpu_custom_call" | custom-call | flops 1024 | bytes 1024 | tf_op jit(solution)/shard_map/contract/pallas_call | solution.py:277
  50.1 13.8 %all_to_all.5.src_ref = f32[32,8,128]{2,1,0:T(8,128)S(1)} all-to-all(f32[32,8,128]{2,1,0:T(8,128)S(1)} %bitcast.6), channel_id=1, replica_groups=mesh['ao'=8,'ri'=4] {'ao','ri'}, dimensions={0} | all-to-all | bytes 262144 | tf_op jit(solution)/shard_map/all_to_all | solution.py:350
  63.8 0.7 %total.1 = f32[16,64]{1,0:T(8,128)} custom-call(f32[32,8,128]{2,1,0:T(8,128)S(1)} %all_to_all.5.src_ref), custom_call_target="tpu_custom_call" | custom-call | flops 1024 | bytes 1024 | tf_op jit(solution)/shard_map/total/pallas_call | solution.py:351
  (1 shorter events, 0.0 us)
Async XLA Ops:
  0.0 7.8 %copy-start = (bf16[16,384,128]{2,1,0:T(8,128)(2,1)S(1)}, bf16[16,384,128]{2,1,0:T(8,128)(2,1)}, u32[]{:S(2)}) copy-start(bf16[16,384,128]{2,1,0:T(8,128)(2,1)} %src_ref.3) | copy-start | bytes 4718596
  0.0 9.4 %copy-start.5 = (s32[1,3]{1,0:T(1,128)S(1)}, s32[1,3]{1,0:T(1,128)}, u32[]{:S(2)}) copy-start(s32[1,3]{1,0:T(1,128)} %three_mask.1) | copy-start | bytes 40
  1.9 10.6 %collective-permute-start = (bf16[128,640]{1,0:T(8,128)(2,1)}, bf16[128,640]{1,0:T(8,128)(2,1)S(1)}, u32[]{:S(2)}, u32[]{:S(2)}) collective-permute-start(bf16[128,640]{1,0:T(8,128)(2,1)} %get-tuple-element.20), channel_id=1, source_target_pairs={{0,28},{1,5},{2,30},{3,7},{4,0},{5,9},{6,2},{7,11},{8,4},{9,13},{1... | collective-permute-start | bytes 491528 | tf_op jit(solution)/shard_map/ppermute | solution.py:319
  7.8 32.8 %collective-permute-start.6 = (bf16[16,384,128]{2,1,0:T(8,128)(2,1)S(1)}, bf16[16,384,128]{2,1,0:T(8,128)(2,1)S(1)}, u32[]{:S(2)}, u32[]{:S(2)}) collective-permute-start(bf16[16,384,128]{2,1,0:T(8,128)(2,1)S(1)} %copy-done), channel_id=1, source_target_pairs={{0,2},{1,3},{2,0},{3,1},{4,6},{5,7},{6,4},{7,5},{8,10},{9,11},{10,... | collective-permute-start | bytes 4718600 | tf_op jit(solution)/shard_map/ppermute | solution.py:293
  9.6 23.5 %collective-permute-start.3 = (bf16[8,384,128]{2,1,0:T(8,128)(2,1)S(1)}, bf16[8,384,128]{2,1,0:T(8,128)(2,1)S(1)}, u32[]{:S(2)}, u32[]{:S(2)}) collective-permute-start(bf16[8,384,128]{2,1,0:T(8,128)(2,1)S(1)} %slice_multiply_fusion.1), channel_id=1, source_target_pairs={{0,28},{4,0},{8,4},{12,8},{16,12},{20,16},{24,20},{28,24},{1,29},{... | collective-permute-start | bytes 2359304 | tf_op jit(solution)/shard_map/ppermute | solution.py:293
  10.3 2.2 %copy-start.6 = (bf16[128,256]{1,0:T(8,128)(2,1)S(1)}, bf16[128,256]{1,0:T(8,128)(2,1)}, u32[]{:S(2)}) copy-start(bf16[128,256]{1,0:T(8,128)(2,1)} %get-tuple-element.24) | copy-start | bytes 196612
  10.3 20.3 %copy-start.1 = (bf16[128,640]{1,0:T(8,128)(2,1)S(1)}, bf16[128,640]{1,0:T(8,128)(2,1)}, u32[]{:S(2)}) copy-start(bf16[128,640]{1,0:T(8,128)(2,1)} %occ_ref.3) | copy-start | bytes 491524
  10.3 20.3 %copy-start.2 = (bf16[128,384]{1,0:T(8,128)(2,1)S(1)}, bf16[128,384]{1,0:T(8,128)(2,1)}, u32[]{:S(2)}) copy-start(bf16[128,384]{1,0:T(8,128)(2,1)} %virt_ref.3) | copy-start | bytes 294916
  10.3 20.3 %copy-start.3 = (s32[1,5]{1,0:T(1,128)S(1)}, s32[1,5]{1,0:T(1,128)}, u32[]{:S(2)}) copy-start(s32[1,5]{1,0:T(1,128)} %occ_mask.3) | copy-start | bytes 64
  10.4 20.3 %copy-start.4 = (s32[1,3]{1,0:T(1,128)S(1)}, s32[1,3]{1,0:T(1,128)}, u32[]{:S(2)}) copy-start(s32[1,3]{1,0:T(1,128)} %virt_mask.3) | copy-start | bytes 40
  12.5 18.2 %collective-permute-start.1 = (bf16[128,640]{1,0:T(8,128)(2,1)S(1)}, bf16[128,640]{1,0:T(8,128)(2,1)S(1)}, u32[]{:S(2)}, u32[]{:S(2)}) collective-permute-start(bf16[128,640]{1,0:T(8,128)(2,1)S(1)} %collective-permute-done.one_ref), channel_id=1, source_target_pairs={{0,1},{1,0},{2,3},{3,2},{4,5},{5,4},{6,7},{7,6},{8,9},{9,8},{10,11... | collective-permute-start | bytes 491528 | tf_op jit(solution)/shard_map/ppermute | solution.py:311
  12.5 18.1 %collective-permute-start.2 = (bf16[128,256]{1,0:T(8,128)(2,1)S(1)}, bf16[128,256]{1,0:T(8,128)(2,1)S(1)}, u32[]{:S(2)}, u32[]{:S(2)}) collective-permute-start(bf16[128,256]{1,0:T(8,128)(2,1)S(1)} %copy-done.6), channel_id=1, source_target_pairs={{0,24},{4,28},{8,0},{12,4},{16,8},{20,12},{24,16},{28,20},{1,25},{... | collective-permute-start | bytes 196616 | tf_op jit(solution)/shard_map/ppermute | solution.py:293
  15.6 30.4 %collective-permute-start.5 = (bf16[8,384,128]{2,1,0:T(8,128)(2,1)S(1)}, bf16[8,384,128]{2,1,0:T(8,128)(2,1)S(1)}, u32[]{:S(2)}, u32[]{:S(2)}) collective-permute-start(bf16[8,384,128]{2,1,0:T(8,128)(2,1)S(1)} %slice_multiply_fusion.after_ref), channel_id=1, source_target_pairs={{0,28},{4,0},{8,4},{12,8},{16,12},{20,16},{24,20},{28,24},{1,29},{... | collective-permute-start | bytes 2359304 | tf_op jit(solution)/shard_map/ppermute | solution.py:293
  33.0 13.0 %collective-permute-start.4 = (bf16[384,16,128]{2,1,0:T(8,128)(2,1)S(1)}, bf16[384,16,128]{2,1,0:T(8,128)(2,1)S(1)}, u32[]{:S(2)}, u32[]{:S(2)}) collective-permute-start(bf16[384,16,128]{2,1,0:T(8,128)(2,1)S(1)} %relayout.1.after_ref.refs_2_), channel_id=1, source_target_pairs={{0,1},{1,0},{2,3},{3,2},{4,5},{5,4},{6,7},{7,6},{8,9},{9,8},{10,11... | collective-permute-start | bytes 4718600 | tf_op jit(solution)/shard_map/ppermute | solution.py:311
  40.6 3.4 %collective-permute-start.7 = (bf16[16,384,128]{2,1,0:T(8,128)(2,1)S(1)}, bf16[16,384,128]{2,1,0:T(8,128)(2,1)S(1)}, u32[]{:S(2)}, u32[]{:S(2)}) collective-permute-start(bf16[16,384,128]{2,1,0:T(8,128)(2,1)S(1)} %collective-permute-done.6.near_ref), channel_id=1, source_target_pairs={{0,1},{1,0},{2,3},{3,2},{4,5},{5,4},{6,7},{7,6},{8,9},{9,8},{10,11... | collective-permute-start | bytes 4718600 | tf_op jit(solution)/shard_map/ppermute | solution.py:311

commit v6 on v5

--- a/solution.py
+++ b/solution.py
@@ -134,27 +134,16 @@
     )(after, src)
 
 
-def far_kernel(after_ref, near_ref, other_ref, out_ref, held, sems):
-    batch, height, width = held.shape[1:]
-    moves = [
-        pltpu.make_async_copy(ref, held.at[k], sems.at[k])
-        for k, ref in enumerate((near_ref, other_ref))
-    ]
-    for move in moves:
-        move.start()
-    for move in moves:
-        move.wait()
-    out_ref[...] = jnp.swapaxes(held[...].reshape(2 * batch, height, width), 0, 1)
+def far_kernel(after_ref, near_ref, other_ref, out_ref):
+    batch = near_ref.shape[0]
+    out_ref[:, :batch] = jnp.swapaxes(near_ref[...], 0, 1)
+    out_ref[:, batch:] = jnp.swapaxes(other_ref[...], 0, 1)
 
 
 def far_rows(after, near, other):
     batch, height, width = near.shape
     return call(
-        far_kernel, "far_rows", shape(height, 2 * batch, width), [ANY] * 3,
-        scratch_shapes=[
-            pltpu.VMEM((2, batch, height, width), BF16),
-            pltpu.SemaphoreType.DMA((2,)),
-        ],
+        far_kernel, "far_rows", shape(height, 2 * batch, width), [ANY] + [VMEM] * 2,
     )(after, near, other)
 
 
@@ -257,7 +246,8 @@
     at = (row == chunk * half + index) & (row >= 0) & (row < batch)
     pick_x = jnp.where(at & (part == 0), 1.0, 0.0).astype(F32)
     pick_v = jnp.where(at & (part == 1), 1.0, 0.0).astype(F32)
-    result = dot_nn(pick_x, placed, **exact) + dot_nn(pick_v, placed, **exact).T
+    both = dot_nn(jnp.concatenate([pick_x, pick_v], 0), placed, **exact)
+    result = both[:cols] + both[cols:].T
     fold = batch // deep
     for k in range(chunks):
         piece = jnp.concatenate(

time: 64.7 us -> 64.8 us (level)
  no operation moved by 1% of the time
where the time goes in v6:
time: 64.8 us; the launch traced here: 64.6 us
  waiting for transfers between devices  24.8 us (38%)
  blocking collectives  13.8 us (21%)
  starting transfers between devices  13.3 us (21%)
  Pallas kernels  12.2 us (19%)
    ppermute x4, waiting for transfers between devices, shifted(): lax.ppermute(value, axis, [(i, (i + distance) % size) for i in range(size)])  21.6 us
    all_to_all x1, blocking collectives, per_device(): lax.all_to_all(parts.reshape(lines * groups, *parts.shape[2:]), BOTH, 0,...  13.8 us
    ppermute x4, starting transfers between devices, shifted(): lax.ppermute(value, axis, [(i, (i + distance) % size) for i in range(size)])  7.24 us
    ppermute x1, starting transfers between devices, per_device(): lax.ppermute(one, BOTH, mixed((1, 0), (-1, 0)))  5.98 us
    pallas_call x2, Pallas kernels, halo_panels(): call(halo_kernel, name, shape(height, 2 * batch, width), [ANY] + [VMEM] *...  3.54 us
    pallas_call x1, Pallas kernels, contract(): call(functools.partial(contract_kernel, len(lefts), len(rights), 16, dist...  2.33 us
    pallas_call x1, Pallas kernels, per_device(): call(pack_kernel, 'pack', [shape(tile, 5 * tile), shape(tile, 2 * tile)],...  1.85 us
    ppermute x3, waiting for transfers between devices, partner(): return lax.ppermute(value, 'ri', [(i, i ^ 1) for i in range(groups)])  1.64 us
  transfers between devices with their start and end apart: 8, of which 5 were waited for; matrix products, arithmetic and copies ran while one was open for 1% of the time, Pallas kernels for 9%

profile of v6, /device:TPU:0, one launch (start us, length us, event | category | flops | bytes accessed | tf_op | source)
XLA Modules:
  0.0 64.6 jit_solution(15024692379206527335)
XLA Ops:
  0.0 0.0 copy-start
  0.0 0.0 copy-start.5
  0.0 1.8 %pack.1 = (bf16[128,640]{1,0:T(8,128)(2,1)}, bf16[128,256]{1,0:T(8,128)(2,1)}) custom-call(s32[1]{0:T(128)} %bitcast.mine_ref, s32[1,5]{1,0:T(1,128)} %occ_mask.3, s32[1,3]{1,0:T(1,128)} %virt_mask.3, bf16[128,640]{1,0:T(8,128)(2,1)} %occ_ref.3, bf16[128,384]{1,0:T(8,128)(2,1)} %virt_ref.3), custom_call_target="tpu_custom_call" | custom-call | flops 99999997952 | bytes 1024 | tf_op jit(solution)/shard_map/pack/pallas_call | solution.py:305
  1.9 6.0 %collective-permute-start = (bf16[128,640]{1,0:T(8,128)(2,1)}, bf16[128,640]{1,0:T(8,128)(2,1)S(1)}, u32[]{:S(2)}, u32[]{:S(2)}) collective-permute-start(bf16[128,640]{1,0:T(8,128)(2,1)} %get-tuple-element.20), channel_id=1, source_target_pairs={{0,28},{1,5},{2,30},{3,7},{4,0},{5,9},{6,2},{7,11},{8,4},{9,13},{1... | collective-permute-start | bytes 491528 | tf_op jit(solution)/shard_map/ppermute | solution.py:309
  7.8 0.0 copy-done
  7.8 1.5 %collective-permute-start.6 = (bf16[16,384,128]{2,1,0:T(8,128)(2,1)S(1)}, bf16[16,384,128]{2,1,0:T(8,128)(2,1)S(1)}, u32[]{:S(2)}, u32[]{:S(2)}) collective-permute-start(bf16[16,384,128]{2,1,0:T(8,128)(2,1)S(1)} %copy-done), channel_id=1, source_target_pairs={{0,2},{1,3},{2,0},{3,1},{4,6},{5,7},{6,4},{7,5},{8,10},{9,11},{10,... | collective-permute-start | bytes 4718600 | tf_op jit(solution)/shard_map/ppermute | solution.py:283
  9.4 0.0 copy-done.5
  9.4 0.1 broadcast_bitcast_fusion
  9.4 0.1 slice_multiply_fusion.1
  9.6 0.6 collective-permute-start.3
  10.2 0.1 slice_multiply_fusion.after_ref
  10.3 0.0 copy-start.6
  10.3 0.0 copy-start.1
  10.3 0.0 copy-start.2
  10.3 0.0 copy-start.3
  10.4 0.0 copy-start.4
  10.4 0.6 relayout.1.after_ref.refs_2_
  10.9 1.6 %collective-permute-done.one_ref = bf16[128,640]{1,0:T(8,128)(2,1)S(1)} collective-permute-done((bf16[128,640]{1,0:T(8,128)(2,1)}, bf16[128,640]{1,0:T(8,128)(2,1)S(1)}, u32[]{:S(2)}, u32[]{:S(2)}) %collective-permute-start) | collective-permute-done | bytes 163872 | tf_op jit(solution)/shard_map/ppermute | solution.py:309
  12.5 0.0 collective-permute-start.1
  12.5 0.0 copy-done.6
  12.5 3.1 %collective-permute-start.2 = (bf16[128,256]{1,0:T(8,128)(2,1)S(1)}, bf16[128,256]{1,0:T(8,128)(2,1)S(1)}, u32[]{:S(2)}, u32[]{:S(2)}) collective-permute-start(bf16[128,256]{1,0:T(8,128)(2,1)S(1)} %copy-done.6), channel_id=1, source_target_pairs={{0,24},{4,28},{8,0},{12,4},{16,8},{20,12},{24,16},{28,20},{1,25},{... | collective-permute-start | bytes 196616 | tf_op jit(solution)/shard_map/ppermute | solution.py:283
  15.6 2.0 %collective-permute-start.5 = (bf16[8,384,128]{2,1,0:T(8,128)(2,1)S(1)}, bf16[8,384,128]{2,1,0:T(8,128)(2,1)S(1)}, u32[]{:S(2)}, u32[]{:S(2)}) collective-permute-start(bf16[8,384,128]{2,1,0:T(8,128)(2,1)S(1)} %slice_multiply_fusion.after_ref), channel_id=1, source_target_pairs={{0,28},{4,0},{8,4},{12,8},{16,12},{20,16},{24,20},{28,24},{1,29},{... | collective-permute-start | bytes 2359304 | tf_op jit(solution)/shard_map/ppermute | solution.py:283
  17.6 13.0 %collective-permute-done.2.upper2 = bf16[128,256]{1,0:T(8,128)(2,1)S(1)} collective-permute-done((bf16[128,256]{1,0:T(8,128)(2,1)S(1)}, bf16[128,256]{1,0:T(8,128)(2,1)S(1)}, u32[]{:S(2)}, u32[]{:S(2)}) %collective-permute-start.2) | collective-permute-done | bytes 65568 | tf_op jit(solution)/shard_map/ppermute | solution.py:283
  30.7 0.0 collective-permute-done.1.other_ref
  30.7 0.0 copy-done.1
  30.7 0.0 copy-done.2
  30.7 0.0 copy-done.3
  30.7 0.0 copy-done.4
  30.7 0.8 %tables.1 = (bf16[384,384]{1,0:T(8,128)(2,1)S(1)}, bf16[768,384]{1,0:T(8,128)(2,1)S(1)}, bf16[128,256]{1,0:T(8,128)(2,1)S(1)}, bf16[128,128]{1,0:T(8,128)(2,1)S(1)}) custom-call(s32[1]{0:T(128)} %bitcast.mine_ref, s32[1,5]{1,0:T(1,128)S(1)} %copy-done.3, s32[1,3]{1,0:T(1,128)S(1)} %copy-done.4, s32[1,3]{1,0:T(1,128)S(1)} %copy-done.5, ...), custom_call_target="tpu_custom_call" | custom-call | flops 1024 | bytes 1024 | tf_op jit(solution)/shard_map/tables/pallas_call | solution.py:317
  31.5 1.5 %own_m.1 = (bf16[3072,128]{1,0:T(8,128)(2,1)S(1)}, bf16[3072,128]{1,0:T(8,128)(2,1)S(1)}) custom-call(bf16[384,384]{1,0:T(8,128)(2,1)S(1)} %get-tuple-element.25.green_ref, bf16[16,384,128]{2,1,0:T(8,128)(2,1)S(1)} %copy-done), custom_call_target="tpu_custom_call" | custom-call | flops 1024 | bytes 1024 | tf_op jit(solution)/shard_map/own_m/pallas_call | solution.py:166
  33.0 0.1 collective-permute-start.4
  33.1 0.0 collective-permute-done.3.held
  33.1 7.6 %collective-permute-done.6.near_ref = bf16[16,384,128]{2,1,0:T(8,128)(2,1)S(1)} collective-permute-done((bf16[16,384,128]{2,1,0:T(8,128)(2,1)S(1)}, bf16[16,384,128]{2,1,0:T(8,128)(2,1)S(1)}, u32[]{:S(2)}, u32[]{:S(2)}) %collective-permute-start.6) | collective-permute-done | bytes 1572896 | tf_op jit(solution)/shard_map/ppermute | solution.py:283
  40.6 0.0 collective-permute-start.7
  40.6 1.8 %halo_near.1.after_ref.refs_0_ = bf16[384,16,128]{2,1,0:T(8,128)(2,1)S(1)} custom-call(bf16[3072,128]{1,0:T(8,128)(2,1)S(1)} %get-tuple-element.26.after_ref.m_own, bf16[8,384,128]{2,1,0:T(8,128)(2,1)S(1)} %collective-permute-done.3.held, bf16[3072,128]{1,0:T(8,128)(2,1)S(1)} %get-tuple-element.27.m_own, bf16[768,384]{1,0:T(8,128)(2,1)S(1)} %get-tuple-element.29.green_ref, ...), custom_call_target="tpu_custom_call" | custom-call | flops 99999997952 | bytes 1024 | tf_op jit(solution)/shard_map/halo_near/pallas_call | solution.py:201
  42.4 1.6 %collective-permute-done.7.other_ref = bf16[16,384,128]{2,1,0:T(8,128)(2,1)S(1)} collective-permute-done((bf16[16,384,128]{2,1,0:T(8,128)(2,1)S(1)}, bf16[16,384,128]{2,1,0:T(8,128)(2,1)S(1)}, u32[]{:S(2)}, u32[]{:S(2)}) %collective-permute-start.7) | collective-permute-done | bytes 1572896 | tf_op jit(solution)/shard_map/ppermute | solution.py:301
  44.1 0.9 %far_rows.1.refs_4_ = bf16[384,32,128]{2,1,0:T(8,128)(2,1)S(1)} custom-call(bf16[384,16,128]{2,1,0:T(8,128)(2,1)S(1)} %halo_near.1.after_ref.refs_0_, bf16[16,384,128]{2,1,0:T(8,128)(2,1)S(1)} %collective-permute-done.6.near_ref, bf16[16,384,128]{2,1,0:T(8,128)(2,1)S(1)} %collective-permute-done.7.other_ref), custom_call_target="tpu_custom_call" | custom-call | flops 1024 | bytes 1024 | tf_op jit(solution)/shard_map/far_rows/pallas_call | solution.py:145
  45.0 1.0 %collective-permute-done.5.held = bf16[8,384,128]{2,1,0:T(8,128)(2,1)S(1)} collective-permute-done((bf16[8,384,128]{2,1,0:T(8,128)(2,1)S(1)}, bf16[8,384,128]{2,1,0:T(8,128)(2,1)S(1)}, u32[]{:S(2)}, u32[]{:S(2)}) %collective-permute-start.5) | collective-permute-done | bytes 786464 | tf_op jit(solution)/shard_map/ppermute | solution.py:283
  46.0 0.0 collective-permute-done.4.after_ref.refs_3_
  46.0 1.8 %halo_late.1.refs_1_ = bf16[384,16,128]{2,1,0:T(8,128)(2,1)S(1)} custom-call(bf16[384,16,128]{2,1,0:T(8,128)(2,1)S(1)} %collective-permute-done.4.after_ref.refs_3_, bf16[8,384,128]{2,1,0:T(8,128)(2,1)S(1)} %collective-permute-done.5.held, bf16[3072,128]{1,0:T(8,128)(2,1)S(1)} %get-tuple-element.26.after_ref.m_own, ...), custom_call_target="tpu_custom_call" | custom-call | flops 1024 | bytes 1024 | tf_op jit(solution)/shard_map/halo_late/pallas_call | solution.py:201
  47.8 2.3 %contract.1 = f32[8,4,8,128]{3,2,1,0:T(8,128)S(1)} custom-call(s32[1]{0:T(128)} %bitcast.mine_ref, bf16[384,16,128]{2,1,0:T(8,128)(2,1)S(1)} %halo_near.1.after_ref.refs_0_, bf16[384,16,128]{2,1,0:T(8,128)(2,1)S(1)} %halo_late.1.refs_1_, bf16[384,16,128]{2,1,0:T(8,128)(2,1)S(1)} %relayout.1.after_ref.refs_2_, ...), custom_call_target="tpu_custom_call" | custom-call | flops 1024 | bytes 1024 | tf_op jit(solution)/shard_map/contract/pallas_call | solution.py:267
  50.1 13.8 %all_to_all.5.src_ref = f32[32,8,128]{2,1,0:T(8,128)S(1)} all-to-all(f32[32,8,128]{2,1,0:T(8,128)S(1)} %bitcast.6), channel_id=1, replica_groups=mesh['ao'=8,'ri'=4] {'ao','ri'}, dimensions={0} | all-to-all | bytes 262144 | tf_op jit(solution)/shard_map/all_to_all | solution.py:340
  63.9 0.7 %total.1 = f32[16,64]{1,0:T(8,128)} custom-call(f32[32,8,128]{2,1,0:T(8,128)S(1)} %all_to_all.5.src_ref), custom_call_target="tpu_custom_call" | custom-call | flops 1024 | bytes 1024 | tf_op jit(solution)/shard_map/total/pallas_call | solution.py:341
  (1 shorter events, 0.0 us)
Async XLA Ops:
  0.0 7.8 %copy-start = (bf16[16,384,128]{2,1,0:T(8,128)(2,1)S(1)}, bf16[16,384,128]{2,1,0:T(8,128)(2,1)}, u32[]{:S(2)}) copy-start(bf16[16,384,128]{2,1,0:T(8,128)(2,1)} %src_ref.3) | copy-start | bytes 4718596
  0.0 9.4 %copy-start.5 = (s32[1,3]{1,0:T(1,128)S(1)}, s32[1,3]{1,0:T(1,128)}, u32[]{:S(2)}) copy-start(s32[1,3]{1,0:T(1,128)} %three_mask.1) | copy-start | bytes 40
  1.9 10.6 %collective-permute-start = (bf16[128,640]{1,0:T(8,128)(2,1)}, bf16[128,640]{1,0:T(8,128)(2,1)S(1)}, u32[]{:S(2)}, u32[]{:S(2)}) collective-permute-start(bf16[128,640]{1,0:T(8,128)(2,1)} %get-tuple-element.20), channel_id=1, source_target_pairs={{0,28},{1,5},{2,30},{3,7},{4,0},{5,9},{6,2},{7,11},{8,4},{9,13},{1... | collective-permute-start | bytes 491528 | tf_op jit(solution)/shard_map/ppermute | solution.py:309
  7.8 32.8 %collective-permute-start.6 = (bf16[16,384,128]{2,1,0:T(8,128)(2,1)S(1)}, bf16[16,384,128]{2,1,0:T(8,128)(2,1)S(1)}, u32[]{:S(2)}, u32[]{:S(2)}) collective-permute-start(bf16[16,384,128]{2,1,0:T(8,128)(2,1)S(1)} %copy-done), channel_id=1, source_target_pairs={{0,2},{1,3},{2,0},{3,1},{4,6},{5,7},{6,4},{7,5},{8,10},{9,11},{10,... | collective-permute-start | bytes 4718600 | tf_op jit(solution)/shard_map/ppermute | solution.py:283
  9.6 23.5 %collective-permute-start.3 = (bf16[8,384,128]{2,1,0:T(8,128)(2,1)S(1)}, bf16[8,384,128]{2,1,0:T(8,128)(2,1)S(1)}, u32[]{:S(2)}, u32[]{:S(2)}) collective-permute-start(bf16[8,384,128]{2,1,0:T(8,128)(2,1)S(1)} %slice_multiply_fusion.1), channel_id=1, source_target_pairs={{0,28},{4,0},{8,4},{12,8},{16,12},{20,16},{24,20},{28,24},{1,29},{... | collective-permute-start | bytes 2359304 | tf_op jit(solution)/shard_map/ppermute | solution.py:283
  10.3 2.2 %copy-start.6 = (bf16[128,256]{1,0:T(8,128)(2,1)S(1)}, bf16[128,256]{1,0:T(8,128)(2,1)}, u32[]{:S(2)}) copy-start(bf16[128,256]{1,0:T(8,128)(2,1)} %get-tuple-element.24) | copy-start | bytes 196612
  10.3 20.3 %copy-start.1 = (bf16[128,640]{1,0:T(8,128)(2,1)S(1)}, bf16[128,640]{1,0:T(8,128)(2,1)}, u32[]{:S(2)}) copy-start(bf16[128,640]{1,0:T(8,128)(2,1)} %occ_ref.3) | copy-start | bytes 491524
  10.3 20.3 %copy-start.2 = (bf16[128,384]{1,0:T(8,128)(2,1)S(1)}, bf16[128,384]{1,0:T(8,128)(2,1)}, u32[]{:S(2)}) copy-start(bf16[128,384]{1,0:T(8,128)(2,1)} %virt_ref.3) | copy-start | bytes 294916
  10.3 20.3 %copy-start.3 = (s32[1,5]{1,0:T(1,128)S(1)}, s32[1,5]{1,0:T(1,128)}, u32[]{:S(2)}) copy-start(s32[1,5]{1,0:T(1,128)} %occ_mask.3) | copy-start | bytes 64
  10.4 20.3 %copy-start.4 = (s32[1,3]{1,0:T(1,128)S(1)}, s32[1,3]{1,0:T(1,128)}, u32[]{:S(2)}) copy-start(s32[1,3]{1,0:T(1,128)} %virt_mask.3) | copy-start | bytes 40
  12.5 18.2 %collective-permute-start.1 = (bf16[128,640]{1,0:T(8,128)(2,1)S(1)}, bf16[128,640]{1,0:T(8,128)(2,1)S(1)}, u32[]{:S(2)}, u32[]{:S(2)}) collective-permute-start(bf16[128,640]{1,0:T(8,128)(2,1)S(1)} %collective-permute-done.one_ref), channel_id=1, source_target_pairs={{0,1},{1,0},{2,3},{3,2},{4,5},{5,4},{6,7},{7,6},{8,9},{9,8},{10,11... | collective-permute-start | bytes 491528 | tf_op jit(solution)/shard_map/ppermute | solution.py:301
  12.5 18.1 %collective-permute-start.2 = (bf16[128,256]{1,0:T(8,128)(2,1)S(1)}, bf16[128,256]{1,0:T(8,128)(2,1)S(1)}, u32[]{:S(2)}, u32[]{:S(2)}) collective-permute-start(bf16[128,256]{1,0:T(8,128)(2,1)S(1)} %copy-done.6), channel_id=1, source_target_pairs={{0,24},{4,28},{8,0},{12,4},{16,8},{20,12},{24,16},{28,20},{1,25},{... | collective-permute-start | bytes 196616 | tf_op jit(solution)/shard_map/ppermute | solution.py:283
  15.6 30.4 %collective-permute-start.5 = (bf16[8,384,128]{2,1,0:T(8,128)(2,1)S(1)}, bf16[8,384,128]{2,1,0:T(8,128)(2,1)S(1)}, u32[]{:S(2)}, u32[]{:S(2)}) collective-permute-start(bf16[8,384,128]{2,1,0:T(8,128)(2,1)S(1)} %slice_multiply_fusion.after_ref), channel_id=1, source_target_pairs={{0,28},{4,0},{8,4},{12,8},{16,12},{20,16},{24,20},{28,24},{1,29},{... | collective-permute-start | bytes 2359304 | tf_op jit(solution)/shard_map/ppermute | solution.py:283
  33.0 13.0 %collective-permute-start.4 = (bf16[384,16,128]{2,1,0:T(8,128)(2,1)S(1)}, bf16[384,16,128]{2,1,0:T(8,128)(2,1)S(1)}, u32[]{:S(2)}, u32[]{:S(2)}) collective-permute-start(bf16[384,16,128]{2,1,0:T(8,128)(2,1)S(1)} %relayout.1.after_ref.refs_2_), channel_id=1, source_target_pairs={{0,1},{1,0},{2,3},{3,2},{4,5},{5,4},{6,7},{7,6},{8,9},{9,8},{10,11... | collective-permute-start | bytes 4718600 | tf_op jit(solution)/shard_map/ppermute | solution.py:301
  40.6 3.4 %collective-permute-start.7 = (bf16[16,384,128]{2,1,0:T(8,128)(2,1)S(1)}, bf16[16,384,128]{2,1,0:T(8,128)(2,1)S(1)}, u32[]{:S(2)}, u32[]{:S(2)}) collective-permute-start(bf16[16,384,128]{2,1,0:T(8,128)(2,1)S(1)} %collective-permute-done.6.near_ref), channel_id=1, source_target_pairs={{0,1},{1,0},{2,3},{3,2},{4,5},{5,4},{6,7},{7,6},{8,9},{9,8},{10,11... | collective-permute-start | bytes 4718600 | tf_op jit(solution)/shard_map/ppermute | solution.py:301
